TPU v7x, 32 devices: a whole 2x2x4 slice. The times are simulated.
32 devices in a mesh: groups: 2 (over x), row: 16 (over z, y, core).
Axes of the slice: x: 2, y: 2, z: 4, core: 2. Of those that a mesh axis runs over, the one named last changes fastest.
Arguments:
- coupling: float32 [64, 3, 576, 576], P(('groups', 'row')), parts along dimension 0, may hold values from -0.0625 to 0.0625
- columns: int32 [64, 3], P(('groups', 'row')), parts along dimension 0, may hold values from 0 to 31, as said below
- stiff_diag: float32 [3, 12288], P(None, ('groups', 'row')), parts along dimension 1, may hold values from 0.5 to 2
- interior: int32 [12288], P(('groups', 'row')), parts along dimension 0, may hold values 0 or 1
- loads: float32 [8, 3, 12288], P(None, None, ('groups', 'row')), parts along dimension 2, may hold values from -12 to 12
Outputs:
- displacement: float32 [8, 3, 12288], P(None, None, ('groups', 'row')), parts along dimension 2
- residual: float32 [8, 3, 12288], P(None, None, ('groups', 'row')), parts along dimension 2
There are 2 independent parts, one for each index of `groups`. A program takes and returns all parts, laid end to end along the dimension named above; each array names one. Nothing has to cross between parts.
Inputs may be any that keep to these rules, and one draw needn't show every extreme that they name: Each column of columns is a permutation of the 32 blocks, and columns[b,k] lies on the device that holds block b or on one beside it: |columns[b,k] // 2 - b // 2| <= 1.
All inputs are finite; a program needn't handle non-finite values. No bound on the sum of `interior` on one device may be relied on, other than what follows from the above.
Results may differ from a plain program's by a relative error of at most 0.0004.
Values sent between devices are 32-bit elements; how exact they have to be, the bound alone decides.
No kernel may reach another device: no remote copies, remote signals or barrier semaphores. Data moves between devices by JAX's collectives and lax.ppermute only.
A program may use at most 64 MiB of HBM per device.

v0:
```python
import jax
import jax.numpy as jnp
from jax import lax
from jax.sharding import PartitionSpec as P

ITERS = 2


precise = lax.Precision.HIGHEST
slot_shift = 1.2


def with_halo(block, sides, width):
    for axis, dim in sides:
        count = lax.axis_size(axis)
        forward = [(i, i + 1) for i in range(count - 1)]
        backward = [(target, source) for source, target in forward]
        low = lax.ppermute(
            lax.slice_in_dim(block, block.shape[dim] - width, None, axis=dim), axis, forward
        )
        high = lax.ppermute(lax.slice_in_dim(block, 0, width, axis=dim), axis, backward)
        block = jnp.concatenate([low, block, high], axis=dim)
    return block


def passed_along(block, axis, distance):
    devices = range(lax.axis_size(axis))
    route = [(i - distance, i) for i in devices if i - distance in devices]
    return lax.ppermute(block, axis, route)


def inner_gram(left, right):
    return jnp.einsum("fcn,gcn->fg", left, right, precision=precise)


def combine(vectors, mixing):
    return jnp.einsum("gcn,gf->fcn", vectors, mixing, precision=precise)


def solve_small(matrix, rhs_matrix):
    lower = jnp.linalg.cholesky(matrix)
    middle = lax.linalg.triangular_solve(lower, rhs_matrix, left_side=True, lower=True)
    return lax.linalg.triangular_solve(lower, middle, left_side=True, lower=True, transpose_a=True)


def shards(coupling, columns, stiff_diag, interior, loads):
    blocks_here = coupling.shape[0]
    slot_count = coupling.shape[1]
    block_width = coupling.shape[2]
    fields = loads.shape[0]
    nodes_here = loads.shape[2]
    block_nodes = nodes_here // blocks_here
    inside = interior.astype(jnp.float32)
    diagonal = slot_shift * slot_count + stiff_diag
    device = lax.axis_index("row")
    first_block = (device - 1) * blocks_here
    local_columns = columns - first_block
    displacement = jnp.zeros_like(loads)
    residual = loads
    direction = loads
    res_gram = lax.psum(inner_gram(loads, loads), "row")
    for iteration in range(ITERS):
        to_shaped = (
            (direction * inside).reshape(fields, 3, blocks_here, block_nodes).transpose(2, 0, 1, 3)
        )
        operate_blocks = to_shaped.reshape(blocks_here, fields, block_width)
        own_rows = jnp.zeros_like(operate_blocks)
        extended = with_halo(operate_blocks, (("row", 0),), blocks_here)
        outgoing = jnp.zeros_like(extended)
        for slot_index in range(slot_count):
            matrix = coupling[:, slot_index]
            targets = local_columns[:, slot_index]
            own_rows = own_rows + jnp.einsum(
                "rfj,rij->rfi", extended[targets], matrix, precision=precise
            )
            reverse = jnp.einsum("rfi,rij->rfj", operate_blocks, matrix, precision=precise)
            outgoing = outgoing.at[targets].add(reverse)
        from_left = passed_along(outgoing[2 * blocks_here :], "row", 1)
        from_right = passed_along(outgoing[:blocks_here], "row", -1)
        own_rows = own_rows + outgoing[blocks_here : 2 * blocks_here] + from_left + from_right
        shaped = own_rows.reshape(blocks_here, fields, 3, block_nodes).transpose(1, 2, 0, 3)
        image = diagonal * direction + inside * shaped.reshape(fields, 3, nodes_here)
        curvature = lax.psum(inner_gram(direction, image), "row")
        step_size = solve_small(curvature, res_gram)
        displacement = displacement + combine(direction, step_size)
        residual = residual - combine(image, step_size)
        if iteration + 1 < ITERS:
            res_next = lax.psum(inner_gram(residual, residual), "row")
            mixing = solve_small(res_gram, res_next)
            direction = residual + combine(direction, mixing)
            res_gram = res_next
    return (displacement, residual)


def solution(mesh):
    placed = (
        P(("groups", "row"), None, None, None),
        P(("groups", "row"), None),
        P(None, ("groups", "row")),
        P(("groups", "row")),
        P(None, None, ("groups", "row")),
    )
    return jax.shard_map(
        shards,
        mesh=mesh,
        in_specs=placed,
        out_specs=(P(None, None, ("groups", "row")), P(None, None, ("groups", "row"))),
        check_vma=False,
    )
```

profile of v0, /device:TPU:0, one launch (start us, length us, event | category | flops | bytes accessed | tf_op | source)
XLA Modules:
  0.0 183.7 jit_solution(13024746910942541598)
XLA Ops:
  2.4 2.3 %collective-permute-start = (f32[2,8,576]{2,1,0:T(8,128)S(1)}, f32[2,8,576]{2,1,0:T(8,128)S(1)}, u32[]{:S(2)}, u32[]{:S(2)}) collective-permute-start(f32[2,8,576]{2,1,0:T(8,128)S(1)} %reshape.48), channel_id=1, source_target_pairs={{0,1},{1,2},{2,3},{3,4},{4,5},{5,6},{6,7},{7,8},{8,9},{9,10},{10,1... | collective-permute-start | bytes 110600 | tf_op jit(solution)/shard_map/ppermute | solution.py:18
  4.7 1.3 collective-permute-start.1
  6.0 3.4 %fusion.20 = f32[2,8,576]{2,1,0:T(8,128)S(1)} fusion(f32[2,8,576]{2,1,0:T(8,128)S(1)} %reshape.48, f32[2,3,576,576]{3,2,1,0:T(8,128)} %param.10), kind=kOutput, calls=%fused_computation.32 | convolution fusion | flops 63700992 | bytes 3022848 | tf_op jit(solution)/shard_map/rfi,rij->rfj/dot_general | solution.py:76
  9.4 3.4 %fusion.12 = f32[2,8,576]{2,1,0:T(8,128)S(1)} fusion(f32[2,8,576]{2,1,0:T(8,128)S(1)} %reshape.48, f32[2,3,576,576]{3,2,1,0:T(8,128)} %param.10), kind=kOutput, calls=%fused_computation.24 | convolution fusion | flops 63700992 | bytes 3022848 | tf_op jit(solution)/shard_map/rfi,rij->rfj/dot_general | solution.py:76
  12.7 3.4 %fusion.4 = f32[2,8,576]{2,1,0:T(8,128)S(1)} fusion(f32[2,8,576]{2,1,0:T(8,128)S(1)} %reshape.48, f32[2,3,576,576]{3,2,1,0:T(8,128)} %param.10), kind=kOutput, calls=%fused_computation.16 | convolution fusion | flops 63700992 | bytes 3022848 | tf_op jit(solution)/shard_map/rfi,rij->rfj/dot_general | solution.py:76
  18.2 5.2 %collective-permute-start.2 = (f32[2,8,576]{2,1,0:T(8,128)S(1)}, f32[2,8,576]{2,1,0:T(8,128)S(1)}, u32[]{:S(2)}, u32[]{:S(2)}) collective-permute-start(f32[2,8,576]{2,1,0:T(8,128)S(1)} %get-tuple-element.12), channel_id=1, source_target_pairs={{0,1},{1,2},{2,3},{3,4},{4,5},{5,6},{6,7},{7,8},{8,9},{9,10},{10,1... | collective-permute-start | bytes 110600 | tf_op jit(solution)/shard_map/ppermute | solution.py:29
  23.4 1.3 collective-permute-start.3
  25.6 4.4 %fusion.14 = f32[2,8,576]{2,1,0:T(8,128)S(1)} fusion(f32[2,8,576]{2,1,0:T(8,128)S(1)} %gather_fusion.1, f32[2,3,576,576]{3,2,1,0:T(8,128)} %param.10), kind=kOutput, calls=%fused_computation.26 | convolution fusion | flops 63700992 | bytes 3022848 | tf_op jit(solution)/shard_map/rfj,rij->rfi/dot_general | solution.py:73
  30.5 4.4 %fusion.6 = f32[2,8,576]{2,1,0:T(8,128)S(1)} fusion(f32[2,8,576]{2,1,0:T(8,128)S(1)} %gather_fusion.2, f32[2,3,576,576]{3,2,1,0:T(8,128)} %param.10), kind=kOutput, calls=%fused_computation.18 | convolution fusion | flops 63700992 | bytes 3022848 | tf_op jit(solution)/shard_map/rfj,rij->rfi/dot_general | solution.py:73
  35.5 4.4 %fusion.48 = f32[2,8,576]{2,1,0:T(8,128)S(1)} fusion(f32[2,8,576]{2,1,0:T(8,128)S(1)} %collective-permute-done.3, f32[2,8,576]{2,1,0:T(8,128)S(1)} %collective-permute-done.2, f32[2,8,576]{2,1,0:T(8,128)S(1)} %fusion.6, f32[2,8,576]{2,1,0:T(8,128)S(1)} %fusion.14, f32[2,8,576]{2,1,0:T(8,128)S(1)} %gather_fusion, f32[2,3,576,576]{3,2,1,0:T(8,128)} %param.10, ...), kind=kOutput, calls=%fused_computation.52 | convolution fusion | flops 63747072 | bytes 3207168 | tf_op jit(solution)/shard_map/rfj,rij->rfi/dot_general | solution.py:73
  40.3 35.6 %all-reduce = (f32[8,8]{0,1:T(8,128)S(1)}, f32[8,8]{0,1:T(8,128)S(1)}) all-reduce(f32[8,8]{0,1:T(8,128)S(1)} %convolution_bitcast_fusion.5, f32[8,8]{0,1:T(8,128)S(1)} %convolution_bitcast_fusion.6), channel_id=1, replica_groups=mesh['groups'=2,'row'=16] {'row'}, use_global_device_ids=true, to_apply=%region_6.0 | all-reduce | flops 128 | bytes 1024 | tf_op jit(solution)/shard_map/psum | solution.py:61
  82.1 29.5 %psum.30 = f32[8,8]{1,0:T(8,128)S(1)} all-reduce(f32[8,8]{1,0:T(8,128)S(1)} %convolution_bitcast_fusion.3), channel_id=1, replica_groups=mesh['groups'=2,'row'=16] {'row'}, use_global_device_ids=true, to_apply=%region_7.11 | all-reduce | flops 64 | bytes 512 | tf_op jit(solution)/shard_map/psum | solution.py:88
  112.5 1.8 collective-permute-start.4
  114.2 1.3 collective-permute-start.5
  115.5 3.4 %fusion.16 = f32[2,8,576]{2,1,0:T(8,128)S(1)} fusion(f32[2,8,576]{2,1,0:T(8,128)S(1)} %reshape.52, f32[2,3,576,576]{3,2,1,0:T(8,128)} %param.10), kind=kOutput, calls=%fused_computation.28 | convolution fusion | flops 63700992 | bytes 3022848 | tf_op jit(solution)/shard_map/rfi,rij->rfj/dot_general | solution.py:76
  118.9 3.4 %fusion.8 = f32[2,8,576]{2,1,0:T(8,128)S(1)} fusion(f32[2,8,576]{2,1,0:T(8,128)S(1)} %reshape.52, f32[2,3,576,576]{3,2,1,0:T(8,128)} %param.10), kind=kOutput, calls=%fused_computation.20 | convolution fusion | flops 63700992 | bytes 3022848 | tf_op jit(solution)/shard_map/rfi,rij->rfj/dot_general | solution.py:76
  122.3 3.4 %fusion = f32[2,8,576]{2,1,0:T(8,128)S(1)} fusion(f32[2,8,576]{2,1,0:T(8,128)S(1)} %reshape.52, f32[2,3,576,576]{3,2,1,0:T(8,128)} %param.10), kind=kOutput, calls=%fused_computation.12 | convolution fusion | flops 63700992 | bytes 3022848 | tf_op jit(solution)/shard_map/rfi,rij->rfj/dot_general | solution.py:76
  127.7 3.0 %collective-permute-start.6 = (f32[2,8,576]{2,1,0:T(8,128)S(1)}, f32[2,8,576]{2,1,0:T(8,128)S(1)}, u32[]{:S(2)}, u32[]{:S(2)}) collective-permute-start(f32[2,8,576]{2,1,0:T(8,128)S(1)} %get-tuple-element.10), channel_id=1, source_target_pairs={{0,1},{1,2},{2,3},{3,4},{4,5},{5,6},{6,7},{7,8},{8,9},{9,10},{10,1... | collective-permute-start | bytes 110600 | tf_op jit(solution)/shard_map/ppermute | solution.py:29
  130.7 1.5 collective-permute-start.7
  133.4 4.4 %fusion.10 = f32[2,8,576]{2,1,0:T(8,128)S(1)} fusion(f32[2,8,576]{2,1,0:T(8,128)S(1)} %gather_fusion.4, f32[2,3,576,576]{3,2,1,0:T(8,128)} %param.10), kind=kOutput, calls=%fused_computation.22 | convolution fusion | flops 63700992 | bytes 3022848 | tf_op jit(solution)/shard_map/rfj,rij->rfi/dot_general | solution.py:73
  137.8 4.4 %fusion.2 = f32[2,8,576]{2,1,0:T(8,128)S(1)} fusion(f32[2,8,576]{2,1,0:T(8,128)S(1)} %gather_fusion.5, f32[2,3,576,576]{3,2,1,0:T(8,128)} %param.10), kind=kOutput, calls=%fused_computation.14 | convolution fusion | flops 63700992 | bytes 3022848 | tf_op jit(solution)/shard_map/rfj,rij->rfi/dot_general | solution.py:73
  142.8 4.4 %fusion.63 = f32[2,8,576]{2,1,0:T(8,128)S(1)} fusion(f32[2,8,576]{2,1,0:T(8,128)S(1)} %collective-permute-done.7, f32[2,8,576]{2,1,0:T(8,128)S(1)} %collective-permute-done.6, f32[2,8,576]{2,1,0:T(8,128)S(1)} %fusion.2, f32[2,8,576]{2,1,0:T(8,128)S(1)} %fusion.10, f32[2,8,576]{2,1,0:T(8,128)S(1)} %gather_fusion.3, f32[2,3,576,576]{3,2,1,0:T(8,128)} %param.10, ...), kind=kOutput, calls=%fused_computation.57 | convolution fusion | flops 63747072 | bytes 3207168 | tf_op jit(solution)/shard_map/rfj,rij->rfi/dot_general | solution.py:73
  147.6 31.4 %psum.31 = f32[8,8]{0,1:T(8,128)S(1)} all-reduce(f32[8,8]{0,1:T(8,128)S(1)} %convolution_bitcast_fusion.1), channel_id=1, replica_groups=mesh['groups'=2,'row'=16] {'row'}, use_global_device_ids=true, to_apply=%region_11.15 | all-reduce | flops 64 | bytes 512 | tf_op jit(solution)/shard_map/psum | solution.py:83
  182.1 0.8 convolution_subtract_fusion
  (90 shorter events, 21.2 us)
Async XLA Ops:
  0.6 24.1 %copy-start = (f32[8,3,384]{2,0,1:T(8,128)S(1)}, f32[8,3,384]{2,0,1:T(8,128)}, u32[]{:S(2)}) copy-start(f32[8,3,384]{2,0,1:T(8,128)} %param.14) | copy-start | bytes 110596
  0.6 15.5 %copy-start.2 = (s32[2,3]{1,0:T(2,128)S(1)}, s32[2,3]{1,0:T(2,128)}, u32[]{:S(2)}) copy-start(s32[2,3]{1,0:T(2,128)} %param.11) | copy-start | bytes 76
  0.7 24.2 %copy-start.1 = (f32[3,384]{1,0:T(4,128)S(1)}, f32[3,384]{1,0:T(4,128)}, u32[]{:S(2)}) copy-start(f32[3,384]{1,0:T(4,128)} %param.12) | copy-start | bytes 13828
  2.4 22.6 %collective-permute-start = (f32[2,8,576]{2,1,0:T(8,128)S(1)}, f32[2,8,576]{2,1,0:T(8,128)S(1)}, u32[]{:S(2)}, u32[]{:S(2)}) collective-permute-start(f32[2,8,576]{2,1,0:T(8,128)S(1)} %reshape.48), channel_id=1, source_target_pairs={{0,1},{1,2},{2,3},{3,4},{4,5},{5,6},{6,7},{7,8},{8,9},{9,10},{10,1... | collective-permute-start | bytes 110600 | tf_op jit(solution)/shard_map/ppermute | solution.py:18
  4.7 20.2 %collective-permute-start.1 = (f32[2,8,576]{2,1,0:T(8,128)S(1)}, f32[2,8,576]{2,1,0:T(8,128)S(1)}, u32[]{:S(2)}, u32[]{:S(2)}) collective-permute-start(f32[2,8,576]{2,1,0:T(8,128)S(1)} %reshape.48), channel_id=1, source_target_pairs={{1,0},{2,1},{3,2},{4,3},{5,4},{6,5},{7,6},{8,7},{9,8},{10,9},{11,1... | collective-permute-start | bytes 110600 | tf_op jit(solution)/shard_map/ppermute | solution.py:21
  18.2 17.2 %collective-permute-start.2 = (f32[2,8,576]{2,1,0:T(8,128)S(1)}, f32[2,8,576]{2,1,0:T(8,128)S(1)}, u32[]{:S(2)}, u32[]{:S(2)}) collective-permute-start(f32[2,8,576]{2,1,0:T(8,128)S(1)} %get-tuple-element.12), channel_id=1, source_target_pairs={{0,1},{1,2},{2,3},{3,4},{4,5},{5,6},{6,7},{7,8},{8,9},{9,10},{10,1... | collective-permute-start | bytes 110600 | tf_op jit(solution)/shard_map/ppermute | solution.py:29
  23.4 12.1 %collective-permute-start.3 = (f32[2,8,576]{2,1,0:T(8,128)S(1)}, f32[2,8,576]{2,1,0:T(8,128)S(1)}, u32[]{:S(2)}, u32[]{:S(2)}) collective-permute-start(f32[2,8,576]{2,1,0:T(8,128)S(1)} %get-tuple-element.13), channel_id=1, source_target_pairs={{1,0},{2,1},{3,2},{4,3},{5,4},{6,5},{7,6},{8,7},{9,8},{10,9},{11,1... | collective-permute-start | bytes 110600 | tf_op jit(solution)/shard_map/ppermute | solution.py:29
  112.5 19.8 %collective-permute-start.4 = (f32[2,8,576]{2,1,0:T(8,128)S(1)}, f32[2,8,576]{2,1,0:T(8,128)S(1)}, u32[]{:S(2)}, u32[]{:S(2)}) collective-permute-start(f32[2,8,576]{2,1,0:T(8,128)S(1)} %reshape.52), channel_id=1, source_target_pairs={{0,1},{1,2},{2,3},{3,4},{4,5},{5,6},{6,7},{7,8},{8,9},{9,10},{10,1... | collective-permute-start | bytes 110600 | tf_op jit(solution)/shard_map/ppermute | solution.py:18
  114.2 18.0 %collective-permute-start.5 = (f32[2,8,576]{2,1,0:T(8,128)S(1)}, f32[2,8,576]{2,1,0:T(8,128)S(1)}, u32[]{:S(2)}, u32[]{:S(2)}) collective-permute-start(f32[2,8,576]{2,1,0:T(8,128)S(1)} %reshape.52), channel_id=1, source_target_pairs={{1,0},{2,1},{3,2},{4,3},{5,4},{6,5},{7,6},{8,7},{9,8},{10,9},{11,1... | collective-permute-start | bytes 110600 | tf_op jit(solution)/shard_map/ppermute | solution.py:21
  127.7 15.1 %collective-permute-start.6 = (f32[2,8,576]{2,1,0:T(8,128)S(1)}, f32[2,8,576]{2,1,0:T(8,128)S(1)}, u32[]{:S(2)}, u32[]{:S(2)}) collective-permute-start(f32[2,8,576]{2,1,0:T(8,128)S(1)} %get-tuple-element.10), channel_id=1, source_target_pairs={{0,1},{1,2},{2,3},{3,4},{4,5},{5,6},{6,7},{7,8},{8,9},{9,10},{10,1... | collective-permute-start | bytes 110600 | tf_op jit(solution)/shard_map/ppermute | solution.py:29
  130.7 12.0 %collective-permute-start.7 = (f32[2,8,576]{2,1,0:T(8,128)S(1)}, f32[2,8,576]{2,1,0:T(8,128)S(1)}, u32[]{:S(2)}, u32[]{:S(2)}) collective-permute-start(f32[2,8,576]{2,1,0:T(8,128)S(1)} %get-tuple-element.11), channel_id=1, source_target_pairs={{1,0},{2,1},{3,2},{4,3},{5,4},{6,5},{7,6},{8,7},{9,8},{10,9},{11,1... | collective-permute-start | bytes 110600 | tf_op jit(solution)/shard_map/ppermute | solution.py:29
where the time goes:
time: 185 us; the launch traced here: 184 us
  blocking collectives  96.5 us (52%)
  matrix products  50.4 us (27%)
  starting transfers between devices  17.7 us (10%)
  other arithmetic  13.4 us (7%)
  local copies, waits for them, and re-layouts  4.56 us (2%)
    psum x1, blocking collectives, shards(): res_gram = lax.psum(inner_gram(loads, loads), 'row')  35.6 us
    psum x1, blocking collectives, shards(): curvature = lax.psum(inner_gram(direction, image), 'row')  31.4 us
    psum x1, blocking collectives, shards(): res_next = lax.psum(inner_gram(residual, residual), 'row')  29.5 us
    dot_general x6, matrix products, shards(): jnp.einsum('rfj,rij->rfi', extended[targets], matrix, precision=precise)  26.3 us
    dot_general x6, matrix products, shards(): jnp.einsum('rfi,rij->rfj', operate_blocks, matrix, precision=precise)  20.1 us
    ppermute x4, starting transfers between devices, passed_along(): return lax.ppermute(block, axis, route)  11 us
    another operation x9, other arithmetic, solve_small(): lower = jnp.linalg.cholesky(matrix)  4.18 us
    ppermute x2, starting transfers between devices, with_halo(): lax.ppermute(lax.slice_in_dim(block, block.shape[dim] - width, None, axis...  4.1 us
  transfers between devices with their start and end apart: 8, of which 0 were waited for; matrix products, arithmetic and copies ran while one was open for 25% of the time, Pallas kernels for 0%

commit v1 on v0

v1 whole, which is shorter than its diff:
```python
import jax
import jax.numpy as jnp
from jax import lax
from jax.experimental import pallas as pl
from jax.experimental.pallas import tpu as pltpu
from jax.sharding import PartitionSpec as P

f32 = jnp.float32
bf16 = jnp.bfloat16
precise = lax.Precision.HIGHEST
slot_shift = 1.2
diag_middle = 1.25


def call(body, out_shape, in_specs, scratch=(), flops=0, name=None):
    return pl.pallas_call(
        body,
        out_shape=out_shape,
        in_specs=in_specs,
        out_specs=jax.tree.map(lambda _: pl.BlockSpec(memory_space=pltpu.VMEM), out_shape),
        scratch_shapes=list(scratch),
        compiler_params=pltpu.CompilerParams(vmem_limit_bytes=40 * 2**20),
        cost_estimate=pl.CostEstimate(flops=flops, bytes_accessed=2**20, transcendentals=0),
        name=name,
    )


vmem = pl.BlockSpec(memory_space=pltpu.VMEM)
smem = pl.BlockSpec(memory_space=pltpu.SMEM)


def gram(left, right):
    return lax.dot_general(
        left, right, (((1,), (1,)), ((), ())), precision=precise, preferred_element_type=f32
    )


def parts_of(x):
    high = x.astype(bf16).astype(f32)
    return jnp.concatenate([high, x - high], axis=0).astype(bf16)


def whole_of(x16):
    half = x16.shape[0] // 2
    return x16[:half] + x16[half:]


def plain_dot(x, matrix):
    return lax.dot_general(x, matrix, (((1,), (0,)), ((), ())), preferred_element_type=f32)


def turned_dot(x, matrix):
    return lax.dot_general(x, matrix, (((1,), (1,)), ((), ())), preferred_element_type=f32)


def slot_of(cols, r, k, blocks):
    me = lax.axis_index("row")
    place = cols[r, k] - (me - 1) * blocks
    low = place < blocks
    high = place >= 2 * blocks
    swapped = jnp.where(low, place + 2 * blocks, jnp.where(high, place - 2 * blocks, place))
    return jnp.where(me % 2 == 0, swapped, place)


def prepare(loads, interior, stiff, r0, y0, dg, mk, *, blocks, shift):
    comps = loads.shape[1]
    bn = loads.shape[2] // blocks
    for b in range(blocks):
        nodes = pl.ds(b * bn, bn)
        inside = interior[:, nodes].astype(f32)
        inside = jnp.concatenate([inside] * comps, axis=1)
        field = jnp.concatenate([loads[:, c, nodes] for c in range(comps)], axis=1)
        own = jnp.concatenate([stiff[c : c + 1, nodes] for c in range(comps)], axis=1)
        r0[b] = field
        y0[b] = field * inside
        mk[b] = inside
        dg[b] = own - shift


def reverse_products(kh, kl, cols, ycat, acc):
    blocks, slots = kh.shape[0], kh.shape[1]
    acc[...] = jnp.zeros_like(acc)
    for r in range(blocks):
        for k in range(slots):
            s = slot_of(cols, r, k, blocks)
            acc[s] += plain_dot(ycat[r], kh[r, k]) + plain_dot(ycat[r], kl[r, k])


def reverse_first(coupling, cols, y0, kh, kl, out_e, out_m, out_o, acc):
    blocks, slots = coupling.shape[0], coupling.shape[1]
    acc[...] = jnp.zeros_like(acc)
    for r in range(blocks):
        ycat = parts_of(y0[r])
        for k in range(slots):
            matrix = coupling[r, k]
            high = matrix.astype(bf16)
            low = (matrix - high.astype(f32)).astype(bf16)
            kh[r, k] = high
            kl[r, k] = low
            s = slot_of(cols, r, k, blocks)
            acc[s] += plain_dot(ycat, high) + plain_dot(ycat, low)
    for b in range(blocks):
        out_e[b] = whole_of(acc[b])
        out_m[b] = whole_of(acc[blocks + b])
        out_o[b] = whole_of(acc[2 * blocks + b])


def forward(kh, kl, cols, y, y_e, y_o, x, dg, mk, own, result, xcat):
    blocks, slots = kh.shape[0], kh.shape[1]
    for b in range(blocks):
        xcat[b] = parts_of(y_e[b])
        xcat[blocks + b] = parts_of(y[b])
        xcat[2 * blocks + b] = parts_of(y_o[b])
    for r in range(blocks):
        total = jnp.zeros(xcat.shape[1:], f32)
        for k in range(slots):
            field = xcat[slot_of(cols, r, k, blocks)]
            total += turned_dot(field, kh[r, k]) + turned_dot(field, kl[r, k])
        result[r] = dg[r] * x[r] + mk[r] * (whole_of(total) + own[r])


def reverse_second(kh, kl, cols, y1, r0, w, dg, mk, out_e, out_m, out_o, grams, acc):
    blocks, slots = kh.shape[0], kh.shape[1]
    fields = y1.shape[1]
    acc[...] = jnp.zeros_like(acc)
    for r in range(blocks):
        ycat = parts_of(y1[r])
        for k in range(slots):
            s = slot_of(cols, r, k, blocks)
            acc[s] += plain_dot(ycat, kh[r, k]) + plain_dot(ycat, kl[r, k])
    h00 = h01 = h11 = h12 = jnp.zeros((fields, fields), f32)
    for b in range(blocks):
        own = whole_of(acc[blocks + b])
        out_e[b] = whole_of(acc[b])
        out_m[b] = own
        out_o[b] = whole_of(acc[2 * blocks + b])
        h00 += gram(r0[b], r0[b])
        h01 += gram(r0[b], w[b])
        h11 += gram(w[b], w[b])
        h12 += gram(w[b], dg[b] * w[b]) + gram(own, y1[b]) + gram(y1[b], own)
    rest = jnp.zeros((fields, grams.shape[1] - 4 * fields), f32)
    grams[...] = jnp.concatenate([h00, h01, h11, h12, rest], axis=1)


def halo_grams(out_e, out_o, y_e, y_o, grams, result):
    fields = out_e.shape[1]
    cross = jnp.zeros((fields, fields), f32)
    for b in range(out_e.shape[0]):
        cross += gram(out_e[b], y_e[b]) + gram(y_e[b], out_e[b])
        cross += gram(out_o[b], y_o[b]) + gram(y_o[b], out_o[b])
    before = jnp.zeros((fields, 3 * fields), f32)
    after = jnp.zeros((fields, result.shape[1] - 4 * fields), f32)
    result[...] = grams[...] + jnp.concatenate([before, cross, after], axis=1)


def eliminate(system, count):
    rows = lax.broadcasted_iota(jnp.int32, system.shape, 0)
    for k in range(count):
        pivot = system[k : k + 1, :] / system[k : k + 1, k : k + 1]
        rest = system - system[:, k : k + 1] * pivot
        system = jnp.where(rows == k, pivot, rest)
    return system


def small_dot(left, right):
    total = left[:, 0:1] * right[0:1, :]
    for k in range(1, left.shape[1]):
        total += left[:, k : k + 1] * right[k : k + 1, :]
    return total


def finish(*refs, rounds, shift):
    gram_refs = refs[:rounds]
    r0, w, up, mk, from_e, from_o, disp, resid = refs[rounds:]
    blocks, fields = r0.shape[0], r0.shape[1]
    comps = disp.shape[1]
    bn = disp.shape[2] // blocks
    sums = gram_refs[0][...]
    for ref in gram_refs[1:]:
        sums += ref[...]
    h00, h01, h11, h12 = (sums[:, i * fields : (i + 1) * fields] for i in range(4))
    eye = (
        lax.broadcasted_iota(jnp.int32, (fields, fields), 0)
        == lax.broadcasted_iota(jnp.int32, (fields, fields), 1)
    ).astype(f32)
    first = eliminate(jnp.concatenate([shift * h00 + h01, h00, h01], axis=1), fields)
    step, keep = first[:, fields : 2 * fields], first[:, 2 * fields : 3 * fields]
    inverse = eliminate(jnp.concatenate([h00, eye], axis=1), fields)[:, fields : 2 * fields]
    step_t = step.T
    keep_t = keep.T
    h00k = small_dot(h00, keep)
    h01k = small_dot(h01, keep)
    h01s = small_dot(h01, step)
    h11s = small_dot(h11, step)
    h12s = small_dot(h12, step)
    rho = small_dot(keep_t, h00k - h01s) + small_dot(step_t, h11s - h01k)
    mixing = small_dot(inverse, rho)
    lead = keep + mixing
    lead_t = lead.T
    h00p = small_dot(h00, lead)
    h01p = small_dot(h01, lead)
    h11p = small_dot(h11, lead)
    curvature = small_dot(lead_t, shift * (h00p - h01s) + h01p - h11s) + small_dot(
        step_t, shift * (h11s - h01p) + h12s - h11p
    )
    second = eliminate(jnp.concatenate([curvature, rho], axis=1), fields)
    after = second[:, fields : 2 * fields]
    lead_after = small_dot(lead, after)
    step_after = small_dot(step, after)
    zero = jnp.zeros_like(eye)
    mix = jnp.concatenate(
        [
            jnp.concatenate([step + lead_after, keep - shift * lead_after], axis=1),
            jnp.concatenate([-step_after, shift * step_after - step - lead_after], axis=1),
            jnp.concatenate([zero, step_after], axis=1),
        ],
        axis=0,
    )
    for b in range(blocks):
        u = up[b] + mk[b] * (from_e[b] + from_o[b])
        basis = jnp.concatenate([r0[b], w[b], u], axis=0)
        both = lax.dot_general(
            mix, basis, (((0,), (0,)), ((), ())), precision=precise, preferred_element_type=f32
        )
        for c in range(comps):
            piece = both[:, c * bn : (c + 1) * bn]
            disp[:, c, b * bn : (b + 1) * bn] = piece[:fields]
            resid[:, c, b * bn : (b + 1) * bn] = piece[fields:]


def even_swap(x):
    count = lax.axis_size("row")
    return lax.ppermute(x, "row", [(i, i ^ 1) for i in range(count)])


def odd_swap(x):
    groups, count = lax.axis_size("groups"), lax.axis_size("row")
    route = []
    for g in range(groups):
        for i in range(count):
            if i == 0 or i == count - 1:
                other = g ^ 1 if (g ^ 1) < groups else g
                route.append((g * count + i, other * count + i))
            else:
                route.append((g * count + i, g * count + ((i + 1) ^ 1) - 1))
    return lax.ppermute(x, ("groups", "row"), route)


def swapped_sums(x):
    count = lax.axis_size("row")
    base = 1
    while True:
        masks = [base, 2 * base, 3 * base] if 2 * base < count else [base]
        got = [
            lax.ppermute(x, "row", [(i, i ^ mask) for i in range(count)]) for mask in masks
        ]
        base *= len(masks) + 1
        if base >= count:
            return [x, *got]
        x = x + sum(got)


def shards(coupling, columns, stiff_diag, interior, loads):
    blocks, slots, width = coupling.shape[0], coupling.shape[1], coupling.shape[2]
    fields, comps, nodes = loads.shape
    shift = slot_shift * slots + diag_middle
    flops = 8 * 2 * fields * blocks * slots * width * width
    field = jax.ShapeDtypeStruct((blocks, fields, width), f32)
    row = jax.ShapeDtypeStruct((blocks, 1, width), f32)
    half = jax.ShapeDtypeStruct(coupling.shape, bf16)
    gram_shape = jax.ShapeDtypeStruct((fields, 128), f32)
    acc = pltpu.VMEM((3 * blocks, 2 * fields, width), f32)
    cat = pltpu.VMEM((3 * blocks, 2 * fields, width), bf16)

    r0, y0, dg, mk = call(
        lambda *refs: prepare(*refs, blocks=blocks, shift=diag_middle),
        (field, field, row, row), [vmem] * 3, name="prepare",
    )(loads, interior.reshape(1, nodes), stiff_diag)
    y0_e, y0_o = even_swap(y0), odd_swap(y0)
    kh, kl, a_e, a_m, a_o = call(
        reverse_first, (half, half, field, field, field), [vmem, smem, vmem],
        [acc], flops, name="reverse_first",
    )(coupling, columns, y0)
    b_e, b_o = even_swap(a_e), odd_swap(a_o)
    wp = call(
        forward, field, [vmem, vmem, smem] + [vmem] * 7, [cat], flops, name="forward_first",
    )(kh, kl, columns, y0, y0_e, y0_o, r0, dg, mk, a_m)
    w = wp + mk * (b_e + b_o)
    y1 = w * mk
    y1_e, y1_o = even_swap(y1), odd_swap(y1)
    c_e, c_m, c_o, grams = call(
        reverse_second, (field, field, field, gram_shape), [vmem, vmem, smem] + [vmem] * 5,
        [acc], flops, name="reverse_second",
    )(kh, kl, columns, y1, r0, w, dg, mk)
    grams = call(halo_grams, gram_shape, [vmem] * 5, name="halo_grams")(
        c_e, c_o, y1_e, y1_o, grams
    )
    sums = swapped_sums(grams)
    d_e, d_o = even_swap(c_e), odd_swap(c_o)
    up = call(
        forward, field, [vmem, vmem, smem] + [vmem] * 7, [cat], flops, name="forward_second",
    )(kh, kl, columns, y1, y1_e, y1_o, w, dg, mk, c_m)
    out = jax.ShapeDtypeStruct(loads.shape, f32)
    return call(
        lambda *refs: finish(*refs, rounds=len(sums), shift=shift),
        (out, out), [vmem] * (len(sums) + 6), name="finish",
    )(*sums, r0, w, up, mk, d_e, d_o)


def solution(mesh):
    placed = (
        P(("groups", "row"), None, None, None),
        P(("groups", "row"), None),
        P(None, ("groups", "row")),
        P(("groups", "row")),
        P(None, None, ("groups", "row")),
    )
    return jax.shard_map(
        shards,
        mesh=mesh,
        in_specs=placed,
        out_specs=(P(None, None, ("groups", "row")), P(None, None, ("groups", "row"))),
        check_vma=False,
    )
```

time: 185 us -> 38.1 us (0.21)
  blocking collectives: 96.5 us -> 0 us
  matrix products: 50.4 us -> 0 us
  Pallas kernels: 0 us -> 17.2 us
  other arithmetic: 13.4 us -> 0.02 us
  starting transfers between devices: 17.7 us -> 14.2 us
    psum x3 -> x0, blocking collectives: 96.5 us -> none  [the longest x1 35.6 us: shards(): res_gram = lax.psum(inner_gram(loads, loads), 'row')]
    dot_general x21 -> x0, matrix products: 49.2 us -> none  [the longest x6 26.3 us: shards(): jnp.einsum('rfj,rij->rfi', extended[targets], matrix, precision=precise)]
    pallas_call x0 -> x7, Pallas kernels: none -> 17.2 us  [the longest x2 6 us: shards(): call(forward, field, [vmem, vmem, smem] + [vmem] * 7, [cat], flops, name=...]
    another operation x15 -> x0, other arithmetic: 8 us -> none  [the longest x9 4.18 us: solve_small(): lower = jnp.linalg.cholesky(matrix)]
    scatter-add x6 -> x0, other arithmetic: 3.67 us -> none  [shards(): outgoing = outgoing.at[targets].add(reverse)]
    ppermute x8 -> x14, starting transfers between devices: 17.7 us -> 14.2 us  [the longest x4 6.72 us: odd_swap(): return lax.ppermute(x, ('groups', 'row'), route)]
    gather x6 -> x0, local copies, waits for them, and re-layouts: 3.35 us -> none  [shards(): extended[targets]]
    unnamed x10 -> x6, local copies, waits for them, and re-layouts: 0.04 us -> 2.15 us
  transfers between devices with their start and end apart: 8 -> 14, of which waited for: 0 -> 2; matrix products, arithmetic and copies ran while one was open for 25% -> 0% of each run, Pallas kernels for 0% -> 37%
where the time goes in v1:
time: 38.1 us; the launch traced here: 37.8 us
  Pallas kernels  17.2 us (45%)
  starting transfers between devices  14.2 us (37%)
  local copies, waits for them, and re-layouts  4.07 us (11%)
  waiting for transfers between devices  1.63 us (4%)
  between operations  0.74 us (2%)
    ppermute x4, starting transfers between devices, odd_swap(): return lax.ppermute(x, ('groups', 'row'), route)  6.72 us
    ppermute x6, starting transfers between devices, swapped_sums(): lax.ppermute(x, 'row', [(i, i ^ mask) for i in range(count)])  6.51 us
    pallas_call x2, Pallas kernels, shards(): call(forward, field, [vmem, vmem, smem] + [vmem] * 7, [cat], flops, name=...  6 us
    pallas_call x1, Pallas kernels, shards(): call(reverse_first, (half, half, field, field, field), [vmem, smem, vmem]...  5.33 us
    pallas_call x1, Pallas kernels, shards(): call(reverse_second, (field, field, field, gram_shape), [vmem, vmem, smem...  2.8 us
    pallas_call x1, Pallas kernels, shards(): call(lambda *refs: finish(*refs, rounds=len(sums), shift=shift), (out, ou...  2.46 us
    unnamed x6, local copies, waits for them, and re-layouts  2.15 us
    ppermute x6, waiting for transfers between devices, swapped_sums(): lax.ppermute(x, 'row', [(i, i ^ mask) for i in range(count)])  1.33 us
  transfers between devices with their start and end apart: 14, of which 2 were waited for; matrix products, arithmetic and copies ran while one was open for 0% of the time, Pallas kernels for 37%

profile of v1, /device:TPU:0, one launch (start us, length us, event | category | flops | bytes accessed | tf_op | source)
XLA Modules:
  0.0 37.8 jit_solution(10570177659972996080)
XLA Ops:
  0.6 0.7 %reshape.7.refs_1_ = s32[1,384]{1,0:T(1,128)S(1)} reshape(s32[384]{0:T(512)} %param.8) | data formatting | bytes 3072 | tf_op jit(solution)/shard_map/reshape | solution.py:278
  1.3 0.8 %copy.7.refs_0_ = f32[8,3,384]{2,1,0:T(4,128)S(1)} copy(f32[8,3,384]{2,0,1:T(8,128)} %param.9) | data formatting | bytes 73728 | tf_op args[4]
  2.1 0.7 %copy-done.1 = f32[3,384]{1,0:T(4,128)S(1)} copy-done((f32[3,384]{1,0:T(4,128)S(1)}, f32[3,384]{1,0:T(4,128)}, u32[]{:S(2)}) %copy-start.1) | copy-done | bytes 4632
  2.9 3.0 %collective-permute-start.1 = (f32[2,8,576]{2,1,0:T(8,128)S(1)}, f32[2,8,576]{2,1,0:T(8,128)S(1)}, u32[]{:S(2)}, u32[]{:S(2)}) collective-permute-start(f32[2,8,576]{2,1,0:T(8,128)S(1)} %get-tuple-element.15.y0.y), channel_id=1, source_target_pairs={{0,16},{1,2},{2,1},{3,4},{4,3},{5,6},{6,5},{7,8},{8,7},{9,10},{10,... | collective-permute-start | bytes 110600 | tf_op jit(solution)/shard_map/ppermute | solution.py:246
  6.0 0.7 %copy-done = s32[2,3]{1,0:T(2,128)S(1)} copy-done((s32[2,3]{1,0:T(2,128)S(1)}, s32[2,3]{1,0:T(2,128)}, u32[]{:S(2)}) %copy-start) | copy-done | bytes 48
  6.7 5.3 %reverse_first.1 = (bf16[2,3,576,576]{3,2,1,0:T(8,128)(2,1)S(1)}, bf16[2,3,576,576]{3,2,1,0:T(8,128)(2,1)S(1)}, f32[2,8,576]{2,1,0:T(8,128)S(1)}, f32[2,8,576]{2,1,0:T(8,128)S(1)}, f32[2,8,576]{2,1,0:T(8,128)S(1)}) custom-call(f32[2,3,576,576]{3,2,1,0:T(8,128)} %coupling.1, s32[2,3]{1,0:T(2,128)S(1)} %copy-done, f32[2,8,576]{2,1,0:T(8,128)S(1)} %get-tuple-element.15.y0.y), custom_call_target="tpu_custom_call" | custom-call | flops 254803968 | bytes 1048576 | tf_op jit(solution)/shard_map/reverse_first/pallas_call | solution.py:280
  12.0 0.4 %collective-permute-start.2 = (f32[2,8,576]{2,1,0:T(8,128)S(1)}, f32[2,8,576]{2,1,0:T(8,128)S(1)}, u32[]{:S(2)}, u32[]{:S(2)}) collective-permute-start(f32[2,8,576]{2,1,0:T(8,128)S(1)} %get-tuple-element.22), channel_id=1, source_target_pairs={{0,1},{1,0},{2,3},{3,2},{4,5},{5,4},{6,7},{7,6},{8,9},{9,8},{10,11... | collective-permute-start | bytes 110600 | tf_op jit(solution)/shard_map/ppermute | solution.py:233
  12.5 1.2 %collective-permute-start.3 = (f32[2,8,576]{2,1,0:T(8,128)S(1)}, f32[2,8,576]{2,1,0:T(8,128)S(1)}, u32[]{:S(2)}, u32[]{:S(2)}) collective-permute-start(f32[2,8,576]{2,1,0:T(8,128)S(1)} %get-tuple-element.23), channel_id=1, source_target_pairs={{0,16},{1,2},{2,1},{3,4},{4,3},{5,6},{6,5},{7,8},{8,7},{9,10},{10,... | collective-permute-start | bytes 110600 | tf_op jit(solution)/shard_map/ppermute | solution.py:246
  13.7 3.0 %forward_first.1 = f32[2,8,576]{2,1,0:T(8,128)S(1)} custom-call(bf16[2,3,576,576]{3,2,1,0:T(8,128)(2,1)S(1)} %get-tuple-element.16.kh, bf16[2,3,576,576]{3,2,1,0:T(8,128)(2,1)S(1)} %get-tuple-element.17.kl, s32[2,3]{1,0:T(2,128)S(1)} %copy-done, f32[2,8,576]{2,1,0:T(8,128)S(1)} %get-tuple-element.15.y0.y, f32[2,8,576]{2,1,0:T(8,128)S(1)} %collective-permute-done.y_e, ...), custom_call_target="tpu_custom_call" | custom-call | flops 254803968 | bytes 1048576 | tf_op jit(solution)/shard_map/forward_first/pallas_call | solution.py:285
  16.8 1.0 %collective-permute-start.5 = (f32[2,8,576]{2,1,0:T(8,128)S(1)}, f32[2,8,576]{2,1,0:T(8,128)S(1)}, u32[]{:S(2)}, u32[]{:S(2)}) collective-permute-start(f32[2,8,576]{2,1,0:T(8,128)S(1)} %get-tuple-element.30.y1.y), channel_id=1, source_target_pairs={{0,16},{1,2},{2,1},{3,4},{4,3},{5,6},{6,5},{7,8},{8,7},{9,10},{10,... | collective-permute-start | bytes 110600 | tf_op jit(solution)/shard_map/ppermute | solution.py:246
  17.8 2.8 %reverse_second.1 = (f32[2,8,576]{2,1,0:T(8,128)S(1)}, f32[2,8,576]{2,1,0:T(8,128)S(1)}, f32[2,8,576]{2,1,0:T(8,128)S(1)}, f32[8,128]{1,0:T(8,128)S(1)}) custom-call(bf16[2,3,576,576]{3,2,1,0:T(8,128)(2,1)S(1)} %get-tuple-element.16.kh, bf16[2,3,576,576]{3,2,1,0:T(8,128)(2,1)S(1)} %get-tuple-element.17.kl, s32[2,3]{1,0:T(2,128)S(1)} %copy-done, ...), custom_call_target="tpu_custom_call" | custom-call | flops 254803968 | bytes 1048576 | tf_op jit(solution)/shard_map/reverse_second/pallas_call | solution.py:291
  20.8 0.5 %halo_grams.1 = f32[8,128]{1,0:T(8,128)S(1)} custom-call(f32[2,8,576]{2,1,0:T(8,128)S(1)} %get-tuple-element.24.out_e, f32[2,8,576]{2,1,0:T(8,128)S(1)} %get-tuple-element.25.out_o, f32[2,8,576]{2,1,0:T(8,128)S(1)} %collective-permute-done.4.y_e, f32[2,8,576]{2,1,0:T(8,128)S(1)} %collective-permute-done.5.y_o, f32[8,128]{1,0:T(8,128)S(1)} %get-tuple-element.26.grams), custom_call_target="tpu_custom_call" | custom-call | bytes 1048576 | tf_op jit(solution)/shard_map/halo_grams/pallas_call | solution.py:295
  21.3 1.7 %collective-permute-start.8 = (f32[8,128]{1,0:T(8,128)S(1)}, f32[8,128]{1,0:T(8,128)S(1)}, u32[]{:S(2)}, u32[]{:S(2)}) collective-permute-start(f32[8,128]{1,0:T(8,128)S(1)} %halo_grams.1), channel_id=1, source_target_pairs={{0,3},{1,2},{2,1},{3,0},{4,7},{5,6},{6,5},{7,4},{8,11},{9,10},{10,... | collective-permute-start | bytes 12296 | tf_op jit(solution)/shard_map/ppermute | solution.py:255
  23.0 0.3 collective-permute-start.7
  23.4 0.4 %collective-permute-start.12 = (f32[2,8,576]{2,1,0:T(8,128)S(1)}, f32[2,8,576]{2,1,0:T(8,128)S(1)}, u32[]{:S(2)}, u32[]{:S(2)}) collective-permute-start(f32[2,8,576]{2,1,0:T(8,128)S(1)} %get-tuple-element.24.out_e), channel_id=1, source_target_pairs={{0,1},{1,0},{2,3},{3,2},{4,5},{5,4},{6,7},{7,6},{8,9},{9,8},{10,11... | collective-permute-start | bytes 110600 | tf_op jit(solution)/shard_map/ppermute | solution.py:233
  23.8 1.5 %collective-permute-start.13 = (f32[2,8,576]{2,1,0:T(8,128)S(1)}, f32[2,8,576]{2,1,0:T(8,128)S(1)}, u32[]{:S(2)}, u32[]{:S(2)}) collective-permute-start(f32[2,8,576]{2,1,0:T(8,128)S(1)} %get-tuple-element.25.out_o), channel_id=1, source_target_pairs={{0,16},{1,2},{2,1},{3,4},{4,3},{5,6},{6,5},{7,8},{8,7},{9,10},{10,... | collective-permute-start | bytes 110600 | tf_op jit(solution)/shard_map/ppermute | solution.py:246
  25.3 1.3 %collective-permute-done.7 = f32[8,128]{1,0:T(8,128)S(1)} collective-permute-done((f32[8,128]{1,0:T(8,128)S(1)}, f32[8,128]{1,0:T(8,128)S(1)}, u32[]{:S(2)}, u32[]{:S(2)}) %collective-permute-start.7) | collective-permute-done | bytes 4128 | tf_op jit(solution)/shard_map/ppermute | solution.py:255
  26.6 2.5 %collective-permute-start.11 = (f32[8,128]{1,0:T(8,128)S(1)}, f32[8,128]{1,0:T(8,128)S(1)}, u32[]{:S(2)}, u32[]{:S(2)}) collective-permute-start(f32[8,128]{1,0:T(8,128)S(1)} %add_add_fusion.refs_0_), channel_id=1, source_target_pairs={{0,12},{1,13},{2,14},{3,15},{4,8},{5,9},{6,10},{7,11},{8,4},{9,5},... | collective-permute-start | bytes 12296 | tf_op jit(solution)/shard_map/ppermute | solution.py:255
  29.1 0.7 %collective-permute-start.10 = (f32[8,128]{1,0:T(8,128)S(1)}, f32[8,128]{1,0:T(8,128)S(1)}, u32[]{:S(2)}, u32[]{:S(2)}) collective-permute-start(f32[8,128]{1,0:T(8,128)S(1)} %add_add_fusion.refs_0_), channel_id=1, source_target_pairs={{0,8},{1,9},{2,10},{3,11},{4,12},{5,13},{6,14},{7,15},{8,0},{9,1},... | collective-permute-start | bytes 12296 | tf_op jit(solution)/shard_map/ppermute | solution.py:255
  29.7 1.3 %collective-permute-start.9 = (f32[8,128]{1,0:T(8,128)S(1)}, f32[8,128]{1,0:T(8,128)S(1)}, u32[]{:S(2)}, u32[]{:S(2)}) collective-permute-start(f32[8,128]{1,0:T(8,128)S(1)} %add_add_fusion.refs_0_), channel_id=1, source_target_pairs={{0,4},{1,5},{2,6},{3,7},{4,0},{5,1},{6,2},{7,3},{8,12},{9,13},{10,... | collective-permute-start | bytes 12296 | tf_op jit(solution)/shard_map/ppermute | solution.py:255
  31.1 3.0 %forward_second.1.refs_6_ = f32[2,8,576]{2,1,0:T(8,128)S(1)} custom-call(bf16[2,3,576,576]{3,2,1,0:T(8,128)(2,1)S(1)} %get-tuple-element.16.kh, bf16[2,3,576,576]{3,2,1,0:T(8,128)(2,1)S(1)} %get-tuple-element.17.kl, s32[2,3]{1,0:T(2,128)S(1)} %copy-done, f32[2,8,576]{2,1,0:T(8,128)S(1)} %get-tuple-element.30.y1.y, ...), custom_call_target="tpu_custom_call" | custom-call | flops 254803968 | bytes 1048576 | tf_op jit(solution)/shard_map/forward_second/pallas_call | solution.py:300
  34.1 2.5 %finish.1 = (f32[8,3,384]{2,1,0:T(4,128)S(1)}, f32[8,3,384]{2,1,0:T(4,128)S(1)}) custom-call(f32[8,128]{1,0:T(8,128)S(1)} %add_add_fusion.refs_0_, f32[8,128]{1,0:T(8,128)S(1)} %collective-permute-done.9.refs_1_, f32[8,128]{1,0:T(8,128)S(1)} %collective-permute-done.10.refs_2_, f32[8,128]{1,0:T(8,128)S(1)} %collective-permute-done.11.refs_3_, ...), custom_call_target="tpu_custom_call" | custom-call | bytes 1048576 | tf_op jit(solution)/shard_map/finish/pallas_call | solution.py:304
  36.6 0.6 %copy.8 = f32[8,3,384]{2,0,1:T(8,128)} copy(f32[8,3,384]{2,1,0:T(4,128)S(1)} %get-tuple-element.28) | data formatting | bytes 73728 | tf_op jit(solution)/shard_map/finish/pallas_call | solution.py:304
  37.2 0.6 %copy.9 = f32[8,3,384]{2,0,1:T(8,128)} copy(f32[8,3,384]{2,1,0:T(4,128)S(1)} %get-tuple-element.29) | data formatting | bytes 73728 | tf_op jit(solution)/shard_map/finish/pallas_call | solution.py:304
  (22 shorter events, 0.7 us)
Async XLA Ops:
  2.1 0.7 %copy-start.1 = (f32[3,384]{1,0:T(4,128)S(1)}, f32[3,384]{1,0:T(4,128)}, u32[]{:S(2)}) copy-start(f32[3,384]{1,0:T(4,128)} %refs_2_.1) | copy-start | bytes 13828
  2.9 10.8 %collective-permute-start.1 = (f32[2,8,576]{2,1,0:T(8,128)S(1)}, f32[2,8,576]{2,1,0:T(8,128)S(1)}, u32[]{:S(2)}, u32[]{:S(2)}) collective-permute-start(f32[2,8,576]{2,1,0:T(8,128)S(1)} %get-tuple-element.15.y0.y), channel_id=1, source_target_pairs={{0,16},{1,2},{2,1},{3,4},{4,3},{5,6},{6,5},{7,8},{8,7},{9,10},{10,... | collective-permute-start | bytes 110600 | tf_op jit(solution)/shard_map/ppermute | solution.py:246
  5.9 7.8 %collective-permute-start = (f32[2,8,576]{2,1,0:T(8,128)S(1)}, f32[2,8,576]{2,1,0:T(8,128)S(1)}, u32[]{:S(2)}, u32[]{:S(2)}) collective-permute-start(f32[2,8,576]{2,1,0:T(8,128)S(1)} %get-tuple-element.15.y0.y), channel_id=1, source_target_pairs={{0,1},{1,0},{2,3},{3,2},{4,5},{5,4},{6,7},{7,6},{8,9},{9,8},{10,11... | collective-permute-start | bytes 110600 | tf_op jit(solution)/shard_map/ppermute | solution.py:233
  6.0 0.7 %copy-start = (s32[2,3]{1,0:T(2,128)S(1)}, s32[2,3]{1,0:T(2,128)}, u32[]{:S(2)}) copy-start(s32[2,3]{1,0:T(2,128)} %cols.7) | copy-start | bytes 76
  12.0 4.7 %collective-permute-start.2 = (f32[2,8,576]{2,1,0:T(8,128)S(1)}, f32[2,8,576]{2,1,0:T(8,128)S(1)}, u32[]{:S(2)}, u32[]{:S(2)}) collective-permute-start(f32[2,8,576]{2,1,0:T(8,128)S(1)} %get-tuple-element.22), channel_id=1, source_target_pairs={{0,1},{1,0},{2,3},{3,2},{4,5},{5,4},{6,7},{7,6},{8,9},{9,8},{10,11... | collective-permute-start | bytes 110600 | tf_op jit(solution)/shard_map/ppermute | solution.py:233
  12.5 4.2 %collective-permute-start.3 = (f32[2,8,576]{2,1,0:T(8,128)S(1)}, f32[2,8,576]{2,1,0:T(8,128)S(1)}, u32[]{:S(2)}, u32[]{:S(2)}) collective-permute-start(f32[2,8,576]{2,1,0:T(8,128)S(1)} %get-tuple-element.23), channel_id=1, source_target_pairs={{0,16},{1,2},{2,1},{3,4},{4,3},{5,6},{6,5},{7,8},{8,7},{9,10},{10,... | collective-permute-start | bytes 110600 | tf_op jit(solution)/shard_map/ppermute | solution.py:246
  16.8 4.1 %collective-permute-start.5 = (f32[2,8,576]{2,1,0:T(8,128)S(1)}, f32[2,8,576]{2,1,0:T(8,128)S(1)}, u32[]{:S(2)}, u32[]{:S(2)}) collective-permute-start(f32[2,8,576]{2,1,0:T(8,128)S(1)} %get-tuple-element.30.y1.y), channel_id=1, source_target_pairs={{0,16},{1,2},{2,1},{3,4},{4,3},{5,6},{6,5},{7,8},{8,7},{9,10},{10,... | collective-permute-start | bytes 110600 | tf_op jit(solution)/shard_map/ppermute | solution.py:246
  17.8 3.1 %collective-permute-start.4 = (f32[2,8,576]{2,1,0:T(8,128)S(1)}, f32[2,8,576]{2,1,0:T(8,128)S(1)}, u32[]{:S(2)}, u32[]{:S(2)}) collective-permute-start(f32[2,8,576]{2,1,0:T(8,128)S(1)} %get-tuple-element.30.y1.y), channel_id=1, source_target_pairs={{0,1},{1,0},{2,3},{3,2},{4,5},{5,4},{6,7},{7,6},{8,9},{9,8},{10,11... | collective-permute-start | bytes 110600 | tf_op jit(solution)/shard_map/ppermute | solution.py:233
  21.3 4.0 %collective-permute-start.8 = (f32[8,128]{1,0:T(8,128)S(1)}, f32[8,128]{1,0:T(8,128)S(1)}, u32[]{:S(2)}, u32[]{:S(2)}) collective-permute-start(f32[8,128]{1,0:T(8,128)S(1)} %halo_grams.1), channel_id=1, source_target_pairs={{0,3},{1,2},{2,1},{3,0},{4,7},{5,6},{6,5},{7,4},{8,11},{9,10},{10,... | collective-permute-start | bytes 12296 | tf_op jit(solution)/shard_map/ppermute | solution.py:255
  23.0 3.6 %collective-permute-start.7 = (f32[8,128]{1,0:T(8,128)S(1)}, f32[8,128]{1,0:T(8,128)S(1)}, u32[]{:S(2)}, u32[]{:S(2)}) collective-permute-start(f32[8,128]{1,0:T(8,128)S(1)} %halo_grams.1), channel_id=1, source_target_pairs={{0,2},{1,3},{2,0},{3,1},{4,6},{5,7},{6,4},{7,5},{8,10},{9,11},{10,... | collective-permute-start | bytes 12296 | tf_op jit(solution)/shard_map/ppermute | solution.py:255
  23.3 3.3 %collective-permute-start.6 = (f32[8,128]{1,0:T(8,128)S(1)}, f32[8,128]{1,0:T(8,128)S(1)}, u32[]{:S(2)}, u32[]{:S(2)}) collective-permute-start(f32[8,128]{1,0:T(8,128)S(1)} %halo_grams.1), channel_id=1, source_target_pairs={{0,1},{1,0},{2,3},{3,2},{4,5},{5,4},{6,7},{7,6},{8,9},{9,8},{10,11... | collective-permute-start | bytes 12296 | tf_op jit(solution)/shard_map/ppermute | solution.py:255
  23.4 10.7 %collective-permute-start.12 = (f32[2,8,576]{2,1,0:T(8,128)S(1)}, f32[2,8,576]{2,1,0:T(8,128)S(1)}, u32[]{:S(2)}, u32[]{:S(2)}) collective-permute-start(f32[2,8,576]{2,1,0:T(8,128)S(1)} %get-tuple-element.24.out_e), channel_id=1, source_target_pairs={{0,1},{1,0},{2,3},{3,2},{4,5},{5,4},{6,7},{7,6},{8,9},{9,8},{10,11... | collective-permute-start | bytes 110600 | tf_op jit(solution)/shard_map/ppermute | solution.py:233
  23.8 10.3 %collective-permute-start.13 = (f32[2,8,576]{2,1,0:T(8,128)S(1)}, f32[2,8,576]{2,1,0:T(8,128)S(1)}, u32[]{:S(2)}, u32[]{:S(2)}) collective-permute-start(f32[2,8,576]{2,1,0:T(8,128)S(1)} %get-tuple-element.25.out_o), channel_id=1, source_target_pairs={{0,16},{1,2},{2,1},{3,4},{4,3},{5,6},{6,5},{7,8},{8,7},{9,10},{10,... | collective-permute-start | bytes 110600 | tf_op jit(solution)/shard_map/ppermute | solution.py:246
  26.6 7.5 %collective-permute-start.11 = (f32[8,128]{1,0:T(8,128)S(1)}, f32[8,128]{1,0:T(8,128)S(1)}, u32[]{:S(2)}, u32[]{:S(2)}) collective-permute-start(f32[8,128]{1,0:T(8,128)S(1)} %add_add_fusion.refs_0_), channel_id=1, source_target_pairs={{0,12},{1,13},{2,14},{3,15},{4,8},{5,9},{6,10},{7,11},{8,4},{9,5},... | collective-permute-start | bytes 12296 | tf_op jit(solution)/shard_map/ppermute | solution.py:255
  29.1 5.0 %collective-permute-start.10 = (f32[8,128]{1,0:T(8,128)S(1)}, f32[8,128]{1,0:T(8,128)S(1)}, u32[]{:S(2)}, u32[]{:S(2)}) collective-permute-start(f32[8,128]{1,0:T(8,128)S(1)} %add_add_fusion.refs_0_), channel_id=1, source_target_pairs={{0,8},{1,9},{2,10},{3,11},{4,12},{5,13},{6,14},{7,15},{8,0},{9,1},... | collective-permute-start | bytes 12296 | tf_op jit(solution)/shard_map/ppermute | solution.py:255
  29.7 4.4 %collective-permute-start.9 = (f32[8,128]{1,0:T(8,128)S(1)}, f32[8,128]{1,0:T(8,128)S(1)}, u32[]{:S(2)}, u32[]{:S(2)}) collective-permute-start(f32[8,128]{1,0:T(8,128)S(1)} %add_add_fusion.refs_0_), channel_id=1, source_target_pairs={{0,4},{1,5},{2,6},{3,7},{4,0},{5,1},{6,2},{7,3},{8,12},{9,13},{10,... | collective-permute-start | bytes 12296 | tf_op jit(solution)/shard_map/ppermute | solution.py:255

commit v2 on v1

--- a/solution.py
+++ b/solution.py
@@ -12,14 +12,14 @@
 diag_middle = 1.25
 
 
-def call(body, out_shape, in_specs, scratch=(), flops=0, name=None):
+def call(body, out_shape, in_specs, scratch=(), flops=0, name=None, limit=24):
     return pl.pallas_call(
         body,
         out_shape=out_shape,
         in_specs=in_specs,
         out_specs=jax.tree.map(lambda _: pl.BlockSpec(memory_space=pltpu.VMEM), out_shape),
         scratch_shapes=list(scratch),
-        compiler_params=pltpu.CompilerParams(vmem_limit_bytes=40 * 2**20),
+        compiler_params=pltpu.CompilerParams(vmem_limit_bytes=limit * 2**20),
         cost_estimate=pl.CostEstimate(flops=flops, bytes_accessed=2**20, transcendentals=0),
         name=name,
     )
@@ -27,6 +27,10 @@
 
 vmem = pl.BlockSpec(memory_space=pltpu.VMEM)
 smem = pl.BlockSpec(memory_space=pltpu.SMEM)
+
+
+def in_hbm(x):
+    return pltpu.with_memory_space_constraint(x, pltpu.HBM)
 
 
 def gram(left, right):
@@ -62,14 +66,27 @@
     return jnp.where(me % 2 == 0, swapped, place)
 
 
-def prepare(loads, interior, stiff, r0, y0, dg, mk, *, blocks, shift):
-    comps = loads.shape[1]
+def prepare(
+    loads_in, interior_in, stiff_in, r0, y0, dg, mk, loads, interior, stiff, sems, *, blocks, shift
+):
+    comps = loads.shape[0]
     bn = loads.shape[2] // blocks
+    fetches = [
+        pltpu.make_async_copy(source, target, sems.at[i])
+        for i, (source, target) in enumerate(
+            ((loads_in, loads), (interior_in, interior), (stiff_in, stiff))
+        )
+    ]
+    for fetch in fetches:
+        fetch.start()
+    for fetch in fetches:
+        fetch.wait()
+    inside_all = interior[...].astype(f32).reshape(1, -1)
     for b in range(blocks):
         nodes = pl.ds(b * bn, bn)
-        inside = interior[:, nodes].astype(f32)
+        inside = inside_all[:, b * bn : (b + 1) * bn]
         inside = jnp.concatenate([inside] * comps, axis=1)
-        field = jnp.concatenate([loads[:, c, nodes] for c in range(comps)], axis=1)
+        field = jnp.concatenate([loads[c, :, nodes] for c in range(comps)], axis=1)
         own = jnp.concatenate([stiff[c : c + 1, nodes] for c in range(comps)], axis=1)
         r0[b] = field
         y0[b] = field * inside
@@ -173,7 +190,7 @@
     gram_refs = refs[:rounds]
     r0, w, up, mk, from_e, from_o, disp, resid = refs[rounds:]
     blocks, fields = r0.shape[0], r0.shape[1]
-    comps = disp.shape[1]
+    comps = disp.shape[0]
     bn = disp.shape[2] // blocks
     sums = gram_refs[0][...]
     for ref in gram_refs[1:]:
@@ -224,8 +241,8 @@
         )
         for c in range(comps):
             piece = both[:, c * bn : (c + 1) * bn]
-            disp[:, c, b * bn : (b + 1) * bn] = piece[:fields]
-            resid[:, c, b * bn : (b + 1) * bn] = piece[fields:]
+            disp[c, :, b * bn : (b + 1) * bn] = piece[:fields]
+            resid[c, :, b * bn : (b + 1) * bn] = piece[fields:]
 
 
 def even_swap(x):
@@ -274,8 +291,16 @@
 
     r0, y0, dg, mk = call(
         lambda *refs: prepare(*refs, blocks=blocks, shift=diag_middle),
-        (field, field, row, row), [vmem] * 3, name="prepare",
-    )(loads, interior.reshape(1, nodes), stiff_diag)
+        (field, field, row, row), [pl.BlockSpec(memory_space=pl.ANY)] * 3,
+        [
+            pltpu.VMEM((comps, fields, nodes), f32),
+            pltpu.VMEM((nodes,), jnp.int32),
+            pltpu.VMEM((comps, nodes), f32),
+            pltpu.SemaphoreType.DMA((3,)),
+        ],
+        flops=10**10,
+        name="prepare",
+    )(*(in_hbm(x) for x in (loads.transpose(1, 0, 2), interior, stiff_diag)))
     y0_e, y0_o = even_swap(y0), odd_swap(y0)
     kh, kl, a_e, a_m, a_o = call(
         reverse_first, (half, half, field, field, field), [vmem, smem, vmem],
@@ -300,11 +325,12 @@
     up = call(
         forward, field, [vmem, vmem, smem] + [vmem] * 7, [cat], flops, name="forward_second",
     )(kh, kl, columns, y1, y1_e, y1_o, w, dg, mk, c_m)
-    out = jax.ShapeDtypeStruct(loads.shape, f32)
-    return call(
+    out = jax.ShapeDtypeStruct((comps, fields, nodes), f32)
+    disp, resid = call(
         lambda *refs: finish(*refs, rounds=len(sums), shift=shift),
         (out, out), [vmem] * (len(sums) + 6), name="finish",
     )(*sums, r0, w, up, mk, d_e, d_o)
+    return disp.transpose(1, 0, 2), resid.transpose(1, 0, 2)
 
 
 def solution(mesh):

time: 38.1 us -> 33.3 us (0.87)
  local copies, waits for them, and re-layouts: 4.07 us -> 0.02 us
  Pallas kernels: 17.2 us -> 15.8 us
  starting transfers between devices: 14.2 us -> 15 us
    pallas_call x1, Pallas kernels: 5.33 us -> 2.42 us  [shards(): call(reverse_first, (half, half, field, field, field), [vmem, smem, vmem]...]
    unnamed x6 -> x9, local copies, waits for them, and re-layouts: 2.15 us -> 0.02 us
    pallas_call x2 -> x0, local copies, waits for them, and re-layouts: 1.24 us -> none  [shards(): call(lambda *refs: finish(*refs, rounds=len(sums), shift=shift), (out, ou...]
    pallas_call x1, Pallas kernels: 0.09 us -> 1.03 us  [shards(): call(lambda *refs: prepare(*refs, blocks=blocks, shift=diag_middle), (fie...]
    ppermute x4, starting transfers between devices: 6.72 us -> 7.43 us  [odd_swap(): return lax.ppermute(x, ('groups', 'row'), route)]
    reshape x1 -> x0, local copies, waits for them, and re-layouts: 0.68 us -> none  [shards(): interior.reshape(1, nodes)]
    pallas_call x1, Pallas kernels: 2.46 us -> 3.08 us  [shards(): call(lambda *refs: finish(*refs, rounds=len(sums), shift=shift), (out, ou...]
  transfers between devices with their start and end apart: 14 -> 14, of which waited for: 2 -> 2; matrix products, arithmetic and copies ran while one was open for 0% -> 0% of each run, Pallas kernels for 37% -> 34%
where the time goes in v2:
time: 33.3 us; the launch traced here: 33.2 us
  Pallas kernels  15.8 us (47%)
  starting transfers between devices  15 us (45%)
  waiting for transfers between devices  1.57 us (5%)
  between operations  0.77 us (2%)
    ppermute x4, starting transfers between devices, odd_swap(): return lax.ppermute(x, ('groups', 'row'), route)  7.43 us
    ppermute x6, starting transfers between devices, swapped_sums(): lax.ppermute(x, 'row', [(i, i ^ mask) for i in range(count)])  6.53 us
    pallas_call x2, Pallas kernels, shards(): call(forward, field, [vmem, vmem, smem] + [vmem] * 7, [cat], flops, name=...  6.01 us
    pallas_call x1, Pallas kernels, shards(): call(lambda *refs: finish(*refs, rounds=len(sums), shift=shift), (out, ou...  3.08 us
    pallas_call x1, Pallas kernels, shards(): call(reverse_second, (field, field, field, gram_shape), [vmem, vmem, smem...  2.81 us
    pallas_call x1, Pallas kernels, shards(): call(reverse_first, (half, half, field, field, field), [vmem, smem, vmem]...  2.42 us
    ppermute x6, waiting for transfers between devices, swapped_sums(): lax.ppermute(x, 'row', [(i, i ^ mask) for i in range(count)])  1.29 us
    pallas_call x1, Pallas kernels, shards(): call(lambda *refs: prepare(*refs, blocks=blocks, shift=diag_middle), (fie...  1.03 us
  transfers between devices with their start and end apart: 14, of which 2 were waited for; matrix products, arithmetic and copies ran while one was open for 0% of the time, Pallas kernels for 34%

profile of v2, /device:TPU:0, one launch (start us, length us, event | category | flops | bytes accessed | tf_op | source)
XLA Modules:
  0.0 33.2 jit_solution(17442239007715334147)
XLA Ops:
  0.7 1.0 %prepare.1 = (f32[2,8,576]{2,1,0:T(8,128)S(1)}, f32[2,8,576]{2,1,0:T(8,128)S(1)}, f32[2,1,576]{2,1,0:T(1,128)S(1)}, f32[2,1,576]{2,1,0:T(1,128)S(1)}) custom-call(f32[3,8,384]{2,1,0:T(8,128)} %bitcast.9, s32[384]{0:T(512)} %refs_1_.1, f32[3,384]{1,0:T(4,128)} %refs_2_.1), custom_call_target="tpu_custom_call" | custom-call | flops 10000000000 | bytes 1048576 | tf_op jit(solution)/shard_map/prepare/pallas_call | solution.py:292
  1.7 3.0 %collective-permute-start.1 = (f32[2,8,576]{2,1,0:T(8,128)S(1)}, f32[2,8,576]{2,1,0:T(8,128)S(1)}, u32[]{:S(2)}, u32[]{:S(2)}) collective-permute-start(f32[2,8,576]{2,1,0:T(8,128)S(1)} %get-tuple-element.17.y0.y), channel_id=1, source_target_pairs={{0,16},{1,2},{2,1},{3,4},{4,3},{5,6},{6,5},{7,8},{8,7},{9,10},{10,... | collective-permute-start | bytes 110600 | tf_op jit(solution)/shard_map/ppermute | solution.py:263
  4.7 0.1 collective-permute-start
  4.9 2.4 %reverse_first.1 = (bf16[2,3,576,576]{3,2,1,0:T(8,128)(2,1)S(1)}, bf16[2,3,576,576]{3,2,1,0:T(8,128)(2,1)S(1)}, f32[2,8,576]{2,1,0:T(8,128)S(1)}, f32[2,8,576]{2,1,0:T(8,128)S(1)}, f32[2,8,576]{2,1,0:T(8,128)S(1)}) custom-call(f32[2,3,576,576]{3,2,1,0:T(8,128)S(1)} %bitcast.7, s32[2,3]{1,0:T(2,128)S(1)} %copy-done, f32[2,8,576]{2,1,0:T(8,128)S(1)} %get-tuple-element.17.y0.y), custom_call_target="tpu_custom_call" | custom-call | flops 254803968 | bytes 1048576 | tf_op jit(solution)/shard_map/reverse_first/pallas_call | solution.py:305
  7.3 0.4 %collective-permute-start.2 = (f32[2,8,576]{2,1,0:T(8,128)S(1)}, f32[2,8,576]{2,1,0:T(8,128)S(1)}, u32[]{:S(2)}, u32[]{:S(2)}) collective-permute-start(f32[2,8,576]{2,1,0:T(8,128)S(1)} %get-tuple-element.24), channel_id=1, source_target_pairs={{0,1},{1,0},{2,3},{3,2},{4,5},{5,4},{6,7},{7,6},{8,9},{9,8},{10,11... | collective-permute-start | bytes 110600 | tf_op jit(solution)/shard_map/ppermute | solution.py:250
  7.7 1.9 %collective-permute-start.3 = (f32[2,8,576]{2,1,0:T(8,128)S(1)}, f32[2,8,576]{2,1,0:T(8,128)S(1)}, u32[]{:S(2)}, u32[]{:S(2)}) collective-permute-start(f32[2,8,576]{2,1,0:T(8,128)S(1)} %get-tuple-element.25), channel_id=1, source_target_pairs={{0,16},{1,2},{2,1},{3,4},{4,3},{5,6},{6,5},{7,8},{8,7},{9,10},{10,... | collective-permute-start | bytes 110600 | tf_op jit(solution)/shard_map/ppermute | solution.py:263
  9.7 3.0 %forward_first.1 = f32[2,8,576]{2,1,0:T(8,128)S(1)} custom-call(bf16[2,3,576,576]{3,2,1,0:T(8,128)(2,1)S(1)} %get-tuple-element.18.kh, bf16[2,3,576,576]{3,2,1,0:T(8,128)(2,1)S(1)} %get-tuple-element.19.kl, s32[2,3]{1,0:T(2,128)S(1)} %copy-done, f32[2,8,576]{2,1,0:T(8,128)S(1)} %get-tuple-element.17.y0.y, f32[2,8,576]{2,1,0:T(8,128)S(1)} %collective-permute-done.y_e, ...), custom_call_target="tpu_custom_call" | custom-call | flops 254803968 | bytes 1048576 | tf_op jit(solution)/shard_map/forward_first/pallas_call | solution.py:310
  12.7 0.0 collective-permute-done.2
  12.7 1.0 %collective-permute-start.5 = (f32[2,8,576]{2,1,0:T(8,128)S(1)}, f32[2,8,576]{2,1,0:T(8,128)S(1)}, u32[]{:S(2)}, u32[]{:S(2)}) collective-permute-start(f32[2,8,576]{2,1,0:T(8,128)S(1)} %get-tuple-element.32.y1.y), channel_id=1, source_target_pairs={{0,16},{1,2},{2,1},{3,4},{4,3},{5,6},{6,5},{7,8},{8,7},{9,10},{10,... | collective-permute-start | bytes 110600 | tf_op jit(solution)/shard_map/ppermute | solution.py:263
  13.8 2.8 %reverse_second.1 = (f32[2,8,576]{2,1,0:T(8,128)S(1)}, f32[2,8,576]{2,1,0:T(8,128)S(1)}, f32[2,8,576]{2,1,0:T(8,128)S(1)}, f32[8,128]{1,0:T(8,128)S(1)}) custom-call(bf16[2,3,576,576]{3,2,1,0:T(8,128)(2,1)S(1)} %get-tuple-element.18.kh, bf16[2,3,576,576]{3,2,1,0:T(8,128)(2,1)S(1)} %get-tuple-element.19.kl, s32[2,3]{1,0:T(2,128)S(1)} %copy-done, ...), custom_call_target="tpu_custom_call" | custom-call | flops 254803968 | bytes 1048576 | tf_op jit(solution)/shard_map/reverse_second/pallas_call | solution.py:316
  16.6 0.2 collective-permute-done.5.y_o
  16.8 0.5 %halo_grams.1 = f32[8,128]{1,0:T(8,128)S(1)} custom-call(f32[2,8,576]{2,1,0:T(8,128)S(1)} %get-tuple-element.26.out_e, f32[2,8,576]{2,1,0:T(8,128)S(1)} %get-tuple-element.27.out_o, f32[2,8,576]{2,1,0:T(8,128)S(1)} %collective-permute-done.4.y_e, f32[2,8,576]{2,1,0:T(8,128)S(1)} %collective-permute-done.5.y_o, f32[8,128]{1,0:T(8,128)S(1)} %get-tuple-element.28.grams), custom_call_target="tpu_custom_call" | custom-call | bytes 1048576 | tf_op jit(solution)/shard_map/halo_grams/pallas_call | solution.py:320
  17.3 1.7 %collective-permute-start.8 = (f32[8,128]{1,0:T(8,128)S(1)}, f32[8,128]{1,0:T(8,128)S(1)}, u32[]{:S(2)}, u32[]{:S(2)}) collective-permute-start(f32[8,128]{1,0:T(8,128)S(1)} %halo_grams.1), channel_id=1, source_target_pairs={{0,3},{1,2},{2,1},{3,0},{4,7},{5,6},{6,5},{7,4},{8,11},{9,10},{10,... | collective-permute-start | bytes 12296 | tf_op jit(solution)/shard_map/ppermute | solution.py:272
  19.0 0.3 collective-permute-start.7
  19.3 0.1 collective-permute-start.6
  19.4 0.4 %collective-permute-start.12 = (f32[2,8,576]{2,1,0:T(8,128)S(1)}, f32[2,8,576]{2,1,0:T(8,128)S(1)}, u32[]{:S(2)}, u32[]{:S(2)}) collective-permute-start(f32[2,8,576]{2,1,0:T(8,128)S(1)} %get-tuple-element.26.out_e), channel_id=1, source_target_pairs={{0,1},{1,0},{2,3},{3,2},{4,5},{5,4},{6,7},{7,6},{8,9},{9,8},{10,11... | collective-permute-start | bytes 110600 | tf_op jit(solution)/shard_map/ppermute | solution.py:250
  19.8 1.5 %collective-permute-start.13 = (f32[2,8,576]{2,1,0:T(8,128)S(1)}, f32[2,8,576]{2,1,0:T(8,128)S(1)}, u32[]{:S(2)}, u32[]{:S(2)}) collective-permute-start(f32[2,8,576]{2,1,0:T(8,128)S(1)} %get-tuple-element.27.out_o), channel_id=1, source_target_pairs={{0,16},{1,2},{2,1},{3,4},{4,3},{5,6},{6,5},{7,8},{8,7},{9,10},{10,... | collective-permute-start | bytes 110600 | tf_op jit(solution)/shard_map/ppermute | solution.py:263
  21.3 1.3 %collective-permute-done.7 = f32[8,128]{1,0:T(8,128)S(1)} collective-permute-done((f32[8,128]{1,0:T(8,128)S(1)}, f32[8,128]{1,0:T(8,128)S(1)}, u32[]{:S(2)}, u32[]{:S(2)}) %collective-permute-start.7) | collective-permute-done | bytes 4128 | tf_op jit(solution)/shard_map/ppermute | solution.py:272
  22.6 2.7 %collective-permute-start.11 = (f32[8,128]{1,0:T(8,128)S(1)}, f32[8,128]{1,0:T(8,128)S(1)}, u32[]{:S(2)}, u32[]{:S(2)}) collective-permute-start(f32[8,128]{1,0:T(8,128)S(1)} %add_add_fusion.refs_0_), channel_id=1, source_target_pairs={{0,12},{1,13},{2,14},{3,15},{4,8},{5,9},{6,10},{7,11},{8,4},{9,5},... | collective-permute-start | bytes 12296 | tf_op jit(solution)/shard_map/ppermute | solution.py:272
  25.3 0.4 %collective-permute-start.10 = (f32[8,128]{1,0:T(8,128)S(1)}, f32[8,128]{1,0:T(8,128)S(1)}, u32[]{:S(2)}, u32[]{:S(2)}) collective-permute-start(f32[8,128]{1,0:T(8,128)S(1)} %add_add_fusion.refs_0_), channel_id=1, source_target_pairs={{0,8},{1,9},{2,10},{3,11},{4,12},{5,13},{6,14},{7,15},{8,0},{9,1},... | collective-permute-start | bytes 12296 | tf_op jit(solution)/shard_map/ppermute | solution.py:272
  25.7 1.3 %collective-permute-start.9 = (f32[8,128]{1,0:T(8,128)S(1)}, f32[8,128]{1,0:T(8,128)S(1)}, u32[]{:S(2)}, u32[]{:S(2)}) collective-permute-start(f32[8,128]{1,0:T(8,128)S(1)} %add_add_fusion.refs_0_), channel_id=1, source_target_pairs={{0,4},{1,5},{2,6},{3,7},{4,0},{5,1},{6,2},{7,3},{8,12},{9,13},{10,... | collective-permute-start | bytes 12296 | tf_op jit(solution)/shard_map/ppermute | solution.py:272
  27.0 3.0 %forward_second.1.refs_6_ = f32[2,8,576]{2,1,0:T(8,128)S(1)} custom-call(bf16[2,3,576,576]{3,2,1,0:T(8,128)(2,1)S(1)} %get-tuple-element.18.kh, bf16[2,3,576,576]{3,2,1,0:T(8,128)(2,1)S(1)} %get-tuple-element.19.kl, s32[2,3]{1,0:T(2,128)S(1)} %copy-done, f32[2,8,576]{2,1,0:T(8,128)S(1)} %get-tuple-element.32.y1.y, ...), custom_call_target="tpu_custom_call" | custom-call | flops 254803968 | bytes 1048576 | tf_op jit(solution)/shard_map/forward_second/pallas_call | solution.py:325
  30.0 0.0 collective-permute-done.12.refs_8_
  30.1 3.1 %finish.1 = (f32[3,8,384]{2,1,0:T(8,128)}, f32[3,8,384]{2,1,0:T(8,128)}) custom-call(f32[8,128]{1,0:T(8,128)S(1)} %add_add_fusion.refs_0_, f32[8,128]{1,0:T(8,128)S(1)} %collective-permute-done.9.refs_1_, f32[8,128]{1,0:T(8,128)S(1)} %collective-permute-done.10.refs_2_, f32[8,128]{1,0:T(8,128)S(1)} %collective-permute-done.11.refs_3_, ...), custom_call_target="tpu_custom_call" | custom-call | bytes 1048576 | tf_op jit(solution)/shard_map/finish/pallas_call | solution.py:329
  (23 shorter events, 0.1 us)
Async XLA Ops:
  0.6 4.2 %slice-start = ((s8[8847360]{0:T(1024)(128)(4,1)}), s8[4194304]{0:T(1024)(128)(4,1)S(1)}, s32[]{:S(2)}) async-start(s8[8847360]{0:T(1024)(128)(4,1)} %bitcast.6), calls=%async_computation | async-start | bytes 8388608
  0.6 4.2 %slice-start.1 = ((s8[8847360]{0:T(1024)(128)(4,1)}), s8[4194304]{0:T(1024)(128)(4,1)S(1)}, s32[]{:S(2)}) async-start(s8[8847360]{0:T(1024)(128)(4,1)} %bitcast.6), calls=%async_computation.1 | async-start | bytes 8388608
  0.7 4.2 %slice-start.2 = ((s8[8847360]{0:T(1024)(128)(4,1)}), s8[458752]{0:T(1024)(128)(4,1)S(1)}, s32[]{:S(2)}) async-start(s8[8847360]{0:T(1024)(128)(4,1)} %bitcast.6), calls=%async_computation.2 | async-start | bytes 917504
  0.7 4.2 %copy-start = (s32[2,3]{1,0:T(2,128)S(1)}, s32[2,3]{1,0:T(2,128)}, u32[]{:S(2)}) copy-start(s32[2,3]{1,0:T(2,128)} %cols.7) | copy-start | bytes 76
  1.7 8.0 %collective-permute-start.1 = (f32[2,8,576]{2,1,0:T(8,128)S(1)}, f32[2,8,576]{2,1,0:T(8,128)S(1)}, u32[]{:S(2)}, u32[]{:S(2)}) collective-permute-start(f32[2,8,576]{2,1,0:T(8,128)S(1)} %get-tuple-element.17.y0.y), channel_id=1, source_target_pairs={{0,16},{1,2},{2,1},{3,4},{4,3},{5,6},{6,5},{7,8},{8,7},{9,10},{10,... | collective-permute-start | bytes 110600 | tf_op jit(solution)/shard_map/ppermute | solution.py:263
  4.7 5.0 %collective-permute-start = (f32[2,8,576]{2,1,0:T(8,128)S(1)}, f32[2,8,576]{2,1,0:T(8,128)S(1)}, u32[]{:S(2)}, u32[]{:S(2)}) collective-permute-start(f32[2,8,576]{2,1,0:T(8,128)S(1)} %get-tuple-element.17.y0.y), channel_id=1, source_target_pairs={{0,1},{1,0},{2,3},{3,2},{4,5},{5,4},{6,7},{7,6},{8,9},{9,8},{10,11... | collective-permute-start | bytes 110600 | tf_op jit(solution)/shard_map/ppermute | solution.py:250
  7.3 5.4 %collective-permute-start.2 = (f32[2,8,576]{2,1,0:T(8,128)S(1)}, f32[2,8,576]{2,1,0:T(8,128)S(1)}, u32[]{:S(2)}, u32[]{:S(2)}) collective-permute-start(f32[2,8,576]{2,1,0:T(8,128)S(1)} %get-tuple-element.24), channel_id=1, source_target_pairs={{0,1},{1,0},{2,3},{3,2},{4,5},{5,4},{6,7},{7,6},{8,9},{9,8},{10,11... | collective-permute-start | bytes 110600 | tf_op jit(solution)/shard_map/ppermute | solution.py:250
  7.7 5.0 %collective-permute-start.3 = (f32[2,8,576]{2,1,0:T(8,128)S(1)}, f32[2,8,576]{2,1,0:T(8,128)S(1)}, u32[]{:S(2)}, u32[]{:S(2)}) collective-permute-start(f32[2,8,576]{2,1,0:T(8,128)S(1)} %get-tuple-element.25), channel_id=1, source_target_pairs={{0,16},{1,2},{2,1},{3,4},{4,3},{5,6},{6,5},{7,8},{8,7},{9,10},{10,... | collective-permute-start | bytes 110600 | tf_op jit(solution)/shard_map/ppermute | solution.py:263
  12.7 4.1 %collective-permute-start.5 = (f32[2,8,576]{2,1,0:T(8,128)S(1)}, f32[2,8,576]{2,1,0:T(8,128)S(1)}, u32[]{:S(2)}, u32[]{:S(2)}) collective-permute-start(f32[2,8,576]{2,1,0:T(8,128)S(1)} %get-tuple-element.32.y1.y), channel_id=1, source_target_pairs={{0,16},{1,2},{2,1},{3,4},{4,3},{5,6},{6,5},{7,8},{8,7},{9,10},{10,... | collective-permute-start | bytes 110600 | tf_op jit(solution)/shard_map/ppermute | solution.py:263
  13.8 3.1 %collective-permute-start.4 = (f32[2,8,576]{2,1,0:T(8,128)S(1)}, f32[2,8,576]{2,1,0:T(8,128)S(1)}, u32[]{:S(2)}, u32[]{:S(2)}) collective-permute-start(f32[2,8,576]{2,1,0:T(8,128)S(1)} %get-tuple-element.32.y1.y), channel_id=1, source_target_pairs={{0,1},{1,0},{2,3},{3,2},{4,5},{5,4},{6,7},{7,6},{8,9},{9,8},{10,11... | collective-permute-start | bytes 110600 | tf_op jit(solution)/shard_map/ppermute | solution.py:250
  17.3 4.0 %collective-permute-start.8 = (f32[8,128]{1,0:T(8,128)S(1)}, f32[8,128]{1,0:T(8,128)S(1)}, u32[]{:S(2)}, u32[]{:S(2)}) collective-permute-start(f32[8,128]{1,0:T(8,128)S(1)} %halo_grams.1), channel_id=1, source_target_pairs={{0,3},{1,2},{2,1},{3,0},{4,7},{5,6},{6,5},{7,4},{8,11},{9,10},{10,... | collective-permute-start | bytes 12296 | tf_op jit(solution)/shard_map/ppermute | solution.py:272
  19.0 3.6 %collective-permute-start.7 = (f32[8,128]{1,0:T(8,128)S(1)}, f32[8,128]{1,0:T(8,128)S(1)}, u32[]{:S(2)}, u32[]{:S(2)}) collective-permute-start(f32[8,128]{1,0:T(8,128)S(1)} %halo_grams.1), channel_id=1, source_target_pairs={{0,2},{1,3},{2,0},{3,1},{4,6},{5,7},{6,4},{7,5},{8,10},{9,11},{10,... | collective-permute-start | bytes 12296 | tf_op jit(solution)/shard_map/ppermute | solution.py:272
  19.3 3.3 %collective-permute-start.6 = (f32[8,128]{1,0:T(8,128)S(1)}, f32[8,128]{1,0:T(8,128)S(1)}, u32[]{:S(2)}, u32[]{:S(2)}) collective-permute-start(f32[8,128]{1,0:T(8,128)S(1)} %halo_grams.1), channel_id=1, source_target_pairs={{0,1},{1,0},{2,3},{3,2},{4,5},{5,4},{6,7},{7,6},{8,9},{9,8},{10,11... | collective-permute-start | bytes 12296 | tf_op jit(solution)/shard_map/ppermute | solution.py:272
  19.4 10.7 %collective-permute-start.12 = (f32[2,8,576]{2,1,0:T(8,128)S(1)}, f32[2,8,576]{2,1,0:T(8,128)S(1)}, u32[]{:S(2)}, u32[]{:S(2)}) collective-permute-start(f32[2,8,576]{2,1,0:T(8,128)S(1)} %get-tuple-element.26.out_e), channel_id=1, source_target_pairs={{0,1},{1,0},{2,3},{3,2},{4,5},{5,4},{6,7},{7,6},{8,9},{9,8},{10,11... | collective-permute-start | bytes 110600 | tf_op jit(solution)/shard_map/ppermute | solution.py:250
  19.8 10.3 %collective-permute-start.13 = (f32[2,8,576]{2,1,0:T(8,128)S(1)}, f32[2,8,576]{2,1,0:T(8,128)S(1)}, u32[]{:S(2)}, u32[]{:S(2)}) collective-permute-start(f32[2,8,576]{2,1,0:T(8,128)S(1)} %get-tuple-element.27.out_o), channel_id=1, source_target_pairs={{0,16},{1,2},{2,1},{3,4},{4,3},{5,6},{6,5},{7,8},{8,7},{9,10},{10,... | collective-permute-start | bytes 110600 | tf_op jit(solution)/shard_map/ppermute | solution.py:263
  22.6 7.5 %collective-permute-start.11 = (f32[8,128]{1,0:T(8,128)S(1)}, f32[8,128]{1,0:T(8,128)S(1)}, u32[]{:S(2)}, u32[]{:S(2)}) collective-permute-start(f32[8,128]{1,0:T(8,128)S(1)} %add_add_fusion.refs_0_), channel_id=1, source_target_pairs={{0,12},{1,13},{2,14},{3,15},{4,8},{5,9},{6,10},{7,11},{8,4},{9,5},... | collective-permute-start | bytes 12296 | tf_op jit(solution)/shard_map/ppermute | solution.py:272
  25.3 4.8 %collective-permute-start.10 = (f32[8,128]{1,0:T(8,128)S(1)}, f32[8,128]{1,0:T(8,128)S(1)}, u32[]{:S(2)}, u32[]{:S(2)}) collective-permute-start(f32[8,128]{1,0:T(8,128)S(1)} %add_add_fusion.refs_0_), channel_id=1, source_target_pairs={{0,8},{1,9},{2,10},{3,11},{4,12},{5,13},{6,14},{7,15},{8,0},{9,1},... | collective-permute-start | bytes 12296 | tf_op jit(solution)/shard_map/ppermute | solution.py:272
  25.7 4.4 %collective-permute-start.9 = (f32[8,128]{1,0:T(8,128)S(1)}, f32[8,128]{1,0:T(8,128)S(1)}, u32[]{:S(2)}, u32[]{:S(2)}) collective-permute-start(f32[8,128]{1,0:T(8,128)S(1)} %add_add_fusion.refs_0_), channel_id=1, source_target_pairs={{0,4},{1,5},{2,6},{3,7},{4,0},{5,1},{6,2},{7,3},{8,12},{9,13},{10,... | collective-permute-start | bytes 12296 | tf_op jit(solution)/shard_map/ppermute | solution.py:272

commit v3 on v2

--- a/solution.py
+++ b/solution.py
@@ -7,7 +7,6 @@
 
 f32 = jnp.float32
 bf16 = jnp.bfloat16
-precise = lax.Precision.HIGHEST
 slot_shift = 1.2
 diag_middle = 1.25
 
@@ -33,10 +32,18 @@
     return pltpu.with_memory_space_constraint(x, pltpu.HBM)
 
 
+def thirds_of(x):
+    high = x.astype(bf16).astype(f32)
+    rest = x - high
+    middle = rest.astype(bf16).astype(f32)
+    return jnp.concatenate([high, middle, rest - middle], axis=0).astype(bf16)
+
+
 def gram(left, right):
-    return lax.dot_general(
-        left, right, (((1,), (1,)), ((), ())), precision=precise, preferred_element_type=f32
-    )
+    a, b = left.shape[0], right.shape[0]
+    parts = turned_dot(thirds_of(left), thirds_of(right))
+    rows = parts[:a] + (parts[a : 2 * a] + parts[2 * a :])
+    return rows[:, :b] + (rows[:, b : 2 * b] + rows[:, 2 * b :])
 
 
 def parts_of(x):
@@ -122,7 +129,8 @@
         out_o[b] = whole_of(acc[2 * blocks + b])
 
 
-def forward(kh, kl, cols, y, y_e, y_o, x, dg, mk, own, result, xcat):
+def forward(kh, kl, cols, y, y_e, y_o, x, dg, mk, *rest):
+    *reverse, result, xcat = rest
     blocks, slots = kh.shape[0], kh.shape[1]
     for b in range(blocks):
         xcat[b] = parts_of(y_e[b])
@@ -133,116 +141,134 @@
         for k in range(slots):
             field = xcat[slot_of(cols, r, k, blocks)]
             total += turned_dot(field, kh[r, k]) + turned_dot(field, kl[r, k])
-        result[r] = dg[r] * x[r] + mk[r] * (whole_of(total) + own[r])
+        summed = whole_of(total)
+        for part in reverse:
+            summed += part[r]
+        result[r] = dg[r] * x[r] + mk[r] * summed
 
 
 def reverse_second(kh, kl, cols, y1, r0, w, dg, mk, out_e, out_m, out_o, grams, acc):
     blocks, slots = kh.shape[0], kh.shape[1]
-    fields = y1.shape[1]
+    n = y1.shape[1]
     acc[...] = jnp.zeros_like(acc)
     for r in range(blocks):
         ycat = parts_of(y1[r])
         for k in range(slots):
             s = slot_of(cols, r, k, blocks)
             acc[s] += plain_dot(ycat, kh[r, k]) + plain_dot(ycat, kl[r, k])
-    h00 = h01 = h11 = h12 = jnp.zeros((fields, fields), f32)
+    total = jnp.zeros((3 * n, 4 * n), f32)
     for b in range(blocks):
         own = whole_of(acc[blocks + b])
         out_e[b] = whole_of(acc[b])
         out_m[b] = own
         out_o[b] = whole_of(acc[2 * blocks + b])
-        h00 += gram(r0[b], r0[b])
-        h01 += gram(r0[b], w[b])
-        h11 += gram(w[b], w[b])
-        h12 += gram(w[b], dg[b] * w[b]) + gram(own, y1[b]) + gram(y1[b], own)
-    rest = jnp.zeros((fields, grams.shape[1] - 4 * fields), f32)
-    grams[...] = jnp.concatenate([h00, h01, h11, h12, rest], axis=1)
+        free = mk[b] * own
+        total += gram(
+            jnp.concatenate([r0[b], w[b], free], axis=0),
+            jnp.concatenate([r0[b], w[b], dg[b] * w[b], free], axis=0),
+        )
+    h12 = total[n : 2 * n, 2 * n : 3 * n] + total[n : 2 * n, 3 * n :] + total[2 * n :, n : 2 * n]
+    rest = jnp.zeros((n, grams.shape[1] - 4 * n), f32)
+    grams[...] = jnp.concatenate(
+        [total[:n, : 2 * n], total[n : 2 * n, n : 2 * n], h12, rest], axis=1
+    )
 
 
 def halo_grams(out_e, out_o, y_e, y_o, grams, result):
-    fields = out_e.shape[1]
-    cross = jnp.zeros((fields, fields), f32)
+    n = out_e.shape[1]
+    total = jnp.zeros((2 * n, 2 * n), f32)
     for b in range(out_e.shape[0]):
-        cross += gram(out_e[b], y_e[b]) + gram(y_e[b], out_e[b])
-        cross += gram(out_o[b], y_o[b]) + gram(y_o[b], out_o[b])
-    before = jnp.zeros((fields, 3 * fields), f32)
-    after = jnp.zeros((fields, result.shape[1] - 4 * fields), f32)
+        for out, y in ((out_e, y_e), (out_o, y_o)):
+            total += gram(
+                jnp.concatenate([out[b], y[b]], axis=0), jnp.concatenate([y[b], out[b]], axis=0)
+            )
+    cross = total[:n, :n] + total[n:, n:]
+    before = jnp.zeros((n, 3 * n), f32)
+    after = jnp.zeros((n, result.shape[1] - 4 * n), f32)
     result[...] = grams[...] + jnp.concatenate([before, cross, after], axis=1)
 
 
-def eliminate(system, count):
-    rows = lax.broadcasted_iota(jnp.int32, system.shape, 0)
+def eliminate(systems):
+    count = systems[0][0].shape[0]
+    rows = lax.broadcasted_iota(jnp.int32, (count, 128), 0)
+    spread = [
+        [jnp.broadcast_to(matrix[:, k : k + 1], (count, 128)) for k in range(count)]
+        for matrix, _ in systems
+    ]
+    sides = [side for _, side in systems]
     for k in range(count):
-        pivot = system[k : k + 1, :] / system[k : k + 1, k : k + 1]
-        rest = system - system[:, k : k + 1] * pivot
-        system = jnp.where(rows == k, pivot, rest)
-    return system
-
-
-def small_dot(left, right):
-    total = left[:, 0:1] * right[0:1, :]
-    for k in range(1, left.shape[1]):
-        total += left[:, k : k + 1] * right[k : k + 1, :]
-    return total
+        for i, columns in enumerate(spread):
+            column = columns[k]
+            scale = 1.0 / column[k : k + 1]
+
+            def step(x):
+                width = x.shape[1]
+                pivot = x[k : k + 1] * scale[:, :width]
+                return jnp.where(rows[:, :width] == k, pivot, x - column[:, :width] * pivot)
+
+            spread[i] = [step(c) if j > k else c for j, c in enumerate(columns)]
+            sides[i] = step(sides[i])
+    return sides
+
+
+def columns_of(matrix):
+    return [matrix[:, k : k + 1] for k in range(matrix.shape[1])]
+
+
+def small_dot(columns, right):
+    terms = [column * right[k : k + 1, :] for k, column in enumerate(columns)]
+    while len(terms) > 1:
+        terms = [a + b for a, b in zip(terms[::2], terms[1::2])]
+    return terms[0]
 
 
 def finish(*refs, rounds, shift):
     gram_refs = refs[:rounds]
-    r0, w, up, mk, from_e, from_o, disp, resid = refs[rounds:]
-    blocks, fields = r0.shape[0], r0.shape[1]
+    r0, w, u, disp, resid = refs[rounds:]
+    blocks, n = r0.shape[0], r0.shape[1]
     comps = disp.shape[0]
     bn = disp.shape[2] // blocks
     sums = gram_refs[0][...]
     for ref in gram_refs[1:]:
         sums += ref[...]
-    h00, h01, h11, h12 = (sums[:, i * fields : (i + 1) * fields] for i in range(4))
+    h00, h01, h11, h12 = (sums[:, i * n : (i + 1) * n] for i in range(4))
     eye = (
-        lax.broadcasted_iota(jnp.int32, (fields, fields), 0)
-        == lax.broadcasted_iota(jnp.int32, (fields, fields), 1)
+        lax.broadcasted_iota(jnp.int32, (n, n), 0) == lax.broadcasted_iota(jnp.int32, (n, n), 1)
     ).astype(f32)
-    first = eliminate(jnp.concatenate([shift * h00 + h01, h00, h01], axis=1), fields)
-    step, keep = first[:, fields : 2 * fields], first[:, 2 * fields : 3 * fields]
-    inverse = eliminate(jnp.concatenate([h00, eye], axis=1), fields)[:, fields : 2 * fields]
-    step_t = step.T
-    keep_t = keep.T
-    h00k = small_dot(h00, keep)
-    h01k = small_dot(h01, keep)
-    h01s = small_dot(h01, step)
-    h11s = small_dot(h11, step)
-    h12s = small_dot(h12, step)
-    rho = small_dot(keep_t, h00k - h01s) + small_dot(step_t, h11s - h01k)
-    mixing = small_dot(inverse, rho)
-    lead = keep + mixing
-    lead_t = lead.T
-    h00p = small_dot(h00, lead)
-    h01p = small_dot(h01, lead)
-    h11p = small_dot(h11, lead)
-    curvature = small_dot(lead_t, shift * (h00p - h01s) + h01p - h11s) + small_dot(
-        step_t, shift * (h11s - h01p) + h12s - h11p
-    )
-    second = eliminate(jnp.concatenate([curvature, rho], axis=1), fields)
-    after = second[:, fields : 2 * fields]
-    lead_after = small_dot(lead, after)
-    step_after = small_dot(step, after)
-    zero = jnp.zeros_like(eye)
-    mix = jnp.concatenate(
-        [
-            jnp.concatenate([step + lead_after, keep - shift * lead_after], axis=1),
-            jnp.concatenate([-step_after, shift * step_after - step - lead_after], axis=1),
-            jnp.concatenate([zero, step_after], axis=1),
-        ],
-        axis=0,
-    )
-    for b in range(blocks):
-        u = up[b] + mk[b] * (from_e[b] + from_o[b])
-        basis = jnp.concatenate([r0[b], w[b], u], axis=0)
-        both = lax.dot_general(
-            mix, basis, (((0,), (0,)), ((), ())), precision=precise, preferred_element_type=f32
-        )
-        for c in range(comps):
-            piece = both[:, c * bn : (c + 1) * bn]
-            disp[c, :, b * bn : (b + 1) * bn] = piece[:fields]
-            resid[c, :, b * bn : (b + 1) * bn] = piece[fields:]
+    first, inverse0 = eliminate(
+        [(shift * h00 + h01, jnp.concatenate([h00, h01, eye], axis=1)), (h00, eye)]
+    )
+    step, keep, inverse = (first[:, i * n : (i + 1) * n] for i in range(3))
+    c00, c01, c11, c12 = (columns_of(h) for h in (h00, h01, h11, h12))
+    step_t, keep_t = small_dot(c00, inverse), small_dot(c01, inverse)
+    h11s = small_dot(c11, step)
+    past = h11s - small_dot(c01, keep)
+    image = small_dot(c12, step) + shift * past - small_dot(c11, keep)
+    both = small_dot(
+        columns_of(step_t), jnp.concatenate([past, image, h11 + shift * h01], axis=1)
+    )
+    rho = both[:, :n]
+    mixing = small_dot(columns_of(inverse0), rho)
+    curvature = both[:, n : 2 * n] - small_dot(columns_of(both[:, 2 * n :]), mixing)
+    rho_columns = columns_of(rho)
+    lead_t = keep_t + small_dot(rho_columns, inverse0)
+    after_t = small_dot(rho_columns, eliminate([(curvature, eye)])[0])
+    moved = small_dot(columns_of(after_t), jnp.concatenate([lead_t, step_t], axis=1))
+    lead_after, step_after = moved[:, :n], moved[:, n:]
+    for_disp = (step_t + lead_after, -step_after)
+    for_resid = (
+        keep_t - shift * lead_after, shift * step_after - step_t - lead_after, step_after
+    )
+    for mix, out in ((for_disp, disp), (for_resid, resid)):
+        mix_columns = [columns_of(m) for m in mix]
+        for b in range(blocks):
+            total = None
+            for columns, x in zip(mix_columns, (r0, w, u)):
+                for g in range(n):
+                    term = columns[g] * x[b, g : g + 1, :]
+                    total = term if total is None else total + term
+            for c in range(comps):
+                out[c, :, b * bn : (b + 1) * bn] = total[:, c * bn : (c + 1) * bn]
 
 
 def even_swap(x):
@@ -322,14 +348,14 @@
     )
     sums = swapped_sums(grams)
     d_e, d_o = even_swap(c_e), odd_swap(c_o)
-    up = call(
-        forward, field, [vmem, vmem, smem] + [vmem] * 7, [cat], flops, name="forward_second",
-    )(kh, kl, columns, y1, y1_e, y1_o, w, dg, mk, c_m)
+    u = call(
+        forward, field, [vmem, vmem, smem] + [vmem] * 9, [cat], flops, name="forward_second",
+    )(kh, kl, columns, y1, y1_e, y1_o, w, dg, mk, c_m, d_e, d_o)
     out = jax.ShapeDtypeStruct((comps, fields, nodes), f32)
     disp, resid = call(
         lambda *refs: finish(*refs, rounds=len(sums), shift=shift),
-        (out, out), [vmem] * (len(sums) + 6), name="finish",
-    )(*sums, r0, w, up, mk, d_e, d_o)
+        (out, out), [vmem] * (len(sums) + 3), name="finish",
+    )(*sums, r0, w, u)
     return disp.transpose(1, 0, 2), resid.transpose(1, 0, 2)
 
 

time: 33.3 us -> 32 us (0.961)
  Pallas kernels: 15.8 us -> 14.1 us
  waiting for transfers between devices: 1.57 us -> 2.3 us
    pallas_call x2 -> x1, Pallas kernels: 6.01 us -> 3 us  [shards(): call(forward, field, [vmem, vmem, smem] + [vmem] * 7, [cat], flops, name=...]
    pallas_call x0 -> x1, Pallas kernels: none -> 3.01 us  [shards(): call(forward, field, [vmem, vmem, smem] + [vmem] * 9, [cat], flops, name=...]
    pallas_call x1, Pallas kernels: 3.08 us -> 1.75 us  [shards(): call(lambda *refs: finish(*refs, rounds=len(sums), shift=shift), (out, ou...]
    pallas_call x1, Pallas kernels: 2.81 us -> 2.39 us  [shards(): call(reverse_second, (field, field, field, gram_shape), [vmem, vmem, smem...]
    ppermute x4, waiting for transfers between devices: 0.25 us -> 0.67 us  [odd_swap(): return lax.ppermute(x, ('groups', 'row'), route)]
where the time goes in v3:
time: 32 us; the launch traced here: 31.9 us
  starting transfers between devices  14.7 us (46%)
  Pallas kernels  14.1 us (44%)
  waiting for transfers between devices  2.3 us (7%)
  between operations  0.76 us (2%)
    ppermute x4, starting transfers between devices, odd_swap(): return lax.ppermute(x, ('groups', 'row'), route)  7.44 us
    ppermute x6, starting transfers between devices, swapped_sums(): lax.ppermute(x, 'row', [(i, i ^ mask) for i in range(count)])  6.35 us
    pallas_call x1, Pallas kernels, shards(): call(forward, field, [vmem, vmem, smem] + [vmem] * 9, [cat], flops, name=...  3.01 us
    pallas_call x1, Pallas kernels, shards(): call(forward, field, [vmem, vmem, smem] + [vmem] * 7, [cat], flops, name=...  3 us
    pallas_call x1, Pallas kernels, shards(): call(reverse_first, (half, half, field, field, field), [vmem, smem, vmem]...  2.42 us
    pallas_call x1, Pallas kernels, shards(): call(reverse_second, (field, field, field, gram_shape), [vmem, vmem, smem...  2.39 us
    pallas_call x1, Pallas kernels, shards(): call(lambda *refs: finish(*refs, rounds=len(sums), shift=shift), (out, ou...  1.75 us
    ppermute x6, waiting for transfers between devices, swapped_sums(): lax.ppermute(x, 'row', [(i, i ^ mask) for i in range(count)])  1.61 us
  transfers between devices with their start and end apart: 14, of which 2 were waited for; matrix products, arithmetic and copies ran while one was open for 0% of the time, Pallas kernels for 34%

profile of v3, /device:TPU:0, one launch (start us, length us, event | category | flops | bytes accessed | tf_op | source)
XLA Modules:
  0.0 31.9 jit_solution(4046381094428976415)
XLA Ops:
  0.6 0.0 slice-start.1
  0.7 0.0 slice-start.2
  0.7 1.0 %prepare.1 = (f32[2,8,576]{2,1,0:T(8,128)S(1)}, f32[2,8,576]{2,1,0:T(8,128)S(1)}, f32[2,1,576]{2,1,0:T(1,128)S(1)}, f32[2,1,576]{2,1,0:T(1,128)S(1)}) custom-call(f32[3,8,384]{2,1,0:T(8,128)} %bitcast.9, s32[384]{0:T(512)} %refs_1_.1, f32[3,384]{1,0:T(4,128)} %refs_2_.1), custom_call_target="tpu_custom_call" | custom-call | flops 10000000000 | bytes 1048576 | tf_op jit(solution)/shard_map/prepare/pallas_call | solution.py:318
  1.7 3.0 %collective-permute-start.1 = (f32[2,8,576]{2,1,0:T(8,128)S(1)}, f32[2,8,576]{2,1,0:T(8,128)S(1)}, u32[]{:S(2)}, u32[]{:S(2)}) collective-permute-start(f32[2,8,576]{2,1,0:T(8,128)S(1)} %get-tuple-element.17.y0.y), channel_id=1, source_target_pairs={{0,16},{1,2},{2,1},{3,4},{4,3},{5,6},{6,5},{7,8},{8,7},{9,10},{10,... | collective-permute-start | bytes 110600 | tf_op jit(solution)/shard_map/ppermute | solution.py:289
  4.7 0.1 collective-permute-start
  4.9 2.4 %reverse_first.1 = (bf16[2,3,576,576]{3,2,1,0:T(8,128)(2,1)S(1)}, bf16[2,3,576,576]{3,2,1,0:T(8,128)(2,1)S(1)}, f32[2,8,576]{2,1,0:T(8,128)S(1)}, f32[2,8,576]{2,1,0:T(8,128)S(1)}, f32[2,8,576]{2,1,0:T(8,128)S(1)}) custom-call(f32[2,3,576,576]{3,2,1,0:T(8,128)S(1)} %bitcast.7, s32[2,3]{1,0:T(2,128)S(1)} %copy-done, f32[2,8,576]{2,1,0:T(8,128)S(1)} %get-tuple-element.17.y0.y), custom_call_target="tpu_custom_call" | custom-call | flops 254803968 | bytes 1048576 | tf_op jit(solution)/shard_map/reverse_first/pallas_call | solution.py:331
  7.3 0.4 %collective-permute-start.2 = (f32[2,8,576]{2,1,0:T(8,128)S(1)}, f32[2,8,576]{2,1,0:T(8,128)S(1)}, u32[]{:S(2)}, u32[]{:S(2)}) collective-permute-start(f32[2,8,576]{2,1,0:T(8,128)S(1)} %get-tuple-element.24), channel_id=1, source_target_pairs={{0,1},{1,0},{2,3},{3,2},{4,5},{5,4},{6,7},{7,6},{8,9},{9,8},{10,11... | collective-permute-start | bytes 110600 | tf_op jit(solution)/shard_map/ppermute | solution.py:276
  7.7 1.9 %collective-permute-start.3 = (f32[2,8,576]{2,1,0:T(8,128)S(1)}, f32[2,8,576]{2,1,0:T(8,128)S(1)}, u32[]{:S(2)}, u32[]{:S(2)}) collective-permute-start(f32[2,8,576]{2,1,0:T(8,128)S(1)} %get-tuple-element.25), channel_id=1, source_target_pairs={{0,16},{1,2},{2,1},{3,4},{4,3},{5,6},{6,5},{7,8},{8,7},{9,10},{10,... | collective-permute-start | bytes 110600 | tf_op jit(solution)/shard_map/ppermute | solution.py:289
  9.7 3.0 %forward_first.1 = f32[2,8,576]{2,1,0:T(8,128)S(1)} custom-call(bf16[2,3,576,576]{3,2,1,0:T(8,128)(2,1)S(1)} %get-tuple-element.18.kh, bf16[2,3,576,576]{3,2,1,0:T(8,128)(2,1)S(1)} %get-tuple-element.19.kl, s32[2,3]{1,0:T(2,128)S(1)} %copy-done, f32[2,8,576]{2,1,0:T(8,128)S(1)} %get-tuple-element.17.y0.y, f32[2,8,576]{2,1,0:T(8,128)S(1)} %collective-permute-done.y_e, ...), custom_call_target="tpu_custom_call" | custom-call | flops 254803968 | bytes 1048576 | tf_op jit(solution)/shard_map/forward_first/pallas_call | solution.py:336
  12.7 0.0 collective-permute-done.2
  12.7 1.0 %collective-permute-start.5 = (f32[2,8,576]{2,1,0:T(8,128)S(1)}, f32[2,8,576]{2,1,0:T(8,128)S(1)}, u32[]{:S(2)}, u32[]{:S(2)}) collective-permute-start(f32[2,8,576]{2,1,0:T(8,128)S(1)} %get-tuple-element.32.y1.y), channel_id=1, source_target_pairs={{0,16},{1,2},{2,1},{3,4},{4,3},{5,6},{6,5},{7,8},{8,7},{9,10},{10,... | collective-permute-start | bytes 110600 | tf_op jit(solution)/shard_map/ppermute | solution.py:289
  13.8 2.4 %reverse_second.1 = (f32[2,8,576]{2,1,0:T(8,128)S(1)}, f32[2,8,576]{2,1,0:T(8,128)S(1)}, f32[2,8,576]{2,1,0:T(8,128)S(1)}, f32[8,128]{1,0:T(8,128)S(1)}) custom-call(bf16[2,3,576,576]{3,2,1,0:T(8,128)(2,1)S(1)} %get-tuple-element.18.kh, bf16[2,3,576,576]{3,2,1,0:T(8,128)(2,1)S(1)} %get-tuple-element.19.kl, s32[2,3]{1,0:T(2,128)S(1)} %copy-done, ...), custom_call_target="tpu_custom_call" | custom-call | flops 254803968 | bytes 1048576 | tf_op jit(solution)/shard_map/reverse_second/pallas_call | solution.py:342
  16.1 0.7 %collective-permute-done.5.y_o = f32[2,8,576]{2,1,0:T(8,128)S(1)} collective-permute-done((f32[2,8,576]{2,1,0:T(8,128)S(1)}, f32[2,8,576]{2,1,0:T(8,128)S(1)}, u32[]{:S(2)}, u32[]{:S(2)}) %collective-permute-start.5) | collective-permute-done | bytes 36896 | tf_op jit(solution)/shard_map/ppermute | solution.py:289
  16.8 0.5 %halo_grams.1 = f32[8,128]{1,0:T(8,128)S(1)} custom-call(f32[2,8,576]{2,1,0:T(8,128)S(1)} %get-tuple-element.26.out_e, f32[2,8,576]{2,1,0:T(8,128)S(1)} %get-tuple-element.27.out_o, f32[2,8,576]{2,1,0:T(8,128)S(1)} %collective-permute-done.4.y_e, f32[2,8,576]{2,1,0:T(8,128)S(1)} %collective-permute-done.5.y_o, f32[8,128]{1,0:T(8,128)S(1)} %get-tuple-element.28.grams), custom_call_target="tpu_custom_call" | custom-call | bytes 1048576 | tf_op jit(solution)/shard_map/halo_grams/pallas_call | solution.py:346
  17.3 1.7 %collective-permute-start.8 = (f32[8,128]{1,0:T(8,128)S(1)}, f32[8,128]{1,0:T(8,128)S(1)}, u32[]{:S(2)}, u32[]{:S(2)}) collective-permute-start(f32[8,128]{1,0:T(8,128)S(1)} %halo_grams.1), channel_id=1, source_target_pairs={{0,3},{1,2},{2,1},{3,0},{4,7},{5,6},{6,5},{7,4},{8,11},{9,10},{10,... | collective-permute-start | bytes 12296 | tf_op jit(solution)/shard_map/ppermute | solution.py:298
  19.0 0.2 collective-permute-start.6
  19.2 0.3 collective-permute-start.12
  19.5 1.5 %collective-permute-start.13 = (f32[2,8,576]{2,1,0:T(8,128)S(1)}, f32[2,8,576]{2,1,0:T(8,128)S(1)}, u32[]{:S(2)}, u32[]{:S(2)}) collective-permute-start(f32[2,8,576]{2,1,0:T(8,128)S(1)} %get-tuple-element.27.out_o), channel_id=1, source_target_pairs={{0,16},{1,2},{2,1},{3,4},{4,3},{5,6},{6,5},{7,8},{8,7},{9,10},{10,... | collective-permute-start | bytes 110600 | tf_op jit(solution)/shard_map/ppermute | solution.py:289
  21.0 1.6 %collective-permute-done.7 = f32[8,128]{1,0:T(8,128)S(1)} collective-permute-done((f32[8,128]{1,0:T(8,128)S(1)}, f32[8,128]{1,0:T(8,128)S(1)}, u32[]{:S(2)}, u32[]{:S(2)}) %collective-permute-start.7) | collective-permute-done | bytes 4128 | tf_op jit(solution)/shard_map/ppermute | solution.py:298
  22.6 2.3 %collective-permute-start.11 = (f32[8,128]{1,0:T(8,128)S(1)}, f32[8,128]{1,0:T(8,128)S(1)}, u32[]{:S(2)}, u32[]{:S(2)}) collective-permute-start(f32[8,128]{1,0:T(8,128)S(1)} %add_add_fusion.refs_0_), channel_id=1, source_target_pairs={{0,12},{1,13},{2,14},{3,15},{4,8},{5,9},{6,10},{7,11},{8,4},{9,5},... | collective-permute-start | bytes 12296 | tf_op jit(solution)/shard_map/ppermute | solution.py:298
  24.9 0.8 %collective-permute-start.10 = (f32[8,128]{1,0:T(8,128)S(1)}, f32[8,128]{1,0:T(8,128)S(1)}, u32[]{:S(2)}, u32[]{:S(2)}) collective-permute-start(f32[8,128]{1,0:T(8,128)S(1)} %add_add_fusion.refs_0_), channel_id=1, source_target_pairs={{0,8},{1,9},{2,10},{3,11},{4,12},{5,13},{6,14},{7,15},{8,0},{9,1},... | collective-permute-start | bytes 12296 | tf_op jit(solution)/shard_map/ppermute | solution.py:298
  25.7 1.4 %collective-permute-start.9 = (f32[8,128]{1,0:T(8,128)S(1)}, f32[8,128]{1,0:T(8,128)S(1)}, u32[]{:S(2)}, u32[]{:S(2)}) collective-permute-start(f32[8,128]{1,0:T(8,128)S(1)} %add_add_fusion.refs_0_), channel_id=1, source_target_pairs={{0,4},{1,5},{2,6},{3,7},{4,0},{5,1},{6,2},{7,3},{8,12},{9,13},{10,... | collective-permute-start | bytes 12296 | tf_op jit(solution)/shard_map/ppermute | solution.py:298
  27.1 3.0 %forward_second.1.refs_6_ = f32[2,8,576]{2,1,0:T(8,128)S(1)} custom-call(bf16[2,3,576,576]{3,2,1,0:T(8,128)(2,1)S(1)} %get-tuple-element.18.kh, bf16[2,3,576,576]{3,2,1,0:T(8,128)(2,1)S(1)} %get-tuple-element.19.kl, s32[2,3]{1,0:T(2,128)S(1)} %copy-done, f32[2,8,576]{2,1,0:T(8,128)S(1)} %get-tuple-element.32.y1.y, ...), custom_call_target="tpu_custom_call" | custom-call | flops 254803968 | bytes 1048576 | tf_op jit(solution)/shard_map/forward_second/pallas_call | solution.py:351
  30.1 1.8 %finish.1 = (f32[3,8,384]{2,1,0:T(8,128)}, f32[3,8,384]{2,1,0:T(8,128)}) custom-call(f32[8,128]{1,0:T(8,128)S(1)} %add_add_fusion.refs_0_, f32[8,128]{1,0:T(8,128)S(1)} %collective-permute-done.9.refs_1_, f32[8,128]{1,0:T(8,128)S(1)} %collective-permute-done.10.refs_2_, f32[8,128]{1,0:T(8,128)S(1)} %collective-permute-done.11.refs_3_, ...), custom_call_target="tpu_custom_call" | custom-call | bytes 1048576 | tf_op jit(solution)/shard_map/finish/pallas_call | solution.py:355
  (23 shorter events, 0.1 us)
Async XLA Ops:
  0.6 4.2 %slice-start = ((s8[8847360]{0:T(1024)(128)(4,1)}), s8[4194304]{0:T(1024)(128)(4,1)S(1)}, s32[]{:S(2)}) async-start(s8[8847360]{0:T(1024)(128)(4,1)} %bitcast.6), calls=%async_computation | async-start | bytes 8388608
  0.6 4.2 %slice-start.1 = ((s8[8847360]{0:T(1024)(128)(4,1)}), s8[4194304]{0:T(1024)(128)(4,1)S(1)}, s32[]{:S(2)}) async-start(s8[8847360]{0:T(1024)(128)(4,1)} %bitcast.6), calls=%async_computation.1 | async-start | bytes 8388608
  0.7 4.2 %slice-start.2 = ((s8[8847360]{0:T(1024)(128)(4,1)}), s8[458752]{0:T(1024)(128)(4,1)S(1)}, s32[]{:S(2)}) async-start(s8[8847360]{0:T(1024)(128)(4,1)} %bitcast.6), calls=%async_computation.2 | async-start | bytes 917504
  0.7 4.2 %copy-start = (s32[2,3]{1,0:T(2,128)S(1)}, s32[2,3]{1,0:T(2,128)}, u32[]{:S(2)}) copy-start(s32[2,3]{1,0:T(2,128)} %cols.7) | copy-start | bytes 76
  1.7 8.0 %collective-permute-start.1 = (f32[2,8,576]{2,1,0:T(8,128)S(1)}, f32[2,8,576]{2,1,0:T(8,128)S(1)}, u32[]{:S(2)}, u32[]{:S(2)}) collective-permute-start(f32[2,8,576]{2,1,0:T(8,128)S(1)} %get-tuple-element.17.y0.y), channel_id=1, source_target_pairs={{0,16},{1,2},{2,1},{3,4},{4,3},{5,6},{6,5},{7,8},{8,7},{9,10},{10,... | collective-permute-start | bytes 110600 | tf_op jit(solution)/shard_map/ppermute | solution.py:289
  4.7 5.0 %collective-permute-start = (f32[2,8,576]{2,1,0:T(8,128)S(1)}, f32[2,8,576]{2,1,0:T(8,128)S(1)}, u32[]{:S(2)}, u32[]{:S(2)}) collective-permute-start(f32[2,8,576]{2,1,0:T(8,128)S(1)} %get-tuple-element.17.y0.y), channel_id=1, source_target_pairs={{0,1},{1,0},{2,3},{3,2},{4,5},{5,4},{6,7},{7,6},{8,9},{9,8},{10,11... | collective-permute-start | bytes 110600 | tf_op jit(solution)/shard_map/ppermute | solution.py:276
  7.3 5.4 %collective-permute-start.2 = (f32[2,8,576]{2,1,0:T(8,128)S(1)}, f32[2,8,576]{2,1,0:T(8,128)S(1)}, u32[]{:S(2)}, u32[]{:S(2)}) collective-permute-start(f32[2,8,576]{2,1,0:T(8,128)S(1)} %get-tuple-element.24), channel_id=1, source_target_pairs={{0,1},{1,0},{2,3},{3,2},{4,5},{5,4},{6,7},{7,6},{8,9},{9,8},{10,11... | collective-permute-start | bytes 110600 | tf_op jit(solution)/shard_map/ppermute | solution.py:276
  7.7 5.0 %collective-permute-start.3 = (f32[2,8,576]{2,1,0:T(8,128)S(1)}, f32[2,8,576]{2,1,0:T(8,128)S(1)}, u32[]{:S(2)}, u32[]{:S(2)}) collective-permute-start(f32[2,8,576]{2,1,0:T(8,128)S(1)} %get-tuple-element.25), channel_id=1, source_target_pairs={{0,16},{1,2},{2,1},{3,4},{4,3},{5,6},{6,5},{7,8},{8,7},{9,10},{10,... | collective-permute-start | bytes 110600 | tf_op jit(solution)/shard_map/ppermute | solution.py:289
  12.7 4.1 %collective-permute-start.5 = (f32[2,8,576]{2,1,0:T(8,128)S(1)}, f32[2,8,576]{2,1,0:T(8,128)S(1)}, u32[]{:S(2)}, u32[]{:S(2)}) collective-permute-start(f32[2,8,576]{2,1,0:T(8,128)S(1)} %get-tuple-element.32.y1.y), channel_id=1, source_target_pairs={{0,16},{1,2},{2,1},{3,4},{4,3},{5,6},{6,5},{7,8},{8,7},{9,10},{10,... | collective-permute-start | bytes 110600 | tf_op jit(solution)/shard_map/ppermute | solution.py:289
  13.8 3.1 %collective-permute-start.4 = (f32[2,8,576]{2,1,0:T(8,128)S(1)}, f32[2,8,576]{2,1,0:T(8,128)S(1)}, u32[]{:S(2)}, u32[]{:S(2)}) collective-permute-start(f32[2,8,576]{2,1,0:T(8,128)S(1)} %get-tuple-element.32.y1.y), channel_id=1, source_target_pairs={{0,1},{1,0},{2,3},{3,2},{4,5},{5,4},{6,7},{7,6},{8,9},{9,8},{10,11... | collective-permute-start | bytes 110600 | tf_op jit(solution)/shard_map/ppermute | solution.py:276
  17.3 3.7 %collective-permute-start.8 = (f32[8,128]{1,0:T(8,128)S(1)}, f32[8,128]{1,0:T(8,128)S(1)}, u32[]{:S(2)}, u32[]{:S(2)}) collective-permute-start(f32[8,128]{1,0:T(8,128)S(1)} %halo_grams.1), channel_id=1, source_target_pairs={{0,3},{1,2},{2,1},{3,0},{4,7},{5,6},{6,5},{7,4},{8,11},{9,10},{10,... | collective-permute-start | bytes 12296 | tf_op jit(solution)/shard_map/ppermute | solution.py:298
  19.0 3.6 %collective-permute-start.7 = (f32[8,128]{1,0:T(8,128)S(1)}, f32[8,128]{1,0:T(8,128)S(1)}, u32[]{:S(2)}, u32[]{:S(2)}) collective-permute-start(f32[8,128]{1,0:T(8,128)S(1)} %halo_grams.1), channel_id=1, source_target_pairs={{0,2},{1,3},{2,0},{3,1},{4,6},{5,7},{6,4},{7,5},{8,10},{9,11},{10,... | collective-permute-start | bytes 12296 | tf_op jit(solution)/shard_map/ppermute | solution.py:298
  19.0 3.6 %collective-permute-start.6 = (f32[8,128]{1,0:T(8,128)S(1)}, f32[8,128]{1,0:T(8,128)S(1)}, u32[]{:S(2)}, u32[]{:S(2)}) collective-permute-start(f32[8,128]{1,0:T(8,128)S(1)} %halo_grams.1), channel_id=1, source_target_pairs={{0,1},{1,0},{2,3},{3,2},{4,5},{5,4},{6,7},{7,6},{8,9},{9,8},{10,11... | collective-permute-start | bytes 12296 | tf_op jit(solution)/shard_map/ppermute | solution.py:298
  19.2 7.9 %collective-permute-start.12 = (f32[2,8,576]{2,1,0:T(8,128)S(1)}, f32[2,8,576]{2,1,0:T(8,128)S(1)}, u32[]{:S(2)}, u32[]{:S(2)}) collective-permute-start(f32[2,8,576]{2,1,0:T(8,128)S(1)} %get-tuple-element.26.out_e), channel_id=1, source_target_pairs={{0,1},{1,0},{2,3},{3,2},{4,5},{5,4},{6,7},{7,6},{8,9},{9,8},{10,11... | collective-permute-start | bytes 110600 | tf_op jit(solution)/shard_map/ppermute | solution.py:276
  19.5 7.6 %collective-permute-start.13 = (f32[2,8,576]{2,1,0:T(8,128)S(1)}, f32[2,8,576]{2,1,0:T(8,128)S(1)}, u32[]{:S(2)}, u32[]{:S(2)}) collective-permute-start(f32[2,8,576]{2,1,0:T(8,128)S(1)} %get-tuple-element.27.out_o), channel_id=1, source_target_pairs={{0,16},{1,2},{2,1},{3,4},{4,3},{5,6},{6,5},{7,8},{8,7},{9,10},{10,... | collective-permute-start | bytes 110600 | tf_op jit(solution)/shard_map/ppermute | solution.py:289
  22.6 7.5 %collective-permute-start.11 = (f32[8,128]{1,0:T(8,128)S(1)}, f32[8,128]{1,0:T(8,128)S(1)}, u32[]{:S(2)}, u32[]{:S(2)}) collective-permute-start(f32[8,128]{1,0:T(8,128)S(1)} %add_add_fusion.refs_0_), channel_id=1, source_target_pairs={{0,12},{1,13},{2,14},{3,15},{4,8},{5,9},{6,10},{7,11},{8,4},{9,5},... | collective-permute-start | bytes 12296 | tf_op jit(solution)/shard_map/ppermute | solution.py:298
  24.9 5.2 %collective-permute-start.10 = (f32[8,128]{1,0:T(8,128)S(1)}, f32[8,128]{1,0:T(8,128)S(1)}, u32[]{:S(2)}, u32[]{:S(2)}) collective-permute-start(f32[8,128]{1,0:T(8,128)S(1)} %add_add_fusion.refs_0_), channel_id=1, source_target_pairs={{0,8},{1,9},{2,10},{3,11},{4,12},{5,13},{6,14},{7,15},{8,0},{9,1},... | collective-permute-start | bytes 12296 | tf_op jit(solution)/shard_map/ppermute | solution.py:298
  25.7 4.4 %collective-permute-start.9 = (f32[8,128]{1,0:T(8,128)S(1)}, f32[8,128]{1,0:T(8,128)S(1)}, u32[]{:S(2)}, u32[]{:S(2)}) collective-permute-start(f32[8,128]{1,0:T(8,128)S(1)} %add_add_fusion.refs_0_), channel_id=1, source_target_pairs={{0,4},{1,5},{2,6},{3,7},{4,0},{5,1},{6,2},{7,3},{8,12},{9,13},{10,... | collective-permute-start | bytes 12296 | tf_op jit(solution)/shard_map/ppermute | solution.py:298

commit v4 on v3

--- a/solution.py
+++ b/solution.py
@@ -1,3 +1,5 @@
+import functools
+
 import jax
 import jax.numpy as jnp
 from jax import lax
@@ -101,16 +103,7 @@
         dg[b] = own - shift
 
 
-def reverse_products(kh, kl, cols, ycat, acc):
-    blocks, slots = kh.shape[0], kh.shape[1]
-    acc[...] = jnp.zeros_like(acc)
-    for r in range(blocks):
-        for k in range(slots):
-            s = slot_of(cols, r, k, blocks)
-            acc[s] += plain_dot(ycat[r], kh[r, k]) + plain_dot(ycat[r], kl[r, k])
-
-
-def reverse_first(coupling, cols, y0, kh, kl, out_e, out_m, out_o, acc):
+def reverse_first(coupling, cols, y0, kh, kl, th, out_e, out_m, out_o, acc):
     blocks, slots = coupling.shape[0], coupling.shape[1]
     acc[...] = jnp.zeros_like(acc)
     for r in range(blocks):
@@ -121,6 +114,7 @@
             low = (matrix - high.astype(f32)).astype(bf16)
             kh[r, k] = high
             kl[r, k] = low
+            th[r, k] = high.T
             s = slot_of(cols, r, k, blocks)
             acc[s] += plain_dot(ycat, high) + plain_dot(ycat, low)
     for b in range(blocks):
@@ -129,9 +123,9 @@
         out_o[b] = whole_of(acc[2 * blocks + b])
 
 
-def forward(kh, kl, cols, y, y_e, y_o, x, dg, mk, *rest):
-    *reverse, result, xcat = rest
-    blocks, slots = kh.shape[0], kh.shape[1]
+def forward(th, low, cols, y, y_o, y_e, x, dg, mk, *rest, reverses):
+    reverse, (result, *kept, xcat) = rest[:reverses], rest[reverses:]
+    blocks, slots = th.shape[0], th.shape[1]
     for b in range(blocks):
         xcat[b] = parts_of(y_e[b])
         xcat[blocks + b] = parts_of(y[b])
@@ -140,7 +134,11 @@
         total = jnp.zeros(xcat.shape[1:], f32)
         for k in range(slots):
             field = xcat[slot_of(cols, r, k, blocks)]
-            total += turned_dot(field, kh[r, k]) + turned_dot(field, kl[r, k])
+            matrix = low[r, k]
+            if kept:
+                matrix = matrix.T
+                kept[0][r, k] = matrix
+            total += plain_dot(field, th[r, k]) + plain_dot(field, matrix)
         summed = whole_of(total)
         for part in reverse:
             summed += part[r]
@@ -174,7 +172,7 @@
     )
 
 
-def halo_grams(out_e, out_o, y_e, y_o, grams, result):
+def halo_grams(out_e, out_o, y_o, y_e, grams, result):
     n = out_e.shape[1]
     total = jnp.zeros((2 * n, 2 * n), f32)
     for b in range(out_e.shape[0]):
@@ -293,7 +291,8 @@
     count = lax.axis_size("row")
     base = 1
     while True:
-        masks = [base, 2 * base, 3 * base] if 2 * base < count else [base]
+        order = (1,3,2) if base == 1 else (1,3,2)
+        masks = [m * base for m in order] if 2 * base < count else [base]
         got = [
             lax.ppermute(x, "row", [(i, i ^ mask) for i in range(count)]) for mask in masks
         ]
@@ -328,15 +327,16 @@
         name="prepare",
     )(*(in_hbm(x) for x in (loads.transpose(1, 0, 2), interior, stiff_diag)))
     y0_e, y0_o = even_swap(y0), odd_swap(y0)
-    kh, kl, a_e, a_m, a_o = call(
-        reverse_first, (half, half, field, field, field), [vmem, smem, vmem],
+    kh, kl, th, a_e, a_m, a_o = call(
+        reverse_first, (half, half, half, field, field, field), [vmem, smem, vmem],
         [acc], flops, name="reverse_first",
     )(coupling, columns, y0)
     b_e, b_o = even_swap(a_e), odd_swap(a_o)
-    wp = call(
-        forward, field, [vmem, vmem, smem] + [vmem] * 7, [cat], flops, name="forward_first",
-    )(kh, kl, columns, y0, y0_e, y0_o, r0, dg, mk, a_m)
-    w = wp + mk * (b_e + b_o)
+    wp, tl = call(
+        functools.partial(forward, reverses=1), (field, half), [vmem, vmem, smem] + [vmem] * 7,
+        [cat], flops, name="forward_first",
+    )(th, kl, columns, y0, y0_o, y0_e, r0, dg, mk, a_m)
+    w = wp + mk * (b_o + b_e)
     y1 = w * mk
     y1_e, y1_o = even_swap(y1), odd_swap(y1)
     c_e, c_m, c_o, grams = call(
@@ -344,13 +344,14 @@
         [acc], flops, name="reverse_second",
     )(kh, kl, columns, y1, r0, w, dg, mk)
     grams = call(halo_grams, gram_shape, [vmem] * 5, name="halo_grams")(
-        c_e, c_o, y1_e, y1_o, grams
+        c_e, c_o, y1_o, y1_e, grams
     )
     sums = swapped_sums(grams)
     d_e, d_o = even_swap(c_e), odd_swap(c_o)
     u = call(
-        forward, field, [vmem, vmem, smem] + [vmem] * 9, [cat], flops, name="forward_second",
-    )(kh, kl, columns, y1, y1_e, y1_o, w, dg, mk, c_m, d_e, d_o)
+        functools.partial(forward, reverses=3), field, [vmem, vmem, smem] + [vmem] * 9,
+        [cat], flops, name="forward_second",
+    )(th, tl, columns, y1, y1_o, y1_e, w, dg, mk, c_m, d_o, d_e)
     out = jax.ShapeDtypeStruct((comps, fields, nodes), f32)
     disp, resid = call(
         lambda *refs: finish(*refs, rounds=len(sums), shift=shift),

time: 32 us -> 31.5 us (0.984)
  Pallas kernels: 14.1 us -> 12.4 us
  starting transfers between devices: 14.7 us -> 15.9 us
    pallas_call x3, Pallas kernels: 8.43 us -> 6.74 us  [the longest x1 2.7 us: shards(): call(reverse_first, (half, half, half, field, field, field), [vmem, smem,...]
    ppermute x4, starting transfers between devices: 7.44 us -> 8.56 us  [odd_swap(): return lax.ppermute(x, ('groups', 'row'), route)]
    ppermute x4, waiting for transfers between devices: 0.67 us -> 0.01 us  [odd_swap(): return lax.ppermute(x, ('groups', 'row'), route)]
    ppermute x6, waiting for transfers between devices: 1.61 us -> 2.13 us  [swapped_sums(): lax.ppermute(x, 'row', [(i, i ^ mask) for i in range(count)])]
  transfers between devices with their start and end apart: 14 -> 14, of which waited for: 2 -> 2; matrix products, arithmetic and copies ran while one was open for 0% -> 0% of each run, Pallas kernels for 34% -> 29%
where the time goes in v4:
time: 31.5 us; the launch traced here: 31.3 us
  starting transfers between devices  15.9 us (50%)
  Pallas kernels  12.4 us (39%)
  waiting for transfers between devices  2.15 us (7%)
  between operations  0.74 us (2%)
    ppermute x4, starting transfers between devices, odd_swap(): return lax.ppermute(x, ('groups', 'row'), route)  8.56 us
    ppermute x6, starting transfers between devices, swapped_sums(): lax.ppermute(x, 'row', [(i, i ^ mask) for i in range(count)])  6.59 us
    pallas_call x1, Pallas kernels, shards(): call(reverse_first, (half, half, half, field, field, field), [vmem, smem,...  2.7 us
    pallas_call x1, Pallas kernels, shards(): call(reverse_second, (field, field, field, gram_shape), [vmem, vmem, smem...  2.38 us
    pallas_call x1, Pallas kernels, shards(): call(functools.partial(forward, reverses=1), (field, half), [vmem, vmem,...  2.17 us
    ppermute x6, waiting for transfers between devices, swapped_sums(): lax.ppermute(x, 'row', [(i, i ^ mask) for i in range(count)])  2.13 us
    pallas_call x1, Pallas kernels, shards(): call(functools.partial(forward, reverses=3), field, [vmem, vmem, smem] +...  1.87 us
    pallas_call x1, Pallas kernels, shards(): call(lambda *refs: finish(*refs, rounds=len(sums), shift=shift), (out, ou...  1.75 us
  transfers between devices with their start and end apart: 14, of which 2 were waited for; matrix products, arithmetic and copies ran while one was open for 0% of the time, Pallas kernels for 29%

profile of v4, /device:TPU:0, one launch (start us, length us, event | category | flops | bytes accessed | tf_op | source)
XLA Modules:
  0.0 31.3 jit_solution(163110046770125012)
XLA Ops:
  0.6 0.0 slice-start
  0.7 0.0 slice-start.2
  0.7 1.0 %prepare.1 = (f32[2,8,576]{2,1,0:T(8,128)S(1)}, f32[2,8,576]{2,1,0:T(8,128)S(1)}, f32[2,1,576]{2,1,0:T(1,128)S(1)}, f32[2,1,576]{2,1,0:T(1,128)S(1)}) custom-call(f32[3,8,384]{2,1,0:T(8,128)} %bitcast.9, s32[384]{0:T(512)} %refs_1_.1, f32[3,384]{1,0:T(4,128)} %refs_2_.1), custom_call_target="tpu_custom_call" | custom-call | flops 10000000000 | bytes 1048576 | tf_op jit(solution)/shard_map/prepare/pallas_call | solution.py:317
  1.7 3.0 %collective-permute-start = (f32[2,8,576]{2,1,0:T(8,128)S(1)}, f32[2,8,576]{2,1,0:T(8,128)S(1)}, u32[]{:S(2)}, u32[]{:S(2)}) collective-permute-start(f32[2,8,576]{2,1,0:T(8,128)S(1)} %get-tuple-element.20.y0.y), channel_id=1, source_target_pairs={{0,16},{1,2},{2,1},{3,4},{4,3},{5,6},{6,5},{7,8},{8,7},{9,10},{10,... | collective-permute-start | bytes 110600 | tf_op jit(solution)/shard_map/ppermute | solution.py:287
  4.7 0.1 collective-permute-start.1
  4.9 2.7 %reverse_first.1 = (bf16[2,3,576,576]{3,2,1,0:T(8,128)(2,1)S(1)}, bf16[2,3,576,576]{3,2,1,0:T(8,128)(2,1)S(1)}, bf16[2,3,576,576]{3,2,1,0:T(8,128)(2,1)S(1)}, f3...) custom-call(f32[2,3,576,576]{3,2,1,0:T(8,128)S(1)} %bitcast.7, s32[2,3]{1,0:T(2,128)S(1)} %copy-done, ...), custom_call_target="tpu_custom_call" | custom-call | flops 254803968 | bytes 1048576 | tf_op jit(solution)/shard_map/reverse_first/pallas_call | solution.py:330
  7.6 2.3 %collective-permute-start.2 = (f32[2,8,576]{2,1,0:T(8,128)S(1)}, f32[2,8,576]{2,1,0:T(8,128)S(1)}, u32[]{:S(2)}, u32[]{:S(2)}) collective-permute-start(f32[2,8,576]{2,1,0:T(8,128)S(1)} %get-tuple-element.29), channel_id=1, source_target_pairs={{0,16},{1,2},{2,1},{3,4},{4,3},{5,6},{6,5},{7,8},{8,7},{9,10},{10,... | collective-permute-start | bytes 110600 | tf_op jit(solution)/shard_map/ppermute | solution.py:287
  9.9 0.1 collective-permute-start.3
  10.0 2.2 %forward_first.1 = (f32[2,8,576]{2,1,0:T(8,128)S(1)}, bf16[2,3,576,576]{3,2,1,0:T(8,128)(2,1)S(1)}) custom-call(bf16[2,3,576,576]{3,2,1,0:T(8,128)(2,1)S(1)} %get-tuple-element.23.th, bf16[2,3,576,576]{3,2,1,0:T(8,128)(2,1)S(1)} %get-tuple-element.22.low.kl, s32[2,3]{1,0:T(2,128)S(1)} %copy-done, f32[2,8,576]{2,1,0:T(8,128)S(1)} %get-tuple-element.20.y0.y, ...), custom_call_target="tpu_custom_call" | custom-call | flops 254803968 | bytes 1048576 | tf_op jit(solution)/shard_map/forward_first/pallas_call | solution.py:335
  12.2 1.7 %collective-permute-start.4 = (f32[2,8,576]{2,1,0:T(8,128)S(1)}, f32[2,8,576]{2,1,0:T(8,128)S(1)}, u32[]{:S(2)}, u32[]{:S(2)}) collective-permute-start(f32[2,8,576]{2,1,0:T(8,128)S(1)} %get-tuple-element.38.y1.y), channel_id=1, source_target_pairs={{0,16},{1,2},{2,1},{3,4},{4,3},{5,6},{6,5},{7,8},{8,7},{9,10},{10,... | collective-permute-start | bytes 110600 | tf_op jit(solution)/shard_map/ppermute | solution.py:287
  14.0 2.4 %reverse_second.1 = (f32[2,8,576]{2,1,0:T(8,128)S(1)}, f32[2,8,576]{2,1,0:T(8,128)S(1)}, f32[2,8,576]{2,1,0:T(8,128)S(1)}, f32[8,128]{1,0:T(8,128)S(1)}) custom-call(bf16[2,3,576,576]{3,2,1,0:T(8,128)(2,1)S(1)} %get-tuple-element.21.kh, bf16[2,3,576,576]{3,2,1,0:T(8,128)(2,1)S(1)} %get-tuple-element.22.low.kl, s32[2,3]{1,0:T(2,128)S(1)} %copy-done, ...), custom_call_target="tpu_custom_call" | custom-call | flops 254803968 | bytes 1048576 | tf_op jit(solution)/shard_map/reverse_second/pallas_call | solution.py:342
  16.4 0.5 %halo_grams.1 = f32[8,128]{1,0:T(8,128)S(1)} custom-call(f32[2,8,576]{2,1,0:T(8,128)S(1)} %get-tuple-element.31.out_e, f32[2,8,576]{2,1,0:T(8,128)S(1)} %get-tuple-element.32.out_o, f32[2,8,576]{2,1,0:T(8,128)S(1)} %collective-permute-done.4.y_o, f32[2,8,576]{2,1,0:T(8,128)S(1)} %collective-permute-done.5.y_e, f32[8,128]{1,0:T(8,128)S(1)} %get-tuple-element.33.grams), custom_call_target="tpu_custom_call" | custom-call | bytes 1048576 | tf_op jit(solution)/shard_map/halo_grams/pallas_call | solution.py:346
  16.9 0.5 %collective-permute-start.6 = (f32[8,128]{1,0:T(8,128)S(1)}, f32[8,128]{1,0:T(8,128)S(1)}, u32[]{:S(2)}, u32[]{:S(2)}) collective-permute-start(f32[8,128]{1,0:T(8,128)S(1)} %halo_grams.1), channel_id=1, source_target_pairs={{0,1},{1,0},{2,3},{3,2},{4,5},{5,4},{6,7},{7,6},{8,9},{9,8},{10,11... | collective-permute-start | bytes 12296 | tf_op jit(solution)/shard_map/ppermute | solution.py:297
  17.4 1.6 %collective-permute-start.7 = (f32[8,128]{1,0:T(8,128)S(1)}, f32[8,128]{1,0:T(8,128)S(1)}, u32[]{:S(2)}, u32[]{:S(2)}) collective-permute-start(f32[8,128]{1,0:T(8,128)S(1)} %halo_grams.1), channel_id=1, source_target_pairs={{0,3},{1,2},{2,1},{3,0},{4,7},{5,6},{6,5},{7,4},{8,11},{9,10},{10,... | collective-permute-start | bytes 12296 | tf_op jit(solution)/shard_map/ppermute | solution.py:297
  19.0 0.1 collective-permute-start.8
  19.1 1.6 %collective-permute-start.12 = (f32[2,8,576]{2,1,0:T(8,128)S(1)}, f32[2,8,576]{2,1,0:T(8,128)S(1)}, u32[]{:S(2)}, u32[]{:S(2)}) collective-permute-start(f32[2,8,576]{2,1,0:T(8,128)S(1)} %get-tuple-element.32.out_o), channel_id=1, source_target_pairs={{0,16},{1,2},{2,1},{3,4},{4,3},{5,6},{6,5},{7,8},{8,7},{9,10},{10,... | collective-permute-start | bytes 110600 | tf_op jit(solution)/shard_map/ppermute | solution.py:287
  20.6 0.5 %collective-permute-start.13 = (f32[2,8,576]{2,1,0:T(8,128)S(1)}, f32[2,8,576]{2,1,0:T(8,128)S(1)}, u32[]{:S(2)}, u32[]{:S(2)}) collective-permute-start(f32[2,8,576]{2,1,0:T(8,128)S(1)} %get-tuple-element.31.out_e), channel_id=1, source_target_pairs={{0,1},{1,0},{2,3},{3,2},{4,5},{5,4},{6,7},{7,6},{8,9},{9,8},{10,11... | collective-permute-start | bytes 110600 | tf_op jit(solution)/shard_map/ppermute | solution.py:274
  21.1 1.5 %collective-permute-done.8 = f32[8,128]{1,0:T(8,128)S(1)} collective-permute-done((f32[8,128]{1,0:T(8,128)S(1)}, f32[8,128]{1,0:T(8,128)S(1)}, u32[]{:S(2)}, u32[]{:S(2)}) %collective-permute-start.8) | collective-permute-done | bytes 4128 | tf_op jit(solution)/shard_map/ppermute | solution.py:297
  22.6 2.4 %collective-permute-start.10 = (f32[8,128]{1,0:T(8,128)S(1)}, f32[8,128]{1,0:T(8,128)S(1)}, u32[]{:S(2)}, u32[]{:S(2)}) collective-permute-start(f32[8,128]{1,0:T(8,128)S(1)} %add_add_fusion.refs_0_), channel_id=1, source_target_pairs={{0,12},{1,13},{2,14},{3,15},{4,8},{5,9},{6,10},{7,11},{8,4},{9,5},... | collective-permute-start | bytes 12296 | tf_op jit(solution)/shard_map/ppermute | solution.py:297
  25.0 0.6 %collective-permute-start.11 = (f32[8,128]{1,0:T(8,128)S(1)}, f32[8,128]{1,0:T(8,128)S(1)}, u32[]{:S(2)}, u32[]{:S(2)}) collective-permute-start(f32[8,128]{1,0:T(8,128)S(1)} %add_add_fusion.refs_0_), channel_id=1, source_target_pairs={{0,8},{1,9},{2,10},{3,11},{4,12},{5,13},{6,14},{7,15},{8,0},{9,1},... | collective-permute-start | bytes 12296 | tf_op jit(solution)/shard_map/ppermute | solution.py:297
  25.7 1.3 %collective-permute-start.9 = (f32[8,128]{1,0:T(8,128)S(1)}, f32[8,128]{1,0:T(8,128)S(1)}, u32[]{:S(2)}, u32[]{:S(2)}) collective-permute-start(f32[8,128]{1,0:T(8,128)S(1)} %add_add_fusion.refs_0_), channel_id=1, source_target_pairs={{0,4},{1,5},{2,6},{3,7},{4,0},{5,1},{6,2},{7,3},{8,12},{9,13},{10,... | collective-permute-start | bytes 12296 | tf_op jit(solution)/shard_map/ppermute | solution.py:297
  27.0 1.9 %forward_second.1.refs_6_ = f32[2,8,576]{2,1,0:T(8,128)S(1)} custom-call(bf16[2,3,576,576]{3,2,1,0:T(8,128)(2,1)S(1)} %get-tuple-element.23.th, bf16[2,3,576,576]{3,2,1,0:T(8,128)(2,1)S(1)} %get-tuple-element.34.low, s32[2,3]{1,0:T(2,128)S(1)} %copy-done, f32[2,8,576]{2,1,0:T(8,128)S(1)} %get-tuple-element.38.y1.y, ...), custom_call_target="tpu_custom_call" | custom-call | flops 254803968 | bytes 1048576 | tf_op jit(solution)/shard_map/forward_second/pallas_call | solution.py:351
  28.9 0.7 %collective-permute-done.11.refs_3_ = f32[8,128]{1,0:T(8,128)S(1)} collective-permute-done((f32[8,128]{1,0:T(8,128)S(1)}, f32[8,128]{1,0:T(8,128)S(1)}, u32[]{:S(2)}, u32[]{:S(2)}) %collective-permute-start.11) | collective-permute-done | bytes 4128 | tf_op jit(solution)/shard_map/ppermute | solution.py:297
  29.6 1.8 %finish.1 = (f32[3,8,384]{2,1,0:T(8,128)}, f32[3,8,384]{2,1,0:T(8,128)}) custom-call(f32[8,128]{1,0:T(8,128)S(1)} %add_add_fusion.refs_0_, f32[8,128]{1,0:T(8,128)S(1)} %collective-permute-done.9.refs_1_, f32[8,128]{1,0:T(8,128)S(1)} %collective-permute-done.10.refs_2_, f32[8,128]{1,0:T(8,128)S(1)} %collective-permute-done.11.refs_3_, ...), custom_call_target="tpu_custom_call" | custom-call | bytes 1048576 | tf_op jit(solution)/shard_map/finish/pallas_call | solution.py:356
  (23 shorter events, 0.1 us)
Async XLA Ops:
  0.6 4.2 %slice-start = ((s8[8847360]{0:T(1024)(128)(4,1)}), s8[4194304]{0:T(1024)(128)(4,1)S(1)}, s32[]{:S(2)}) async-start(s8[8847360]{0:T(1024)(128)(4,1)} %bitcast.6), calls=%async_computation | async-start | bytes 8388608
  0.6 4.2 %slice-start.1 = ((s8[8847360]{0:T(1024)(128)(4,1)}), s8[4194304]{0:T(1024)(128)(4,1)S(1)}, s32[]{:S(2)}) async-start(s8[8847360]{0:T(1024)(128)(4,1)} %bitcast.6), calls=%async_computation.1 | async-start | bytes 8388608
  0.7 4.2 %slice-start.2 = ((s8[8847360]{0:T(1024)(128)(4,1)}), s8[458752]{0:T(1024)(128)(4,1)S(1)}, s32[]{:S(2)}) async-start(s8[8847360]{0:T(1024)(128)(4,1)} %bitcast.6), calls=%async_computation.2 | async-start | bytes 917504
  0.7 4.2 %copy-start = (s32[2,3]{1,0:T(2,128)S(1)}, s32[2,3]{1,0:T(2,128)}, u32[]{:S(2)}) copy-start(s32[2,3]{1,0:T(2,128)} %cols.7) | copy-start | bytes 76
  1.7 8.3 %collective-permute-start = (f32[2,8,576]{2,1,0:T(8,128)S(1)}, f32[2,8,576]{2,1,0:T(8,128)S(1)}, u32[]{:S(2)}, u32[]{:S(2)}) collective-permute-start(f32[2,8,576]{2,1,0:T(8,128)S(1)} %get-tuple-element.20.y0.y), channel_id=1, source_target_pairs={{0,16},{1,2},{2,1},{3,4},{4,3},{5,6},{6,5},{7,8},{8,7},{9,10},{10,... | collective-permute-start | bytes 110600 | tf_op jit(solution)/shard_map/ppermute | solution.py:287
  4.7 5.3 %collective-permute-start.1 = (f32[2,8,576]{2,1,0:T(8,128)S(1)}, f32[2,8,576]{2,1,0:T(8,128)S(1)}, u32[]{:S(2)}, u32[]{:S(2)}) collective-permute-start(f32[2,8,576]{2,1,0:T(8,128)S(1)} %get-tuple-element.20.y0.y), channel_id=1, source_target_pairs={{0,1},{1,0},{2,3},{3,2},{4,5},{5,4},{6,7},{7,6},{8,9},{9,8},{10,11... | collective-permute-start | bytes 110600 | tf_op jit(solution)/shard_map/ppermute | solution.py:274
  7.6 4.6 %collective-permute-start.2 = (f32[2,8,576]{2,1,0:T(8,128)S(1)}, f32[2,8,576]{2,1,0:T(8,128)S(1)}, u32[]{:S(2)}, u32[]{:S(2)}) collective-permute-start(f32[2,8,576]{2,1,0:T(8,128)S(1)} %get-tuple-element.29), channel_id=1, source_target_pairs={{0,16},{1,2},{2,1},{3,4},{4,3},{5,6},{6,5},{7,8},{8,7},{9,10},{10,... | collective-permute-start | bytes 110600 | tf_op jit(solution)/shard_map/ppermute | solution.py:287
  9.9 2.3 %collective-permute-start.3 = (f32[2,8,576]{2,1,0:T(8,128)S(1)}, f32[2,8,576]{2,1,0:T(8,128)S(1)}, u32[]{:S(2)}, u32[]{:S(2)}) collective-permute-start(f32[2,8,576]{2,1,0:T(8,128)S(1)} %get-tuple-element.30), channel_id=1, source_target_pairs={{0,1},{1,0},{2,3},{3,2},{4,5},{5,4},{6,7},{7,6},{8,9},{9,8},{10,11... | collective-permute-start | bytes 110600 | tf_op jit(solution)/shard_map/ppermute | solution.py:274
  12.2 4.1 %collective-permute-start.4 = (f32[2,8,576]{2,1,0:T(8,128)S(1)}, f32[2,8,576]{2,1,0:T(8,128)S(1)}, u32[]{:S(2)}, u32[]{:S(2)}) collective-permute-start(f32[2,8,576]{2,1,0:T(8,128)S(1)} %get-tuple-element.38.y1.y), channel_id=1, source_target_pairs={{0,16},{1,2},{2,1},{3,4},{4,3},{5,6},{6,5},{7,8},{8,7},{9,10},{10,... | collective-permute-start | bytes 110600 | tf_op jit(solution)/shard_map/ppermute | solution.py:287
  14.0 2.4 %collective-permute-start.5 = (f32[2,8,576]{2,1,0:T(8,128)S(1)}, f32[2,8,576]{2,1,0:T(8,128)S(1)}, u32[]{:S(2)}, u32[]{:S(2)}) collective-permute-start(f32[2,8,576]{2,1,0:T(8,128)S(1)} %get-tuple-element.38.y1.y), channel_id=1, source_target_pairs={{0,1},{1,0},{2,3},{3,2},{4,5},{5,4},{6,7},{7,6},{8,9},{9,8},{10,11... | collective-permute-start | bytes 110600 | tf_op jit(solution)/shard_map/ppermute | solution.py:274
  16.9 4.3 %collective-permute-start.6 = (f32[8,128]{1,0:T(8,128)S(1)}, f32[8,128]{1,0:T(8,128)S(1)}, u32[]{:S(2)}, u32[]{:S(2)}) collective-permute-start(f32[8,128]{1,0:T(8,128)S(1)} %halo_grams.1), channel_id=1, source_target_pairs={{0,1},{1,0},{2,3},{3,2},{4,5},{5,4},{6,7},{7,6},{8,9},{9,8},{10,11... | collective-permute-start | bytes 12296 | tf_op jit(solution)/shard_map/ppermute | solution.py:297
  17.4 3.7 %collective-permute-start.7 = (f32[8,128]{1,0:T(8,128)S(1)}, f32[8,128]{1,0:T(8,128)S(1)}, u32[]{:S(2)}, u32[]{:S(2)}) collective-permute-start(f32[8,128]{1,0:T(8,128)S(1)} %halo_grams.1), channel_id=1, source_target_pairs={{0,3},{1,2},{2,1},{3,0},{4,7},{5,6},{6,5},{7,4},{8,11},{9,10},{10,... | collective-permute-start | bytes 12296 | tf_op jit(solution)/shard_map/ppermute | solution.py:297
  19.0 3.6 %collective-permute-start.8 = (f32[8,128]{1,0:T(8,128)S(1)}, f32[8,128]{1,0:T(8,128)S(1)}, u32[]{:S(2)}, u32[]{:S(2)}) collective-permute-start(f32[8,128]{1,0:T(8,128)S(1)} %halo_grams.1), channel_id=1, source_target_pairs={{0,2},{1,3},{2,0},{3,1},{4,6},{5,7},{6,4},{7,5},{8,10},{9,11},{10,... | collective-permute-start | bytes 12296 | tf_op jit(solution)/shard_map/ppermute | solution.py:297
  19.1 7.9 %collective-permute-start.12 = (f32[2,8,576]{2,1,0:T(8,128)S(1)}, f32[2,8,576]{2,1,0:T(8,128)S(1)}, u32[]{:S(2)}, u32[]{:S(2)}) collective-permute-start(f32[2,8,576]{2,1,0:T(8,128)S(1)} %get-tuple-element.32.out_o), channel_id=1, source_target_pairs={{0,16},{1,2},{2,1},{3,4},{4,3},{5,6},{6,5},{7,8},{8,7},{9,10},{10,... | collective-permute-start | bytes 110600 | tf_op jit(solution)/shard_map/ppermute | solution.py:287
  20.6 6.4 %collective-permute-start.13 = (f32[2,8,576]{2,1,0:T(8,128)S(1)}, f32[2,8,576]{2,1,0:T(8,128)S(1)}, u32[]{:S(2)}, u32[]{:S(2)}) collective-permute-start(f32[2,8,576]{2,1,0:T(8,128)S(1)} %get-tuple-element.31.out_e), channel_id=1, source_target_pairs={{0,1},{1,0},{2,3},{3,2},{4,5},{5,4},{6,7},{7,6},{8,9},{9,8},{10,11... | collective-permute-start | bytes 110600 | tf_op jit(solution)/shard_map/ppermute | solution.py:274
  22.6 6.3 %collective-permute-start.10 = (f32[8,128]{1,0:T(8,128)S(1)}, f32[8,128]{1,0:T(8,128)S(1)}, u32[]{:S(2)}, u32[]{:S(2)}) collective-permute-start(f32[8,128]{1,0:T(8,128)S(1)} %add_add_fusion.refs_0_), channel_id=1, source_target_pairs={{0,12},{1,13},{2,14},{3,15},{4,8},{5,9},{6,10},{7,11},{8,4},{9,5},... | collective-permute-start | bytes 12296 | tf_op jit(solution)/shard_map/ppermute | solution.py:297
  25.0 4.5 %collective-permute-start.11 = (f32[8,128]{1,0:T(8,128)S(1)}, f32[8,128]{1,0:T(8,128)S(1)}, u32[]{:S(2)}, u32[]{:S(2)}) collective-permute-start(f32[8,128]{1,0:T(8,128)S(1)} %add_add_fusion.refs_0_), channel_id=1, source_target_pairs={{0,8},{1,9},{2,10},{3,11},{4,12},{5,13},{6,14},{7,15},{8,0},{9,1},... | collective-permute-start | bytes 12296 | tf_op jit(solution)/shard_map/ppermute | solution.py:297
  25.7 3.9 %collective-permute-start.9 = (f32[8,128]{1,0:T(8,128)S(1)}, f32[8,128]{1,0:T(8,128)S(1)}, u32[]{:S(2)}, u32[]{:S(2)}) collective-permute-start(f32[8,128]{1,0:T(8,128)S(1)} %add_add_fusion.refs_0_), channel_id=1, source_target_pairs={{0,4},{1,5},{2,6},{3,7},{4,0},{5,1},{6,2},{7,3},{8,12},{9,13},{10,... | collective-permute-start | bytes 12296 | tf_op jit(solution)/shard_map/ppermute | solution.py:297

commit v5 on v4

--- a/solution.py
+++ b/solution.py
@@ -76,7 +76,7 @@
 
 
 def prepare(
-    loads_in, interior_in, stiff_in, r0, y0, dg, mk, loads, interior, stiff, sems, *, blocks, shift
+    loads_in, interior_in, stiff_in, r0, y0, wide, dg, mk, loads, interior, stiff, sems, *, blocks, shift
 ):
     comps = loads.shape[0]
     bn = loads.shape[2] // blocks
@@ -99,88 +99,88 @@
         own = jnp.concatenate([stiff[c : c + 1, nodes] for c in range(comps)], axis=1)
         r0[b] = field
         y0[b] = field * inside
+        wide[b, :, : y0.shape[2]] = field * inside
+        wide[b, :, y0.shape[2] :] = jnp.zeros((wide.shape[1], wide.shape[2] - y0.shape[2]), f32)
         mk[b] = inside
         dg[b] = own - shift
 
 
-def reverse_first(coupling, cols, y0, kh, kl, th, out_e, out_m, out_o, acc):
+def split(matrix):
+    high = matrix.astype(bf16)
+    return high, (matrix - high.astype(f32)).astype(bf16)
+
+
+def reverse_products(coupling, cols, y, acc, th=None):
     blocks, slots = coupling.shape[0], coupling.shape[1]
     acc[...] = jnp.zeros_like(acc)
     for r in range(blocks):
-        ycat = parts_of(y0[r])
+        ycat = parts_of(y[r])
         for k in range(slots):
-            matrix = coupling[r, k]
-            high = matrix.astype(bf16)
-            low = (matrix - high.astype(f32)).astype(bf16)
-            kh[r, k] = high
-            kl[r, k] = low
-            th[r, k] = high.T
+            high, low = split(coupling[r, k])
+            if th is not None:
+                th[r, k] = high.T
             s = slot_of(cols, r, k, blocks)
-            acc[s] += plain_dot(ycat, high) + plain_dot(ycat, low)
-    for b in range(blocks):
-        out_e[b] = whole_of(acc[b])
-        out_m[b] = whole_of(acc[blocks + b])
-        out_o[b] = whole_of(acc[2 * blocks + b])
-
-
-def forward(th, low, cols, y, y_o, y_e, x, dg, mk, *rest, reverses):
+            acc[s] += whole_of(plain_dot(ycat, high) + plain_dot(ycat, low))
+
+
+def reverse_first(coupling, cols, y0, th, out_e, out_m, out_o, acc):
+    blocks = y0.shape[0]
+    reverse_products(coupling, cols, y0, acc, th)
+    for b in range(blocks):
+        out_e[b] = acc[b]
+        out_m[b] = acc[blocks + b]
+        out_o[b] = acc[2 * blocks + b]
+
+
+def forward(th, source, cols, y, y_o, y_e, x, dg, mk, *rest, reverses):
     reverse, (result, *kept, xcat) = rest[:reverses], rest[reverses:]
     blocks, slots = th.shape[0], th.shape[1]
     for b in range(blocks):
         xcat[b] = parts_of(y_e[b])
         xcat[blocks + b] = parts_of(y[b])
-        xcat[2 * blocks + b] = parts_of(y_o[b])
+        xcat[2 * blocks + b] = parts_of(y_o[b, :, : y.shape[2]])
     for r in range(blocks):
         total = jnp.zeros(xcat.shape[1:], f32)
         for k in range(slots):
             field = xcat[slot_of(cols, r, k, blocks)]
-            matrix = low[r, k]
+            low = source[r, k]
             if kept:
-                matrix = matrix.T
-                kept[0][r, k] = matrix
-            total += plain_dot(field, th[r, k]) + plain_dot(field, matrix)
+                low = split(low)[1].T
+                kept[0][r, k] = low
+            total += plain_dot(field, th[r, k]) + plain_dot(field, low)
         summed = whole_of(total)
         for part in reverse:
-            summed += part[r]
+            summed += part[r, :, : y.shape[2]]
         result[r] = dg[r] * x[r] + mk[r] * summed
 
 
-def reverse_second(kh, kl, cols, y1, r0, w, dg, mk, out_e, out_m, out_o, grams, acc):
-    blocks, slots = kh.shape[0], kh.shape[1]
-    n = y1.shape[1]
-    acc[...] = jnp.zeros_like(acc)
-    for r in range(blocks):
-        ycat = parts_of(y1[r])
-        for k in range(slots):
-            s = slot_of(cols, r, k, blocks)
-            acc[s] += plain_dot(ycat, kh[r, k]) + plain_dot(ycat, kl[r, k])
-    total = jnp.zeros((3 * n, 4 * n), f32)
-    for b in range(blocks):
-        own = whole_of(acc[blocks + b])
-        out_e[b] = whole_of(acc[b])
-        out_m[b] = own
-        out_o[b] = whole_of(acc[2 * blocks + b])
-        free = mk[b] * own
+def reverse_second(coupling, cols, y1, r0, w, dg, out_e, out_m, out_o, grams, acc):
+    blocks, n = y1.shape[0], y1.shape[1]
+    total = jnp.zeros((2 * n, 3 * n), f32)
+    for b in range(blocks):
         total += gram(
-            jnp.concatenate([r0[b], w[b], free], axis=0),
-            jnp.concatenate([r0[b], w[b], dg[b] * w[b], free], axis=0),
+            jnp.concatenate([r0[b], w[b]], axis=0),
+            jnp.concatenate([r0[b], w[b], dg[b] * w[b]], axis=0),
         )
-    h12 = total[n : 2 * n, 2 * n : 3 * n] + total[n : 2 * n, 3 * n :] + total[2 * n :, n : 2 * n]
     rest = jnp.zeros((n, grams.shape[1] - 4 * n), f32)
-    grams[...] = jnp.concatenate(
-        [total[:n, : 2 * n], total[n : 2 * n, n : 2 * n], h12, rest], axis=1
-    )
-
-
-def halo_grams(out_e, out_o, y_o, y_e, grams, result):
-    n = out_e.shape[1]
-    total = jnp.zeros((2 * n, 2 * n), f32)
-    for b in range(out_e.shape[0]):
-        for out, y in ((out_e, y_e), (out_o, y_o)):
-            total += gram(
-                jnp.concatenate([out[b], y[b]], axis=0), jnp.concatenate([y[b], out[b]], axis=0)
-            )
-    cross = total[:n, :n] + total[n:, n:]
+    grams[...] = jnp.concatenate([total[:n, : 2 * n], total[n:, n:], rest], axis=1)
+    reverse_products(coupling, cols, y1, acc)
+    for b in range(blocks):
+        out_e[b] = acc[b]
+        out_m[b] = acc[blocks + b]
+        out_o[b] = acc[2 * blocks + b]
+
+
+def cross_grams(out_e, out_m, out_o, y_e, y, y_o, grams, result):
+    n, width = y.shape[1], y.shape[2]
+    one = other = jnp.zeros((2 * n, 2 * n), f32)
+    for b in range(y.shape[0]):
+        for out, field in ((out_m, y), (out_e, y_e), (out_o, y_o)):
+            sent, seen = parts_of(out[b]), parts_of(field[b, :, :width])
+            one += turned_dot(sent, seen)
+            other += turned_dot(seen, sent)
+    both = whole_of(one + other)
+    cross = both[:, :n] + both[:, n:]
     before = jnp.zeros((n, 3 * n), f32)
     after = jnp.zeros((n, result.shape[1] - 4 * n), f32)
     result[...] = grams[...] + jnp.concatenate([before, cross, after], axis=1)
@@ -228,7 +228,7 @@
     bn = disp.shape[2] // blocks
     sums = gram_refs[0][...]
     for ref in gram_refs[1:]:
-        sums += ref[...]
+        sums += ref[:, : sums.shape[1]]
     h00, h01, h11, h12 = (sums[:, i * n : (i + 1) * n] for i in range(4))
     eye = (
         lax.broadcasted_iota(jnp.int32, (n, n), 0) == lax.broadcasted_iota(jnp.int32, (n, n), 1)
@@ -269,6 +269,10 @@
                 out[c, :, b * bn : (b + 1) * bn] = total[:, c * bn : (c + 1) * bn]
 
 
+def widened(x):
+    return jnp.pad(x, ((0, 0), (0, 0), (0, 64)))
+
+
 def even_swap(x):
     count = lax.axis_size("row")
     return lax.ppermute(x, "row", [(i, i ^ 1) for i in range(count)])
@@ -289,17 +293,19 @@
 
 def swapped_sums(x):
     count = lax.axis_size("row")
+    width = x.shape[1]
     base = 1
     while True:
-        order = (1,3,2) if base == 1 else (1,3,2)
-        masks = [m * base for m in order] if 2 * base < count else [base]
-        got = [
-            lax.ppermute(x, "row", [(i, i ^ mask) for i in range(count)]) for mask in masks
-        ]
+        masks = [base, 2 * base, 3 * base] if 2 * base < count else [base]
+        got = []
+        for i, mask in enumerate(masks):
+            sent = jnp.pad(x, ((0, 0), (0, (len(masks) - 1 - i) * width))) if base > 1 else x
+            route = [(j, j ^ mask) for j in range(count)]
+            got.append(lax.ppermute(sent, "row", route))
         base *= len(masks) + 1
         if base >= count:
             return [x, *got]
-        x = x + sum(got)
+        x = x + sum(g[:, :width] for g in got)
 
 
 def shards(coupling, columns, stiff_diag, interior, loads):
@@ -308,15 +314,16 @@
     shift = slot_shift * slots + diag_middle
     flops = 8 * 2 * fields * blocks * slots * width * width
     field = jax.ShapeDtypeStruct((blocks, fields, width), f32)
+    wide = jax.ShapeDtypeStruct((blocks, fields, width + 64), f32)
     row = jax.ShapeDtypeStruct((blocks, 1, width), f32)
     half = jax.ShapeDtypeStruct(coupling.shape, bf16)
     gram_shape = jax.ShapeDtypeStruct((fields, 128), f32)
-    acc = pltpu.VMEM((3 * blocks, 2 * fields, width), f32)
+    acc = pltpu.VMEM((3 * blocks, fields, width), f32)
     cat = pltpu.VMEM((3 * blocks, 2 * fields, width), bf16)
 
-    r0, y0, dg, mk = call(
+    r0, y0, wide0, dg, mk = call(
         lambda *refs: prepare(*refs, blocks=blocks, shift=diag_middle),
-        (field, field, row, row), [pl.BlockSpec(memory_space=pl.ANY)] * 3,
+        (field, field, wide, row, row), [pl.BlockSpec(memory_space=pl.ANY)] * 3,
         [
             pltpu.VMEM((comps, fields, nodes), f32),
             pltpu.VMEM((nodes,), jnp.int32),
@@ -326,25 +333,25 @@
         flops=10**10,
         name="prepare",
     )(*(in_hbm(x) for x in (loads.transpose(1, 0, 2), interior, stiff_diag)))
-    y0_e, y0_o = even_swap(y0), odd_swap(y0)
-    kh, kl, th, a_e, a_m, a_o = call(
-        reverse_first, (half, half, half, field, field, field), [vmem, smem, vmem],
+    y0_e, y0_o = even_swap(y0), odd_swap(wide0)
+    th, a_e, a_m, a_o = call(
+        reverse_first, (half, field, field, field), [vmem, smem, vmem],
         [acc], flops, name="reverse_first",
     )(coupling, columns, y0)
     b_e, b_o = even_swap(a_e), odd_swap(a_o)
     wp, tl = call(
         functools.partial(forward, reverses=1), (field, half), [vmem, vmem, smem] + [vmem] * 7,
         [cat], flops, name="forward_first",
-    )(th, kl, columns, y0, y0_o, y0_e, r0, dg, mk, a_m)
+    )(th, coupling, columns, y0, y0_o, y0_e, r0, dg, mk, a_m)
     w = wp + mk * (b_o + b_e)
     y1 = w * mk
-    y1_e, y1_o = even_swap(y1), odd_swap(y1)
+    y1_e, y1_o = even_swap(y1), odd_swap(widened(y1))
     c_e, c_m, c_o, grams = call(
-        reverse_second, (field, field, field, gram_shape), [vmem, vmem, smem] + [vmem] * 5,
+        reverse_second, (field, field, field, gram_shape), [vmem, smem] + [vmem] * 4,
         [acc], flops, name="reverse_second",
-    )(kh, kl, columns, y1, r0, w, dg, mk)
-    grams = call(halo_grams, gram_shape, [vmem] * 5, name="halo_grams")(
-        c_e, c_o, y1_o, y1_e, grams
+    )(coupling, columns, y1, r0, w, dg)
+    grams = call(cross_grams, gram_shape, [vmem] * 7, name="cross_grams")(
+        c_e, c_m, c_o, y1_e, y1, y1_o, grams
     )
     sums = swapped_sums(grams)
     d_e, d_o = even_swap(c_e), odd_swap(c_o)

time: 31.5 us -> 31 us (0.984)
  Pallas kernels: 12.4 us -> 11.7 us
  waiting for transfers between devices: 2.15 us -> 2.51 us
    pallas_call x3, Pallas kernels: 5.6 us -> 4.92 us  [the longest x1 2.33 us: shards(): call(reverse_first, (half, field, field, field), [vmem, smem, vmem], [acc...]
  transfers between devices with their start and end apart: 14 -> 14, of which waited for: 2 -> 3; matrix products, arithmetic and copies ran while one was open for 0% -> 0% of each run, Pallas kernels for 29% -> 28%
where the time goes in v5:
time: 31 us; the launch traced here: 30.8 us
  starting transfers between devices  15.7 us (51%)
  Pallas kernels  11.7 us (38%)
  waiting for transfers between devices  2.51 us (8%)
  between operations  0.78 us (3%)
    ppermute x4, starting transfers between devices, odd_swap(): return lax.ppermute(x, ('groups', 'row'), route)  8.37 us
    ppermute x6, starting transfers between devices, swapped_sums(): got.append(lax.ppermute(sent, 'row', route))  6.56 us
    ppermute x6, waiting for transfers between devices, swapped_sums(): got.append(lax.ppermute(sent, 'row', route))  2.4 us
    pallas_call x1, Pallas kernels, shards(): call(reverse_first, (half, field, field, field), [vmem, smem, vmem], [acc...  2.33 us
    pallas_call x1, Pallas kernels, shards(): call(reverse_second, (field, field, field, gram_shape), [vmem, smem] + [v...  2.22 us
    pallas_call x1, Pallas kernels, shards(): call(functools.partial(forward, reverses=1), (field, half), [vmem, vmem,...  2.15 us
    pallas_call x1, Pallas kernels, shards(): call(functools.partial(forward, reverses=3), field, [vmem, vmem, smem] +...  1.87 us
    pallas_call x1, Pallas kernels, shards(): call(lambda *refs: finish(*refs, rounds=len(sums), shift=shift), (out, ou...  1.75 us
  transfers between devices with their start and end apart: 14, of which 3 were waited for; matrix products, arithmetic and copies ran while one was open for 0% of the time, Pallas kernels for 28%

profile of v5, /device:TPU:0, one launch (start us, length us, event | category | flops | bytes accessed | tf_op | source)
XLA Modules:
  0.0 30.8 jit_solution(13082447465578364841)
XLA Ops:
  0.6 0.0 slice-start.1
  0.7 1.0 %prepare.1 = (f32[2,8,576]{2,1,0:T(8,128)S(1)}, f32[2,8,576]{2,1,0:T(8,128)S(1)}, f32[2,8,640]{2,1,0:T(8,128)S(1)}, f32[2,1,576]{2,1,0:T(1,128)S(1)}, f32[2,1,576]{2,1,0:T(1,128)S(1)}) custom-call(f32[3,8,384]{2,1,0:T(8,128)} %bitcast.9, s32[384]{0:T(512)} %refs_1_.1, f32[3,384]{1,0:T(4,128)} %refs_2_.1), custom_call_target="tpu_custom_call" | custom-call | flops 10000000000 | bytes 1048576 | tf_op jit(solution)/shard_map/prepare/pallas_call | solution.py:324
  1.7 3.0 %collective-permute-start = (f32[2,8,640]{2,1,0:T(8,128)S(1)}, f32[2,8,640]{2,1,0:T(8,128)S(1)}, u32[]{:S(2)}, u32[]{:S(2)}) collective-permute-start(f32[2,8,640]{2,1,0:T(8,128)S(1)} %get-tuple-element.21), channel_id=1, source_target_pairs={{0,16},{1,2},{2,1},{3,4},{4,3},{5,6},{6,5},{7,8},{8,7},{9,10},{10,... | collective-permute-start | bytes 122888 | tf_op jit(solution)/shard_map/ppermute | solution.py:291
  4.7 0.1 collective-permute-start.1
  4.9 2.3 %reverse_first.1 = (bf16[2,3,576,576]{3,2,1,0:T(8,128)(2,1)S(1)}, f32[2,8,576]{2,1,0:T(8,128)S(1)}, f32[2,8,576]{2,1,0:T(8,128)S(1)}, f32[2,8,576]{2,1,0:T(8,128)S(1)}) custom-call(f32[2,3,576,576]{3,2,1,0:T(8,128)S(1)} %bitcast.7, s32[2,3]{1,0:T(2,128)S(1)} %copy-done, f32[2,8,576]{2,1,0:T(8,128)S(1)} %get-tuple-element.19.y0.y), custom_call_target="tpu_custom_call" | custom-call | flops 254803968 | bytes 1048576 | tf_op jit(solution)/shard_map/reverse_first/pallas_call | solution.py:337
  7.2 2.3 %collective-permute-start.2 = (f32[2,8,576]{2,1,0:T(8,128)S(1)}, f32[2,8,576]{2,1,0:T(8,128)S(1)}, u32[]{:S(2)}, u32[]{:S(2)}) collective-permute-start(f32[2,8,576]{2,1,0:T(8,128)S(1)} %get-tuple-element.27), channel_id=1, source_target_pairs={{0,16},{1,2},{2,1},{3,4},{4,3},{5,6},{6,5},{7,8},{8,7},{9,10},{10,... | collective-permute-start | bytes 110600 | tf_op jit(solution)/shard_map/ppermute | solution.py:291
  9.5 0.1 collective-permute-start.3
  9.7 2.1 %forward_first.1 = (f32[2,8,576]{2,1,0:T(8,128)S(1)}, bf16[2,3,576,576]{3,2,1,0:T(8,128)(2,1)S(1)}) custom-call(bf16[2,3,576,576]{3,2,1,0:T(8,128)(2,1)S(1)} %get-tuple-element.20.th, f32[2,3,576,576]{3,2,1,0:T(8,128)S(1)} %bitcast.7, s32[2,3]{1,0:T(2,128)S(1)} %copy-done, f32[2,8,576]{2,1,0:T(8,128)S(1)} %get-tuple-element.19.y0.y, ...), custom_call_target="tpu_custom_call" | custom-call | flops 254803968 | bytes 1048576 | tf_op jit(solution)/shard_map/forward_first/pallas_call | solution.py:342
  11.8 0.0 collective-permute-done.2
  11.9 1.7 %collective-permute-start.5 = (f32[2,8,640]{2,1,0:T(8,128)S(1)}, f32[2,8,640]{2,1,0:T(8,128)S(1)}, u32[]{:S(2)}, u32[]{:S(2)}) collective-permute-start(f32[2,8,640]{2,1,0:T(8,128)S(1)} %pad.12), channel_id=1, source_target_pairs={{0,16},{1,2},{2,1},{3,4},{4,3},{5,6},{6,5},{7,8},{8,7},{9,10},{10,... | collective-permute-start | bytes 122888 | tf_op jit(solution)/shard_map/ppermute | solution.py:291
  13.6 2.2 %reverse_second.1 = (f32[2,8,576]{2,1,0:T(8,128)S(1)}, f32[2,8,576]{2,1,0:T(8,128)S(1)}, f32[2,8,576]{2,1,0:T(8,128)S(1)}, f32[8,128]{1,0:T(8,128)S(1)}) custom-call(f32[2,3,576,576]{3,2,1,0:T(8,128)S(1)} %bitcast.7, s32[2,3]{1,0:T(2,128)S(1)} %copy-done, f32[2,8,576]{2,1,0:T(8,128)S(1)} %get-tuple-element.36.y1.y, ...), custom_call_target="tpu_custom_call" | custom-call | flops 254803968 | bytes 1048576 | tf_op jit(solution)/shard_map/reverse_second/pallas_call | solution.py:349
  15.8 0.1 collective-permute-done.5.y_o
  15.9 0.4 %cross_grams.1 = f32[8,128]{1,0:T(8,128)S(1)} custom-call(f32[2,8,576]{2,1,0:T(8,128)S(1)} %get-tuple-element.29.out_e, f32[2,8,576]{2,1,0:T(8,128)S(1)} %get-tuple-element.30.out_m.rest_0_, f32[2,8,576]{2,1,0:T(8,128)S(1)} %get-tuple-element.31.out_o, f32[2,8,576]{2,1,0:T(8,128)S(1)} %collective-permute-done.4.y_e, ...), custom_call_target="tpu_custom_call" | custom-call | bytes 1048576 | tf_op jit(solution)/shard_map/cross_grams/pallas_call | solution.py:353
  16.3 1.8 %collective-permute-start.8 = (f32[8,128]{1,0:T(8,128)S(1)}, f32[8,128]{1,0:T(8,128)S(1)}, u32[]{:S(2)}, u32[]{:S(2)}) collective-permute-start(f32[8,128]{1,0:T(8,128)S(1)} %cross_grams.1), channel_id=1, source_target_pairs={{0,3},{1,2},{2,1},{3,0},{4,7},{5,6},{6,5},{7,4},{8,11},{9,10},{10,... | collective-permute-start | bytes 12296 | tf_op jit(solution)/shard_map/ppermute | solution.py:304
  18.1 0.3 collective-permute-start.7
  18.4 0.5 %collective-permute-start.13 = (f32[2,8,576]{2,1,0:T(8,128)S(1)}, f32[2,8,576]{2,1,0:T(8,128)S(1)}, u32[]{:S(2)}, u32[]{:S(2)}) collective-permute-start(f32[2,8,576]{2,1,0:T(8,128)S(1)} %get-tuple-element.29.out_e), channel_id=1, source_target_pairs={{0,1},{1,0},{2,3},{3,2},{4,5},{5,4},{6,7},{7,6},{8,9},{9,8},{10,11... | collective-permute-start | bytes 110600 | tf_op jit(solution)/shard_map/ppermute | solution.py:278
  18.9 1.4 %collective-permute-start.12 = (f32[2,8,576]{2,1,0:T(8,128)S(1)}, f32[2,8,576]{2,1,0:T(8,128)S(1)}, u32[]{:S(2)}, u32[]{:S(2)}) collective-permute-start(f32[2,8,576]{2,1,0:T(8,128)S(1)} %get-tuple-element.31.out_o), channel_id=1, source_target_pairs={{0,16},{1,2},{2,1},{3,4},{4,3},{5,6},{6,5},{7,8},{8,7},{9,10},{10,... | collective-permute-start | bytes 110600 | tf_op jit(solution)/shard_map/ppermute | solution.py:291
  20.3 1.4 %collective-permute-done.7 = f32[8,128]{1,0:T(8,128)S(1)} collective-permute-done((f32[8,128]{1,0:T(8,128)S(1)}, f32[8,128]{1,0:T(8,128)S(1)}, u32[]{:S(2)}, u32[]{:S(2)}) %collective-permute-start.7) | collective-permute-done | bytes 4128 | tf_op jit(solution)/shard_map/ppermute | solution.py:304
  21.8 2.7 %collective-permute-start.11 = (f32[8,128]{1,0:T(8,128)S(1)}, f32[8,128]{1,0:T(8,128)S(1)}, u32[]{:S(2)}, u32[]{:S(2)}) collective-permute-start(f32[8,128]{1,0:T(8,128)S(1)} %add_add_fusion.refs_0_), channel_id=1, source_target_pairs={{0,12},{1,13},{2,14},{3,15},{4,8},{5,9},{6,10},{7,11},{8,4},{9,5},... | collective-permute-start | bytes 12296 | tf_op jit(solution)/shard_map/ppermute | solution.py:304
  24.5 0.4 %collective-permute-start.10 = (f32[8,256]{1,0:T(8,128)S(1)}, f32[8,256]{1,0:T(8,128)S(1)}, u32[]{:S(2)}, u32[]{:S(2)}) collective-permute-start(f32[8,256]{1,0:T(8,128)S(1)} %pad.14), channel_id=1, source_target_pairs={{0,8},{1,9},{2,10},{3,11},{4,12},{5,13},{6,14},{7,15},{8,0},{9,1},... | collective-permute-start | bytes 24584 | tf_op jit(solution)/shard_map/ppermute | solution.py:304
  24.9 1.4 %collective-permute-start.9 = (f32[8,384]{1,0:T(8,128)S(1)}, f32[8,384]{1,0:T(8,128)S(1)}, u32[]{:S(2)}, u32[]{:S(2)}) collective-permute-start(f32[8,384]{1,0:T(8,128)S(1)} %pad.13), channel_id=1, source_target_pairs={{0,4},{1,5},{2,6},{3,7},{4,0},{5,1},{6,2},{7,3},{8,12},{9,13},{10,... | collective-permute-start | bytes 36872 | tf_op jit(solution)/shard_map/ppermute | solution.py:304
  26.2 1.9 %forward_second.1.refs_6_ = f32[2,8,576]{2,1,0:T(8,128)S(1)} custom-call(bf16[2,3,576,576]{3,2,1,0:T(8,128)(2,1)S(1)} %get-tuple-element.20.th, bf16[2,3,576,576]{3,2,1,0:T(8,128)(2,1)S(1)} %get-tuple-element.33.source, s32[2,3]{1,0:T(2,128)S(1)} %copy-done, f32[2,8,576]{2,1,0:T(8,128)S(1)} %get-tuple-element.36.y1.y, ...), custom_call_target="tpu_custom_call" | custom-call | flops 254803968 | bytes 1048576 | tf_op jit(solution)/shard_map/forward_second/pallas_call | solution.py:358
  28.1 0.9 %collective-permute-done.10.refs_2_ = f32[8,256]{1,0:T(8,128)S(1)} collective-permute-done((f32[8,256]{1,0:T(8,128)S(1)}, f32[8,256]{1,0:T(8,128)S(1)}, u32[]{:S(2)}, u32[]{:S(2)}) %collective-permute-start.10) | collective-permute-done | bytes 8224 | tf_op jit(solution)/shard_map/ppermute | solution.py:304
  29.0 1.8 %finish.1 = (f32[3,8,384]{2,1,0:T(8,128)}, f32[3,8,384]{2,1,0:T(8,128)}) custom-call(f32[8,128]{1,0:T(8,128)S(1)} %add_add_fusion.refs_0_, f32[8,384]{1,0:T(8,128)S(1)} %collective-permute-done.9.refs_1_, f32[8,256]{1,0:T(8,128)S(1)} %collective-permute-done.10.refs_2_, f32[8,128]{1,0:T(8,128)S(1)} %collective-permute-done.11.refs_3_, ...), custom_call_target="tpu_custom_call" | custom-call | bytes 1048576 | tf_op jit(solution)/shard_map/finish/pallas_call | solution.py:363
  (26 shorter events, 0.1 us)
Async XLA Ops:
  0.6 4.2 %slice-start = ((s8[8847360]{0:T(1024)(128)(4,1)}), s8[4194304]{0:T(1024)(128)(4,1)S(1)}, s32[]{:S(2)}) async-start(s8[8847360]{0:T(1024)(128)(4,1)} %bitcast.6), calls=%async_computation | async-start | bytes 8388608
  0.6 4.2 %slice-start.1 = ((s8[8847360]{0:T(1024)(128)(4,1)}), s8[4194304]{0:T(1024)(128)(4,1)S(1)}, s32[]{:S(2)}) async-start(s8[8847360]{0:T(1024)(128)(4,1)} %bitcast.6), calls=%async_computation.1 | async-start | bytes 8388608
  0.7 4.2 %slice-start.2 = ((s8[8847360]{0:T(1024)(128)(4,1)}), s8[458752]{0:T(1024)(128)(4,1)S(1)}, s32[]{:S(2)}) async-start(s8[8847360]{0:T(1024)(128)(4,1)} %bitcast.6), calls=%async_computation.2 | async-start | bytes 917504
  0.7 4.2 %copy-start = (s32[2,3]{1,0:T(2,128)S(1)}, s32[2,3]{1,0:T(2,128)}, u32[]{:S(2)}) copy-start(s32[2,3]{1,0:T(2,128)} %cols.7) | copy-start | bytes 76
  1.7 7.9 %collective-permute-start = (f32[2,8,640]{2,1,0:T(8,128)S(1)}, f32[2,8,640]{2,1,0:T(8,128)S(1)}, u32[]{:S(2)}, u32[]{:S(2)}) collective-permute-start(f32[2,8,640]{2,1,0:T(8,128)S(1)} %get-tuple-element.21), channel_id=1, source_target_pairs={{0,16},{1,2},{2,1},{3,4},{4,3},{5,6},{6,5},{7,8},{8,7},{9,10},{10,... | collective-permute-start | bytes 122888 | tf_op jit(solution)/shard_map/ppermute | solution.py:291
  4.7 4.9 %collective-permute-start.1 = (f32[2,8,576]{2,1,0:T(8,128)S(1)}, f32[2,8,576]{2,1,0:T(8,128)S(1)}, u32[]{:S(2)}, u32[]{:S(2)}) collective-permute-start(f32[2,8,576]{2,1,0:T(8,128)S(1)} %get-tuple-element.19.y0.y), channel_id=1, source_target_pairs={{0,1},{1,0},{2,3},{3,2},{4,5},{5,4},{6,7},{7,6},{8,9},{9,8},{10,11... | collective-permute-start | bytes 110600 | tf_op jit(solution)/shard_map/ppermute | solution.py:278
  7.2 4.6 %collective-permute-start.2 = (f32[2,8,576]{2,1,0:T(8,128)S(1)}, f32[2,8,576]{2,1,0:T(8,128)S(1)}, u32[]{:S(2)}, u32[]{:S(2)}) collective-permute-start(f32[2,8,576]{2,1,0:T(8,128)S(1)} %get-tuple-element.27), channel_id=1, source_target_pairs={{0,16},{1,2},{2,1},{3,4},{4,3},{5,6},{6,5},{7,8},{8,7},{9,10},{10,... | collective-permute-start | bytes 110600 | tf_op jit(solution)/shard_map/ppermute | solution.py:291
  9.5 2.3 %collective-permute-start.3 = (f32[2,8,576]{2,1,0:T(8,128)S(1)}, f32[2,8,576]{2,1,0:T(8,128)S(1)}, u32[]{:S(2)}, u32[]{:S(2)}) collective-permute-start(f32[2,8,576]{2,1,0:T(8,128)S(1)} %get-tuple-element.28), channel_id=1, source_target_pairs={{0,1},{1,0},{2,3},{3,2},{4,5},{5,4},{6,7},{7,6},{8,9},{9,8},{10,11... | collective-permute-start | bytes 110600 | tf_op jit(solution)/shard_map/ppermute | solution.py:278
  11.9 4.1 %collective-permute-start.5 = (f32[2,8,640]{2,1,0:T(8,128)S(1)}, f32[2,8,640]{2,1,0:T(8,128)S(1)}, u32[]{:S(2)}, u32[]{:S(2)}) collective-permute-start(f32[2,8,640]{2,1,0:T(8,128)S(1)} %pad.12), channel_id=1, source_target_pairs={{0,16},{1,2},{2,1},{3,4},{4,3},{5,6},{6,5},{7,8},{8,7},{9,10},{10,... | collective-permute-start | bytes 122888 | tf_op jit(solution)/shard_map/ppermute | solution.py:291
  13.6 2.2 %collective-permute-start.4 = (f32[2,8,576]{2,1,0:T(8,128)S(1)}, f32[2,8,576]{2,1,0:T(8,128)S(1)}, u32[]{:S(2)}, u32[]{:S(2)}) collective-permute-start(f32[2,8,576]{2,1,0:T(8,128)S(1)} %get-tuple-element.36.y1.y), channel_id=1, source_target_pairs={{0,1},{1,0},{2,3},{3,2},{4,5},{5,4},{6,7},{7,6},{8,9},{9,8},{10,11... | collective-permute-start | bytes 110600 | tf_op jit(solution)/shard_map/ppermute | solution.py:278
  16.3 4.0 %collective-permute-start.8 = (f32[8,128]{1,0:T(8,128)S(1)}, f32[8,128]{1,0:T(8,128)S(1)}, u32[]{:S(2)}, u32[]{:S(2)}) collective-permute-start(f32[8,128]{1,0:T(8,128)S(1)} %cross_grams.1), channel_id=1, source_target_pairs={{0,3},{1,2},{2,1},{3,0},{4,7},{5,6},{6,5},{7,4},{8,11},{9,10},{10,... | collective-permute-start | bytes 12296 | tf_op jit(solution)/shard_map/ppermute | solution.py:304
  18.1 3.6 %collective-permute-start.7 = (f32[8,128]{1,0:T(8,128)S(1)}, f32[8,128]{1,0:T(8,128)S(1)}, u32[]{:S(2)}, u32[]{:S(2)}) collective-permute-start(f32[8,128]{1,0:T(8,128)S(1)} %cross_grams.1), channel_id=1, source_target_pairs={{0,2},{1,3},{2,0},{3,1},{4,6},{5,7},{6,4},{7,5},{8,10},{9,11},{10,... | collective-permute-start | bytes 12296 | tf_op jit(solution)/shard_map/ppermute | solution.py:304
  18.4 3.3 %collective-permute-start.6 = (f32[8,128]{1,0:T(8,128)S(1)}, f32[8,128]{1,0:T(8,128)S(1)}, u32[]{:S(2)}, u32[]{:S(2)}) collective-permute-start(f32[8,128]{1,0:T(8,128)S(1)} %cross_grams.1), channel_id=1, source_target_pairs={{0,1},{1,0},{2,3},{3,2},{4,5},{5,4},{6,7},{7,6},{8,9},{9,8},{10,11... | collective-permute-start | bytes 12296 | tf_op jit(solution)/shard_map/ppermute | solution.py:304
  18.4 7.8 %collective-permute-start.13 = (f32[2,8,576]{2,1,0:T(8,128)S(1)}, f32[2,8,576]{2,1,0:T(8,128)S(1)}, u32[]{:S(2)}, u32[]{:S(2)}) collective-permute-start(f32[2,8,576]{2,1,0:T(8,128)S(1)} %get-tuple-element.29.out_e), channel_id=1, source_target_pairs={{0,1},{1,0},{2,3},{3,2},{4,5},{5,4},{6,7},{7,6},{8,9},{9,8},{10,11... | collective-permute-start | bytes 110600 | tf_op jit(solution)/shard_map/ppermute | solution.py:278
  18.9 7.3 %collective-permute-start.12 = (f32[2,8,576]{2,1,0:T(8,128)S(1)}, f32[2,8,576]{2,1,0:T(8,128)S(1)}, u32[]{:S(2)}, u32[]{:S(2)}) collective-permute-start(f32[2,8,576]{2,1,0:T(8,128)S(1)} %get-tuple-element.31.out_o), channel_id=1, source_target_pairs={{0,16},{1,2},{2,1},{3,4},{4,3},{5,6},{6,5},{7,8},{8,7},{9,10},{10,... | collective-permute-start | bytes 110600 | tf_op jit(solution)/shard_map/ppermute | solution.py:291
  21.8 6.3 %collective-permute-start.11 = (f32[8,128]{1,0:T(8,128)S(1)}, f32[8,128]{1,0:T(8,128)S(1)}, u32[]{:S(2)}, u32[]{:S(2)}) collective-permute-start(f32[8,128]{1,0:T(8,128)S(1)} %add_add_fusion.refs_0_), channel_id=1, source_target_pairs={{0,12},{1,13},{2,14},{3,15},{4,8},{5,9},{6,10},{7,11},{8,4},{9,5},... | collective-permute-start | bytes 12296 | tf_op jit(solution)/shard_map/ppermute | solution.py:304
  24.5 4.6 %collective-permute-start.10 = (f32[8,256]{1,0:T(8,128)S(1)}, f32[8,256]{1,0:T(8,128)S(1)}, u32[]{:S(2)}, u32[]{:S(2)}) collective-permute-start(f32[8,256]{1,0:T(8,128)S(1)} %pad.14), channel_id=1, source_target_pairs={{0,8},{1,9},{2,10},{3,11},{4,12},{5,13},{6,14},{7,15},{8,0},{9,1},... | collective-permute-start | bytes 24584 | tf_op jit(solution)/shard_map/ppermute | solution.py:304
  24.9 4.2 %collective-permute-start.9 = (f32[8,384]{1,0:T(8,128)S(1)}, f32[8,384]{1,0:T(8,128)S(1)}, u32[]{:S(2)}, u32[]{:S(2)}) collective-permute-start(f32[8,384]{1,0:T(8,128)S(1)} %pad.13), channel_id=1, source_target_pairs={{0,4},{1,5},{2,6},{3,7},{4,0},{5,1},{6,2},{7,3},{8,12},{9,13},{10,... | collective-permute-start | bytes 36872 | tf_op jit(solution)/shard_map/ppermute | solution.py:304

commit v6 on v5

--- a/solution.py
+++ b/solution.py
@@ -242,16 +242,14 @@
     h11s = small_dot(c11, step)
     past = h11s - small_dot(c01, keep)
     image = small_dot(c12, step) + shift * past - small_dot(c11, keep)
-    both = small_dot(
-        columns_of(step_t), jnp.concatenate([past, image, h11 + shift * h01], axis=1)
-    )
+    onward = small_dot(columns_of(h11 + shift * h01), inverse0)
+    both = small_dot(columns_of(step_t), jnp.concatenate([past, image, onward], axis=1))
     rho = both[:, :n]
-    mixing = small_dot(columns_of(inverse0), rho)
-    curvature = both[:, n : 2 * n] - small_dot(columns_of(both[:, 2 * n :]), mixing)
+    curvature = both[:, n : 2 * n] - small_dot(columns_of(both[:, 2 * n :]), rho)
     rho_columns = columns_of(rho)
     lead_t = keep_t + small_dot(rho_columns, inverse0)
-    after_t = small_dot(rho_columns, eliminate([(curvature, eye)])[0])
-    moved = small_dot(columns_of(after_t), jnp.concatenate([lead_t, step_t], axis=1))
+    solved = eliminate([(curvature, jnp.concatenate([lead_t, step_t], axis=1))])[0]
+    moved = small_dot(rho_columns, solved)
     lead_after, step_after = moved[:, :n], moved[:, n:]
     for_disp = (step_t + lead_after, -step_after)
     for_resid = (
@@ -296,10 +294,12 @@
     width = x.shape[1]
     base = 1
     while True:
-        masks = [base, 2 * base, 3 * base] if 2 * base < count else [base]
+        cross = 1 if base > 1 else 0
+        masks = [base, 2 * base + cross, 3 * base + cross] if 2 * base < count else [base]
         got = []
         for i, mask in enumerate(masks):
-            sent = jnp.pad(x, ((0, 0), (0, (len(masks) - 1 - i) * width))) if base > 1 else x
+            extra = (len(masks) - 1 - i) * width if base > 1 else 0
+            sent = jnp.pad(x, ((0, 0), (0, extra))) if extra else x
             route = [(j, j ^ mask) for j in range(count)]
             got.append(lax.ppermute(sent, "row", route))
         base *= len(masks) + 1

time: 31 us -> 30.1 us (0.971)
  waiting for transfers between devices: 2.51 us -> 2.01 us
    ppermute x6, waiting for transfers between devices: 2.4 us -> 1.9 us  [swapped_sums(): got.append(lax.ppermute(sent, 'row', route))]
  transfers between devices with their start and end apart: 14 -> 14, of which waited for: 3 -> 3; matrix products, arithmetic and copies ran while one was open for 0% -> 0% of each run, Pallas kernels for 28% -> 29%
where the time goes in v6:
time: 30.1 us; the launch traced here: 30 us
  starting transfers between devices  15.4 us (51%)
  Pallas kernels  11.7 us (39%)
  waiting for transfers between devices  2.01 us (7%)
  between operations  0.79 us (3%)
    ppermute x4, starting transfers between devices, odd_swap(): return lax.ppermute(x, ('groups', 'row'), route)  8.37 us
    ppermute x6, starting transfers between devices, swapped_sums(): got.append(lax.ppermute(sent, 'row', route))  6.28 us
    pallas_call x1, Pallas kernels, shards(): call(reverse_first, (half, field, field, field), [vmem, smem, vmem], [acc...  2.33 us
    pallas_call x1, Pallas kernels, shards(): call(reverse_second, (field, field, field, gram_shape), [vmem, smem] + [v...  2.22 us
    pallas_call x1, Pallas kernels, shards(): call(functools.partial(forward, reverses=1), (field, half), [vmem, vmem,...  2.15 us
    ppermute x6, waiting for transfers between devices, swapped_sums(): got.append(lax.ppermute(sent, 'row', route))  1.9 us
    pallas_call x1, Pallas kernels, shards(): call(functools.partial(forward, reverses=3), field, [vmem, vmem, smem] +...  1.87 us
    pallas_call x1, Pallas kernels, shards(): call(lambda *refs: finish(*refs, rounds=len(sums), shift=shift), (out, ou...  1.7 us
  transfers between devices with their start and end apart: 14, of which 3 were waited for; matrix products, arithmetic and copies ran while one was open for 0% of the time, Pallas kernels for 29%

profile of v6, /device:TPU:0, one launch (start us, length us, event | category | flops | bytes accessed | tf_op | source)
XLA Modules:
  0.0 30.0 jit_solution(16074821808784608738)
XLA Ops:
  0.6 0.0 slice-start
  0.7 1.0 %prepare.1 = (f32[2,8,576]{2,1,0:T(8,128)S(1)}, f32[2,8,576]{2,1,0:T(8,128)S(1)}, f32[2,8,640]{2,1,0:T(8,128)S(1)}, f32[2,1,576]{2,1,0:T(1,128)S(1)}, f32[2,1,576]{2,1,0:T(1,128)S(1)}) custom-call(f32[3,8,384]{2,1,0:T(8,128)} %bitcast.9, s32[384]{0:T(512)} %refs_1_.1, f32[3,384]{1,0:T(4,128)} %refs_2_.1), custom_call_target="tpu_custom_call" | custom-call | flops 10000000000 | bytes 1048576 | tf_op jit(solution)/shard_map/prepare/pallas_call | solution.py:324
  1.7 3.0 %collective-permute-start = (f32[2,8,640]{2,1,0:T(8,128)S(1)}, f32[2,8,640]{2,1,0:T(8,128)S(1)}, u32[]{:S(2)}, u32[]{:S(2)}) collective-permute-start(f32[2,8,640]{2,1,0:T(8,128)S(1)} %get-tuple-element.21), channel_id=1, source_target_pairs={{0,16},{1,2},{2,1},{3,4},{4,3},{5,6},{6,5},{7,8},{8,7},{9,10},{10,... | collective-permute-start | bytes 122888 | tf_op jit(solution)/shard_map/ppermute | solution.py:289
  4.7 0.1 collective-permute-start.1
  4.9 2.3 %reverse_first.1 = (bf16[2,3,576,576]{3,2,1,0:T(8,128)(2,1)S(1)}, f32[2,8,576]{2,1,0:T(8,128)S(1)}, f32[2,8,576]{2,1,0:T(8,128)S(1)}, f32[2,8,576]{2,1,0:T(8,128)S(1)}) custom-call(f32[2,3,576,576]{3,2,1,0:T(8,128)S(1)} %bitcast.7, s32[2,3]{1,0:T(2,128)S(1)} %copy-done, f32[2,8,576]{2,1,0:T(8,128)S(1)} %get-tuple-element.19.y0.y), custom_call_target="tpu_custom_call" | custom-call | flops 254803968 | bytes 1048576 | tf_op jit(solution)/shard_map/reverse_first/pallas_call | solution.py:337
  7.2 2.3 %collective-permute-start.2 = (f32[2,8,576]{2,1,0:T(8,128)S(1)}, f32[2,8,576]{2,1,0:T(8,128)S(1)}, u32[]{:S(2)}, u32[]{:S(2)}) collective-permute-start(f32[2,8,576]{2,1,0:T(8,128)S(1)} %get-tuple-element.27), channel_id=1, source_target_pairs={{0,16},{1,2},{2,1},{3,4},{4,3},{5,6},{6,5},{7,8},{8,7},{9,10},{10,... | collective-permute-start | bytes 110600 | tf_op jit(solution)/shard_map/ppermute | solution.py:289
  9.5 0.1 collective-permute-start.3
  9.7 2.1 %forward_first.1 = (f32[2,8,576]{2,1,0:T(8,128)S(1)}, bf16[2,3,576,576]{3,2,1,0:T(8,128)(2,1)S(1)}) custom-call(bf16[2,3,576,576]{3,2,1,0:T(8,128)(2,1)S(1)} %get-tuple-element.20.th, f32[2,3,576,576]{3,2,1,0:T(8,128)S(1)} %bitcast.7, s32[2,3]{1,0:T(2,128)S(1)} %copy-done, f32[2,8,576]{2,1,0:T(8,128)S(1)} %get-tuple-element.19.y0.y, ...), custom_call_target="tpu_custom_call" | custom-call | flops 254803968 | bytes 1048576 | tf_op jit(solution)/shard_map/forward_first/pallas_call | solution.py:342
  11.8 0.0 collective-permute-done.2
  11.9 1.7 %collective-permute-start.5 = (f32[2,8,640]{2,1,0:T(8,128)S(1)}, f32[2,8,640]{2,1,0:T(8,128)S(1)}, u32[]{:S(2)}, u32[]{:S(2)}) collective-permute-start(f32[2,8,640]{2,1,0:T(8,128)S(1)} %pad.12), channel_id=1, source_target_pairs={{0,16},{1,2},{2,1},{3,4},{4,3},{5,6},{6,5},{7,8},{8,7},{9,10},{10,... | collective-permute-start | bytes 122888 | tf_op jit(solution)/shard_map/ppermute | solution.py:289
  13.6 2.2 %reverse_second.1 = (f32[2,8,576]{2,1,0:T(8,128)S(1)}, f32[2,8,576]{2,1,0:T(8,128)S(1)}, f32[2,8,576]{2,1,0:T(8,128)S(1)}, f32[8,128]{1,0:T(8,128)S(1)}) custom-call(f32[2,3,576,576]{3,2,1,0:T(8,128)S(1)} %bitcast.7, s32[2,3]{1,0:T(2,128)S(1)} %copy-done, f32[2,8,576]{2,1,0:T(8,128)S(1)} %get-tuple-element.36.y1.y, ...), custom_call_target="tpu_custom_call" | custom-call | flops 254803968 | bytes 1048576 | tf_op jit(solution)/shard_map/reverse_second/pallas_call | solution.py:349
  15.8 0.1 collective-permute-done.5.y_o
  15.9 0.4 %cross_grams.1 = f32[8,128]{1,0:T(8,128)S(1)} custom-call(f32[2,8,576]{2,1,0:T(8,128)S(1)} %get-tuple-element.29.out_e, f32[2,8,576]{2,1,0:T(8,128)S(1)} %get-tuple-element.30.out_m.rest_0_, f32[2,8,576]{2,1,0:T(8,128)S(1)} %get-tuple-element.31.out_o, f32[2,8,576]{2,1,0:T(8,128)S(1)} %collective-permute-done.4.y_e, ...), custom_call_target="tpu_custom_call" | custom-call | bytes 1048576 | tf_op jit(solution)/shard_map/cross_grams/pallas_call | solution.py:353
  16.3 1.8 %collective-permute-start.8 = (f32[8,128]{1,0:T(8,128)S(1)}, f32[8,128]{1,0:T(8,128)S(1)}, u32[]{:S(2)}, u32[]{:S(2)}) collective-permute-start(f32[8,128]{1,0:T(8,128)S(1)} %cross_grams.1), channel_id=1, source_target_pairs={{0,3},{1,2},{2,1},{3,0},{4,7},{5,6},{6,5},{7,4},{8,11},{9,10},{10,... | collective-permute-start | bytes 12296 | tf_op jit(solution)/shard_map/ppermute | solution.py:304
  18.1 0.3 collective-permute-start.7
  18.4 0.5 %collective-permute-start.13 = (f32[2,8,576]{2,1,0:T(8,128)S(1)}, f32[2,8,576]{2,1,0:T(8,128)S(1)}, u32[]{:S(2)}, u32[]{:S(2)}) collective-permute-start(f32[2,8,576]{2,1,0:T(8,128)S(1)} %get-tuple-element.29.out_e), channel_id=1, source_target_pairs={{0,1},{1,0},{2,3},{3,2},{4,5},{5,4},{6,7},{7,6},{8,9},{9,8},{10,11... | collective-permute-start | bytes 110600 | tf_op jit(solution)/shard_map/ppermute | solution.py:276
  18.9 1.4 %collective-permute-start.12 = (f32[2,8,576]{2,1,0:T(8,128)S(1)}, f32[2,8,576]{2,1,0:T(8,128)S(1)}, u32[]{:S(2)}, u32[]{:S(2)}) collective-permute-start(f32[2,8,576]{2,1,0:T(8,128)S(1)} %get-tuple-element.31.out_o), channel_id=1, source_target_pairs={{0,16},{1,2},{2,1},{3,4},{4,3},{5,6},{6,5},{7,8},{8,7},{9,10},{10,... | collective-permute-start | bytes 110600 | tf_op jit(solution)/shard_map/ppermute | solution.py:289
  20.3 1.4 %collective-permute-done.7 = f32[8,128]{1,0:T(8,128)S(1)} collective-permute-done((f32[8,128]{1,0:T(8,128)S(1)}, f32[8,128]{1,0:T(8,128)S(1)}, u32[]{:S(2)}, u32[]{:S(2)}) %collective-permute-start.7) | collective-permute-done | bytes 4128 | tf_op jit(solution)/shard_map/ppermute | solution.py:304
  21.8 1.8 %collective-permute-start.11 = (f32[8,128]{1,0:T(8,128)S(1)}, f32[8,128]{1,0:T(8,128)S(1)}, u32[]{:S(2)}, u32[]{:S(2)}) collective-permute-start(f32[8,128]{1,0:T(8,128)S(1)} %add_add_fusion.refs_0_), channel_id=1, source_target_pairs={{0,13},{1,12},{2,15},{3,14},{4,9},{5,8},{6,11},{7,10},{8,5},{9,4},... | collective-permute-start | bytes 12296 | tf_op jit(solution)/shard_map/ppermute | solution.py:304
  23.6 1.0 %collective-permute-start.10 = (f32[8,256]{1,0:T(8,128)S(1)}, f32[8,256]{1,0:T(8,128)S(1)}, u32[]{:S(2)}, u32[]{:S(2)}) collective-permute-start(f32[8,256]{1,0:T(8,128)S(1)} %pad.14), channel_id=1, source_target_pairs={{0,9},{1,8},{2,11},{3,10},{4,13},{5,12},{6,15},{7,14},{8,1},{9,0},... | collective-permute-start | bytes 24584 | tf_op jit(solution)/shard_map/ppermute | solution.py:304
  24.6 1.4 %collective-permute-start.9 = (f32[8,384]{1,0:T(8,128)S(1)}, f32[8,384]{1,0:T(8,128)S(1)}, u32[]{:S(2)}, u32[]{:S(2)}) collective-permute-start(f32[8,384]{1,0:T(8,128)S(1)} %pad.13), channel_id=1, source_target_pairs={{0,4},{1,5},{2,6},{3,7},{4,0},{5,1},{6,2},{7,3},{8,12},{9,13},{10,... | collective-permute-start | bytes 36872 | tf_op jit(solution)/shard_map/ppermute | solution.py:304
  25.9 1.9 %forward_second.1.refs_6_ = f32[2,8,576]{2,1,0:T(8,128)S(1)} custom-call(bf16[2,3,576,576]{3,2,1,0:T(8,128)(2,1)S(1)} %get-tuple-element.20.th, bf16[2,3,576,576]{3,2,1,0:T(8,128)(2,1)S(1)} %get-tuple-element.33.source, s32[2,3]{1,0:T(2,128)S(1)} %copy-done, f32[2,8,576]{2,1,0:T(8,128)S(1)} %get-tuple-element.36.y1.y, ...), custom_call_target="tpu_custom_call" | custom-call | flops 254803968 | bytes 1048576 | tf_op jit(solution)/shard_map/forward_second/pallas_call | solution.py:358
  27.8 0.4 %collective-permute-done.9.refs_1_ = f32[8,384]{1,0:T(8,128)S(1)} collective-permute-done((f32[8,384]{1,0:T(8,128)S(1)}, f32[8,384]{1,0:T(8,128)S(1)}, u32[]{:S(2)}, u32[]{:S(2)}) %collective-permute-start.9) | collective-permute-done | bytes 12320 | tf_op jit(solution)/shard_map/ppermute | solution.py:304
  28.3 1.7 %finish.1 = (f32[3,8,384]{2,1,0:T(8,128)}, f32[3,8,384]{2,1,0:T(8,128)}) custom-call(f32[8,128]{1,0:T(8,128)S(1)} %add_add_fusion.refs_0_, f32[8,384]{1,0:T(8,128)S(1)} %collective-permute-done.9.refs_1_, f32[8,256]{1,0:T(8,128)S(1)} %collective-permute-done.10.refs_2_, f32[8,128]{1,0:T(8,128)S(1)} %collective-permute-done.11.refs_3_, ...), custom_call_target="tpu_custom_call" | custom-call | bytes 1048576 | tf_op jit(solution)/shard_map/finish/pallas_call | solution.py:363
  (26 shorter events, 0.1 us)
Async XLA Ops:
  0.6 4.2 %slice-start = ((s8[8847360]{0:T(1024)(128)(4,1)}), s8[4194304]{0:T(1024)(128)(4,1)S(1)}, s32[]{:S(2)}) async-start(s8[8847360]{0:T(1024)(128)(4,1)} %bitcast.6), calls=%async_computation | async-start | bytes 8388608
  0.6 4.2 %slice-start.1 = ((s8[8847360]{0:T(1024)(128)(4,1)}), s8[4194304]{0:T(1024)(128)(4,1)S(1)}, s32[]{:S(2)}) async-start(s8[8847360]{0:T(1024)(128)(4,1)} %bitcast.6), calls=%async_computation.1 | async-start | bytes 8388608
  0.7 4.2 %slice-start.2 = ((s8[8847360]{0:T(1024)(128)(4,1)}), s8[458752]{0:T(1024)(128)(4,1)S(1)}, s32[]{:S(2)}) async-start(s8[8847360]{0:T(1024)(128)(4,1)} %bitcast.6), calls=%async_computation.2 | async-start | bytes 917504
  0.7 4.2 %copy-start = (s32[2,3]{1,0:T(2,128)S(1)}, s32[2,3]{1,0:T(2,128)}, u32[]{:S(2)}) copy-start(s32[2,3]{1,0:T(2,128)} %cols.7) | copy-start | bytes 76
  1.7 7.9 %collective-permute-start = (f32[2,8,640]{2,1,0:T(8,128)S(1)}, f32[2,8,640]{2,1,0:T(8,128)S(1)}, u32[]{:S(2)}, u32[]{:S(2)}) collective-permute-start(f32[2,8,640]{2,1,0:T(8,128)S(1)} %get-tuple-element.21), channel_id=1, source_target_pairs={{0,16},{1,2},{2,1},{3,4},{4,3},{5,6},{6,5},{7,8},{8,7},{9,10},{10,... | collective-permute-start | bytes 122888 | tf_op jit(solution)/shard_map/ppermute | solution.py:289
  4.7 4.9 %collective-permute-start.1 = (f32[2,8,576]{2,1,0:T(8,128)S(1)}, f32[2,8,576]{2,1,0:T(8,128)S(1)}, u32[]{:S(2)}, u32[]{:S(2)}) collective-permute-start(f32[2,8,576]{2,1,0:T(8,128)S(1)} %get-tuple-element.19.y0.y), channel_id=1, source_target_pairs={{0,1},{1,0},{2,3},{3,2},{4,5},{5,4},{6,7},{7,6},{8,9},{9,8},{10,11... | collective-permute-start | bytes 110600 | tf_op jit(solution)/shard_map/ppermute | solution.py:276
  7.2 4.6 %collective-permute-start.2 = (f32[2,8,576]{2,1,0:T(8,128)S(1)}, f32[2,8,576]{2,1,0:T(8,128)S(1)}, u32[]{:S(2)}, u32[]{:S(2)}) collective-permute-start(f32[2,8,576]{2,1,0:T(8,128)S(1)} %get-tuple-element.27), channel_id=1, source_target_pairs={{0,16},{1,2},{2,1},{3,4},{4,3},{5,6},{6,5},{7,8},{8,7},{9,10},{10,... | collective-permute-start | bytes 110600 | tf_op jit(solution)/shard_map/ppermute | solution.py:289
  9.5 2.3 %collective-permute-start.3 = (f32[2,8,576]{2,1,0:T(8,128)S(1)}, f32[2,8,576]{2,1,0:T(8,128)S(1)}, u32[]{:S(2)}, u32[]{:S(2)}) collective-permute-start(f32[2,8,576]{2,1,0:T(8,128)S(1)} %get-tuple-element.28), channel_id=1, source_target_pairs={{0,1},{1,0},{2,3},{3,2},{4,5},{5,4},{6,7},{7,6},{8,9},{9,8},{10,11... | collective-permute-start | bytes 110600 | tf_op jit(solution)/shard_map/ppermute | solution.py:276
  11.9 4.1 %collective-permute-start.5 = (f32[2,8,640]{2,1,0:T(8,128)S(1)}, f32[2,8,640]{2,1,0:T(8,128)S(1)}, u32[]{:S(2)}, u32[]{:S(2)}) collective-permute-start(f32[2,8,640]{2,1,0:T(8,128)S(1)} %pad.12), channel_id=1, source_target_pairs={{0,16},{1,2},{2,1},{3,4},{4,3},{5,6},{6,5},{7,8},{8,7},{9,10},{10,... | collective-permute-start | bytes 122888 | tf_op jit(solution)/shard_map/ppermute | solution.py:289
  13.6 2.2 %collective-permute-start.4 = (f32[2,8,576]{2,1,0:T(8,128)S(1)}, f32[2,8,576]{2,1,0:T(8,128)S(1)}, u32[]{:S(2)}, u32[]{:S(2)}) collective-permute-start(f32[2,8,576]{2,1,0:T(8,128)S(1)} %get-tuple-element.36.y1.y), channel_id=1, source_target_pairs={{0,1},{1,0},{2,3},{3,2},{4,5},{5,4},{6,7},{7,6},{8,9},{9,8},{10,11... | collective-permute-start | bytes 110600 | tf_op jit(solution)/shard_map/ppermute | solution.py:276
  16.3 4.0 %collective-permute-start.8 = (f32[8,128]{1,0:T(8,128)S(1)}, f32[8,128]{1,0:T(8,128)S(1)}, u32[]{:S(2)}, u32[]{:S(2)}) collective-permute-start(f32[8,128]{1,0:T(8,128)S(1)} %cross_grams.1), channel_id=1, source_target_pairs={{0,3},{1,2},{2,1},{3,0},{4,7},{5,6},{6,5},{7,4},{8,11},{9,10},{10,... | collective-permute-start | bytes 12296 | tf_op jit(solution)/shard_map/ppermute | solution.py:304
  18.1 3.6 %collective-permute-start.7 = (f32[8,128]{1,0:T(8,128)S(1)}, f32[8,128]{1,0:T(8,128)S(1)}, u32[]{:S(2)}, u32[]{:S(2)}) collective-permute-start(f32[8,128]{1,0:T(8,128)S(1)} %cross_grams.1), channel_id=1, source_target_pairs={{0,2},{1,3},{2,0},{3,1},{4,6},{5,7},{6,4},{7,5},{8,10},{9,11},{10,... | collective-permute-start | bytes 12296 | tf_op jit(solution)/shard_map/ppermute | solution.py:304
  18.4 3.3 %collective-permute-start.6 = (f32[8,128]{1,0:T(8,128)S(1)}, f32[8,128]{1,0:T(8,128)S(1)}, u32[]{:S(2)}, u32[]{:S(2)}) collective-permute-start(f32[8,128]{1,0:T(8,128)S(1)} %cross_grams.1), channel_id=1, source_target_pairs={{0,1},{1,0},{2,3},{3,2},{4,5},{5,4},{6,7},{7,6},{8,9},{9,8},{10,11... | collective-permute-start | bytes 12296 | tf_op jit(solution)/shard_map/ppermute | solution.py:304
  18.4 7.5 %collective-permute-start.13 = (f32[2,8,576]{2,1,0:T(8,128)S(1)}, f32[2,8,576]{2,1,0:T(8,128)S(1)}, u32[]{:S(2)}, u32[]{:S(2)}) collective-permute-start(f32[2,8,576]{2,1,0:T(8,128)S(1)} %get-tuple-element.29.out_e), channel_id=1, source_target_pairs={{0,1},{1,0},{2,3},{3,2},{4,5},{5,4},{6,7},{7,6},{8,9},{9,8},{10,11... | collective-permute-start | bytes 110600 | tf_op jit(solution)/shard_map/ppermute | solution.py:276
  18.9 7.0 %collective-permute-start.12 = (f32[2,8,576]{2,1,0:T(8,128)S(1)}, f32[2,8,576]{2,1,0:T(8,128)S(1)}, u32[]{:S(2)}, u32[]{:S(2)}) collective-permute-start(f32[2,8,576]{2,1,0:T(8,128)S(1)} %get-tuple-element.31.out_o), channel_id=1, source_target_pairs={{0,16},{1,2},{2,1},{3,4},{4,3},{5,6},{6,5},{7,8},{8,7},{9,10},{10,... | collective-permute-start | bytes 110600 | tf_op jit(solution)/shard_map/ppermute | solution.py:289
  21.8 6.1 %collective-permute-start.11 = (f32[8,128]{1,0:T(8,128)S(1)}, f32[8,128]{1,0:T(8,128)S(1)}, u32[]{:S(2)}, u32[]{:S(2)}) collective-permute-start(f32[8,128]{1,0:T(8,128)S(1)} %add_add_fusion.refs_0_), channel_id=1, source_target_pairs={{0,13},{1,12},{2,15},{3,14},{4,9},{5,8},{6,11},{7,10},{8,5},{9,4},... | collective-permute-start | bytes 12296 | tf_op jit(solution)/shard_map/ppermute | solution.py:304
  23.6 4.2 %collective-permute-start.10 = (f32[8,256]{1,0:T(8,128)S(1)}, f32[8,256]{1,0:T(8,128)S(1)}, u32[]{:S(2)}, u32[]{:S(2)}) collective-permute-start(f32[8,256]{1,0:T(8,128)S(1)} %pad.14), channel_id=1, source_target_pairs={{0,9},{1,8},{2,11},{3,10},{4,13},{5,12},{6,15},{7,14},{8,1},{9,0},... | collective-permute-start | bytes 24584 | tf_op jit(solution)/shard_map/ppermute | solution.py:304
  24.6 3.7 %collective-permute-start.9 = (f32[8,384]{1,0:T(8,128)S(1)}, f32[8,384]{1,0:T(8,128)S(1)}, u32[]{:S(2)}, u32[]{:S(2)}) collective-permute-start(f32[8,384]{1,0:T(8,128)S(1)} %pad.13), channel_id=1, source_target_pairs={{0,4},{1,5},{2,6},{3,7},{4,0},{5,1},{6,2},{7,3},{8,12},{9,13},{10,... | collective-permute-start | bytes 36872 | tf_op jit(solution)/shard_map/ppermute | solution.py:304

commit v7 on v6

--- a/solution.py
+++ b/solution.py
@@ -168,7 +168,8 @@
     for b in range(blocks):
         out_e[b] = acc[b]
         out_m[b] = acc[blocks + b]
-        out_o[b] = acc[2 * blocks + b]
+        out_o[b] = jnp.zeros(out_o.shape[1:], f32)
+        out_o[b, :, : y1.shape[2]] = acc[2 * blocks + b]
 
 
 def cross_grams(out_e, out_m, out_o, y_e, y, y_o, grams, result):
@@ -176,7 +177,7 @@
     one = other = jnp.zeros((2 * n, 2 * n), f32)
     for b in range(y.shape[0]):
         for out, field in ((out_m, y), (out_e, y_e), (out_o, y_o)):
-            sent, seen = parts_of(out[b]), parts_of(field[b, :, :width])
+            sent, seen = parts_of(out[b, :, :width]), parts_of(field[b, :, :width])
             one += turned_dot(sent, seen)
             other += turned_dot(seen, sent)
     both = whole_of(one + other)
@@ -347,7 +348,7 @@
     y1 = w * mk
     y1_e, y1_o = even_swap(y1), odd_swap(widened(y1))
     c_e, c_m, c_o, grams = call(
-        reverse_second, (field, field, field, gram_shape), [vmem, smem] + [vmem] * 4,
+        reverse_second, (field, field, wide, gram_shape), [vmem, smem] + [vmem] * 4,
         [acc], flops, name="reverse_second",
     )(coupling, columns, y1, r0, w, dg)
     grams = call(cross_grams, gram_shape, [vmem] * 7, name="cross_grams")(

time: 30.1 us -> 30.1 us (level)
  no operation moved by 1% of the time
where the time goes in v7:
time: 30.1 us; the launch traced here: 30 us
  starting transfers between devices  15.4 us (51%)
  Pallas kernels  11.7 us (39%)
  waiting for transfers between devices  2 us (7%)
  between operations  0.79 us (3%)
    ppermute x4, starting transfers between devices, odd_swap(): return lax.ppermute(x, ('groups', 'row'), route)  8.39 us
    ppermute x6, starting transfers between devices, swapped_sums(): got.append(lax.ppermute(sent, 'row', route))  6.27 us
    pallas_call x1, Pallas kernels, shards(): call(reverse_first, (half, field, field, field), [vmem, smem, vmem], [acc...  2.33 us
    pallas_call x1, Pallas kernels, shards(): call(reverse_second, (field, field, wide, gram_shape), [vmem, smem] + [vm...  2.23 us
    pallas_call x1, Pallas kernels, shards(): call(functools.partial(forward, reverses=1), (field, half), [vmem, vmem,...  2.15 us
    ppermute x6, waiting for transfers between devices, swapped_sums(): got.append(lax.ppermute(sent, 'row', route))  1.9 us
    pallas_call x1, Pallas kernels, shards(): call(functools.partial(forward, reverses=3), field, [vmem, vmem, smem] +...  1.87 us
    pallas_call x1, Pallas kernels, shards(): call(lambda *refs: finish(*refs, rounds=len(sums), shift=shift), (out, ou...  1.7 us
  transfers between devices with their start and end apart: 14, of which 3 were waited for; matrix products, arithmetic and copies ran while one was open for 0% of the time, Pallas kernels for 29%

profile of v7, /device:TPU:0, one launch (start us, length us, event | category | flops | bytes accessed | tf_op | source)
XLA Modules:
  0.0 30.0 jit_solution(285963621533696508)
XLA Ops:
  0.7 0.0 slice-start.2
  0.7 1.0 %prepare.1 = (f32[2,8,576]{2,1,0:T(8,128)S(1)}, f32[2,8,576]{2,1,0:T(8,128)S(1)}, f32[2,8,640]{2,1,0:T(8,128)S(1)}, f32[2,1,576]{2,1,0:T(1,128)S(1)}, f32[2,1,576]{2,1,0:T(1,128)S(1)}) custom-call(f32[3,8,384]{2,1,0:T(8,128)} %bitcast.9, s32[384]{0:T(512)} %refs_1_.1, f32[3,384]{1,0:T(4,128)} %refs_2_.1), custom_call_target="tpu_custom_call" | custom-call | flops 10000000000 | bytes 1048576 | tf_op jit(solution)/shard_map/prepare/pallas_call | solution.py:325
  1.7 3.0 %collective-permute-start = (f32[2,8,640]{2,1,0:T(8,128)S(1)}, f32[2,8,640]{2,1,0:T(8,128)S(1)}, u32[]{:S(2)}, u32[]{:S(2)}) collective-permute-start(f32[2,8,640]{2,1,0:T(8,128)S(1)} %get-tuple-element.21), channel_id=1, source_target_pairs={{0,16},{1,2},{2,1},{3,4},{4,3},{5,6},{6,5},{7,8},{8,7},{9,10},{10,... | collective-permute-start | bytes 122888 | tf_op jit(solution)/shard_map/ppermute | solution.py:290
  4.7 0.1 collective-permute-start.1
  4.9 2.3 %reverse_first.1 = (bf16[2,3,576,576]{3,2,1,0:T(8,128)(2,1)S(1)}, f32[2,8,576]{2,1,0:T(8,128)S(1)}, f32[2,8,576]{2,1,0:T(8,128)S(1)}, f32[2,8,576]{2,1,0:T(8,128)S(1)}) custom-call(f32[2,3,576,576]{3,2,1,0:T(8,128)S(1)} %bitcast.7, s32[2,3]{1,0:T(2,128)S(1)} %copy-done, f32[2,8,576]{2,1,0:T(8,128)S(1)} %get-tuple-element.19.y0.y), custom_call_target="tpu_custom_call" | custom-call | flops 254803968 | bytes 1048576 | tf_op jit(solution)/shard_map/reverse_first/pallas_call | solution.py:338
  7.2 2.3 %collective-permute-start.2 = (f32[2,8,576]{2,1,0:T(8,128)S(1)}, f32[2,8,576]{2,1,0:T(8,128)S(1)}, u32[]{:S(2)}, u32[]{:S(2)}) collective-permute-start(f32[2,8,576]{2,1,0:T(8,128)S(1)} %get-tuple-element.27), channel_id=1, source_target_pairs={{0,16},{1,2},{2,1},{3,4},{4,3},{5,6},{6,5},{7,8},{8,7},{9,10},{10,... | collective-permute-start | bytes 110600 | tf_op jit(solution)/shard_map/ppermute | solution.py:290
  9.5 0.1 collective-permute-start.3
  9.7 2.1 %forward_first.1 = (f32[2,8,576]{2,1,0:T(8,128)S(1)}, bf16[2,3,576,576]{3,2,1,0:T(8,128)(2,1)S(1)}) custom-call(bf16[2,3,576,576]{3,2,1,0:T(8,128)(2,1)S(1)} %get-tuple-element.20.th, f32[2,3,576,576]{3,2,1,0:T(8,128)S(1)} %bitcast.7, s32[2,3]{1,0:T(2,128)S(1)} %copy-done, f32[2,8,576]{2,1,0:T(8,128)S(1)} %get-tuple-element.19.y0.y, ...), custom_call_target="tpu_custom_call" | custom-call | flops 254803968 | bytes 1048576 | tf_op jit(solution)/shard_map/forward_first/pallas_call | solution.py:343
  11.8 0.0 collective-permute-done.2
  11.9 1.7 %collective-permute-start.5 = (f32[2,8,640]{2,1,0:T(8,128)S(1)}, f32[2,8,640]{2,1,0:T(8,128)S(1)}, u32[]{:S(2)}, u32[]{:S(2)}) collective-permute-start(f32[2,8,640]{2,1,0:T(8,128)S(1)} %pad.12), channel_id=1, source_target_pairs={{0,16},{1,2},{2,1},{3,4},{4,3},{5,6},{6,5},{7,8},{8,7},{9,10},{10,... | collective-permute-start | bytes 122888 | tf_op jit(solution)/shard_map/ppermute | solution.py:290
  13.6 2.2 %reverse_second.1 = (f32[2,8,576]{2,1,0:T(8,128)S(1)}, f32[2,8,576]{2,1,0:T(8,128)S(1)}, f32[2,8,640]{2,1,0:T(8,128)S(1)}, f32[8,128]{1,0:T(8,128)S(1)}) custom-call(f32[2,3,576,576]{3,2,1,0:T(8,128)S(1)} %bitcast.7, s32[2,3]{1,0:T(2,128)S(1)} %copy-done, f32[2,8,576]{2,1,0:T(8,128)S(1)} %get-tuple-element.36.y1.y, ...), custom_call_target="tpu_custom_call" | custom-call | flops 254803968 | bytes 1048576 | tf_op jit(solution)/shard_map/reverse_second/pallas_call | solution.py:350
  15.9 0.1 collective-permute-done.5.y_o
  15.9 0.4 %cross_grams.1 = f32[8,128]{1,0:T(8,128)S(1)} custom-call(f32[2,8,576]{2,1,0:T(8,128)S(1)} %get-tuple-element.29.out_e, f32[2,8,576]{2,1,0:T(8,128)S(1)} %get-tuple-element.30.out_m.rest_0_, f32[2,8,640]{2,1,0:T(8,128)S(1)} %get-tuple-element.31.out_o, f32[2,8,576]{2,1,0:T(8,128)S(1)} %collective-permute-done.4.y_e, ...), custom_call_target="tpu_custom_call" | custom-call | bytes 1048576 | tf_op jit(solution)/shard_map/cross_grams/pallas_call | solution.py:354
  16.3 1.8 %collective-permute-start.8 = (f32[8,128]{1,0:T(8,128)S(1)}, f32[8,128]{1,0:T(8,128)S(1)}, u32[]{:S(2)}, u32[]{:S(2)}) collective-permute-start(f32[8,128]{1,0:T(8,128)S(1)} %cross_grams.1), channel_id=1, source_target_pairs={{0,3},{1,2},{2,1},{3,0},{4,7},{5,6},{6,5},{7,4},{8,11},{9,10},{10,... | collective-permute-start | bytes 12296 | tf_op jit(solution)/shard_map/ppermute | solution.py:305
  18.1 0.3 collective-permute-start.7
  18.4 0.5 %collective-permute-start.13 = (f32[2,8,576]{2,1,0:T(8,128)S(1)}, f32[2,8,576]{2,1,0:T(8,128)S(1)}, u32[]{:S(2)}, u32[]{:S(2)}) collective-permute-start(f32[2,8,576]{2,1,0:T(8,128)S(1)} %get-tuple-element.29.out_e), channel_id=1, source_target_pairs={{0,1},{1,0},{2,3},{3,2},{4,5},{5,4},{6,7},{7,6},{8,9},{9,8},{10,11... | collective-permute-start | bytes 110600 | tf_op jit(solution)/shard_map/ppermute | solution.py:277
  18.9 1.4 %collective-permute-start.12 = (f32[2,8,640]{2,1,0:T(8,128)S(1)}, f32[2,8,640]{2,1,0:T(8,128)S(1)}, u32[]{:S(2)}, u32[]{:S(2)}) collective-permute-start(f32[2,8,640]{2,1,0:T(8,128)S(1)} %get-tuple-element.31.out_o), channel_id=1, source_target_pairs={{0,16},{1,2},{2,1},{3,4},{4,3},{5,6},{6,5},{7,8},{8,7},{9,10},{10,... | collective-permute-start | bytes 122888 | tf_op jit(solution)/shard_map/ppermute | solution.py:290
  20.3 1.4 %collective-permute-done.7 = f32[8,128]{1,0:T(8,128)S(1)} collective-permute-done((f32[8,128]{1,0:T(8,128)S(1)}, f32[8,128]{1,0:T(8,128)S(1)}, u32[]{:S(2)}, u32[]{:S(2)}) %collective-permute-start.7) | collective-permute-done | bytes 4128 | tf_op jit(solution)/shard_map/ppermute | solution.py:305
  21.8 1.8 %collective-permute-start.11 = (f32[8,128]{1,0:T(8,128)S(1)}, f32[8,128]{1,0:T(8,128)S(1)}, u32[]{:S(2)}, u32[]{:S(2)}) collective-permute-start(f32[8,128]{1,0:T(8,128)S(1)} %add_add_fusion.refs_0_), channel_id=1, source_target_pairs={{0,13},{1,12},{2,15},{3,14},{4,9},{5,8},{6,11},{7,10},{8,5},{9,4},... | collective-permute-start | bytes 12296 | tf_op jit(solution)/shard_map/ppermute | solution.py:305
  23.6 1.0 %collective-permute-start.10 = (f32[8,256]{1,0:T(8,128)S(1)}, f32[8,256]{1,0:T(8,128)S(1)}, u32[]{:S(2)}, u32[]{:S(2)}) collective-permute-start(f32[8,256]{1,0:T(8,128)S(1)} %pad.14), channel_id=1, source_target_pairs={{0,9},{1,8},{2,11},{3,10},{4,13},{5,12},{6,15},{7,14},{8,1},{9,0},... | collective-permute-start | bytes 24584 | tf_op jit(solution)/shard_map/ppermute | solution.py:305
  24.6 1.3 %collective-permute-start.9 = (f32[8,384]{1,0:T(8,128)S(1)}, f32[8,384]{1,0:T(8,128)S(1)}, u32[]{:S(2)}, u32[]{:S(2)}) collective-permute-start(f32[8,384]{1,0:T(8,128)S(1)} %pad.13), channel_id=1, source_target_pairs={{0,4},{1,5},{2,6},{3,7},{4,0},{5,1},{6,2},{7,3},{8,12},{9,13},{10,... | collective-permute-start | bytes 36872 | tf_op jit(solution)/shard_map/ppermute | solution.py:305
  25.9 1.9 %forward_second.1.refs_6_ = f32[2,8,576]{2,1,0:T(8,128)S(1)} custom-call(bf16[2,3,576,576]{3,2,1,0:T(8,128)(2,1)S(1)} %get-tuple-element.20.th, bf16[2,3,576,576]{3,2,1,0:T(8,128)(2,1)S(1)} %get-tuple-element.33.source, s32[2,3]{1,0:T(2,128)S(1)} %copy-done, f32[2,8,576]{2,1,0:T(8,128)S(1)} %get-tuple-element.36.y1.y, ...), custom_call_target="tpu_custom_call" | custom-call | flops 254803968 | bytes 1048576 | tf_op jit(solution)/shard_map/forward_second/pallas_call | solution.py:359
  27.8 0.5 %collective-permute-done.9.refs_1_ = f32[8,384]{1,0:T(8,128)S(1)} collective-permute-done((f32[8,384]{1,0:T(8,128)S(1)}, f32[8,384]{1,0:T(8,128)S(1)}, u32[]{:S(2)}, u32[]{:S(2)}) %collective-permute-start.9) | collective-permute-done | bytes 12320 | tf_op jit(solution)/shard_map/ppermute | solution.py:305
  28.3 1.7 %finish.1 = (f32[3,8,384]{2,1,0:T(8,128)}, f32[3,8,384]{2,1,0:T(8,128)}) custom-call(f32[8,128]{1,0:T(8,128)S(1)} %add_add_fusion.refs_0_, f32[8,384]{1,0:T(8,128)S(1)} %collective-permute-done.9.refs_1_, f32[8,256]{1,0:T(8,128)S(1)} %collective-permute-done.10.refs_2_, f32[8,128]{1,0:T(8,128)S(1)} %collective-permute-done.11.refs_3_, ...), custom_call_target="tpu_custom_call" | custom-call | bytes 1048576 | tf_op jit(solution)/shard_map/finish/pallas_call | solution.py:364
  (26 shorter events, 0.1 us)
Async XLA Ops:
  0.6 4.2 %slice-start = ((s8[8847360]{0:T(1024)(128)(4,1)}), s8[4194304]{0:T(1024)(128)(4,1)S(1)}, s32[]{:S(2)}) async-start(s8[8847360]{0:T(1024)(128)(4,1)} %bitcast.6), calls=%async_computation | async-start | bytes 8388608
  0.6 4.2 %slice-start.1 = ((s8[8847360]{0:T(1024)(128)(4,1)}), s8[4194304]{0:T(1024)(128)(4,1)S(1)}, s32[]{:S(2)}) async-start(s8[8847360]{0:T(1024)(128)(4,1)} %bitcast.6), calls=%async_computation.1 | async-start | bytes 8388608
  0.7 4.2 %slice-start.2 = ((s8[8847360]{0:T(1024)(128)(4,1)}), s8[458752]{0:T(1024)(128)(4,1)S(1)}, s32[]{:S(2)}) async-start(s8[8847360]{0:T(1024)(128)(4,1)} %bitcast.6), calls=%async_computation.2 | async-start | bytes 917504
  0.7 4.2 %copy-start = (s32[2,3]{1,0:T(2,128)S(1)}, s32[2,3]{1,0:T(2,128)}, u32[]{:S(2)}) copy-start(s32[2,3]{1,0:T(2,128)} %cols.7) | copy-start | bytes 76
  1.7 7.9 %collective-permute-start = (f32[2,8,640]{2,1,0:T(8,128)S(1)}, f32[2,8,640]{2,1,0:T(8,128)S(1)}, u32[]{:S(2)}, u32[]{:S(2)}) collective-permute-start(f32[2,8,640]{2,1,0:T(8,128)S(1)} %get-tuple-element.21), channel_id=1, source_target_pairs={{0,16},{1,2},{2,1},{3,4},{4,3},{5,6},{6,5},{7,8},{8,7},{9,10},{10,... | collective-permute-start | bytes 122888 | tf_op jit(solution)/shard_map/ppermute | solution.py:290
  4.7 4.9 %collective-permute-start.1 = (f32[2,8,576]{2,1,0:T(8,128)S(1)}, f32[2,8,576]{2,1,0:T(8,128)S(1)}, u32[]{:S(2)}, u32[]{:S(2)}) collective-permute-start(f32[2,8,576]{2,1,0:T(8,128)S(1)} %get-tuple-element.19.y0.y), channel_id=1, source_target_pairs={{0,1},{1,0},{2,3},{3,2},{4,5},{5,4},{6,7},{7,6},{8,9},{9,8},{10,11... | collective-permute-start | bytes 110600 | tf_op jit(solution)/shard_map/ppermute | solution.py:277
  7.2 4.6 %collective-permute-start.2 = (f32[2,8,576]{2,1,0:T(8,128)S(1)}, f32[2,8,576]{2,1,0:T(8,128)S(1)}, u32[]{:S(2)}, u32[]{:S(2)}) collective-permute-start(f32[2,8,576]{2,1,0:T(8,128)S(1)} %get-tuple-element.27), channel_id=1, source_target_pairs={{0,16},{1,2},{2,1},{3,4},{4,3},{5,6},{6,5},{7,8},{8,7},{9,10},{10,... | collective-permute-start | bytes 110600 | tf_op jit(solution)/shard_map/ppermute | solution.py:290
  9.5 2.3 %collective-permute-start.3 = (f32[2,8,576]{2,1,0:T(8,128)S(1)}, f32[2,8,576]{2,1,0:T(8,128)S(1)}, u32[]{:S(2)}, u32[]{:S(2)}) collective-permute-start(f32[2,8,576]{2,1,0:T(8,128)S(1)} %get-tuple-element.28), channel_id=1, source_target_pairs={{0,1},{1,0},{2,3},{3,2},{4,5},{5,4},{6,7},{7,6},{8,9},{9,8},{10,11... | collective-permute-start | bytes 110600 | tf_op jit(solution)/shard_map/ppermute | solution.py:277
  11.9 4.1 %collective-permute-start.5 = (f32[2,8,640]{2,1,0:T(8,128)S(1)}, f32[2,8,640]{2,1,0:T(8,128)S(1)}, u32[]{:S(2)}, u32[]{:S(2)}) collective-permute-start(f32[2,8,640]{2,1,0:T(8,128)S(1)} %pad.12), channel_id=1, source_target_pairs={{0,16},{1,2},{2,1},{3,4},{4,3},{5,6},{6,5},{7,8},{8,7},{9,10},{10,... | collective-permute-start | bytes 122888 | tf_op jit(solution)/shard_map/ppermute | solution.py:290
  13.6 2.2 %collective-permute-start.4 = (f32[2,8,576]{2,1,0:T(8,128)S(1)}, f32[2,8,576]{2,1,0:T(8,128)S(1)}, u32[]{:S(2)}, u32[]{:S(2)}) collective-permute-start(f32[2,8,576]{2,1,0:T(8,128)S(1)} %get-tuple-element.36.y1.y), channel_id=1, source_target_pairs={{0,1},{1,0},{2,3},{3,2},{4,5},{5,4},{6,7},{7,6},{8,9},{9,8},{10,11... | collective-permute-start | bytes 110600 | tf_op jit(solution)/shard_map/ppermute | solution.py:277
  16.3 4.0 %collective-permute-start.8 = (f32[8,128]{1,0:T(8,128)S(1)}, f32[8,128]{1,0:T(8,128)S(1)}, u32[]{:S(2)}, u32[]{:S(2)}) collective-permute-start(f32[8,128]{1,0:T(8,128)S(1)} %cross_grams.1), channel_id=1, source_target_pairs={{0,3},{1,2},{2,1},{3,0},{4,7},{5,6},{6,5},{7,4},{8,11},{9,10},{10,... | collective-permute-start | bytes 12296 | tf_op jit(solution)/shard_map/ppermute | solution.py:305
  18.1 3.6 %collective-permute-start.7 = (f32[8,128]{1,0:T(8,128)S(1)}, f32[8,128]{1,0:T(8,128)S(1)}, u32[]{:S(2)}, u32[]{:S(2)}) collective-permute-start(f32[8,128]{1,0:T(8,128)S(1)} %cross_grams.1), channel_id=1, source_target_pairs={{0,2},{1,3},{2,0},{3,1},{4,6},{5,7},{6,4},{7,5},{8,10},{9,11},{10,... | collective-permute-start | bytes 12296 | tf_op jit(solution)/shard_map/ppermute | solution.py:305
  18.4 3.3 %collective-permute-start.6 = (f32[8,128]{1,0:T(8,128)S(1)}, f32[8,128]{1,0:T(8,128)S(1)}, u32[]{:S(2)}, u32[]{:S(2)}) collective-permute-start(f32[8,128]{1,0:T(8,128)S(1)} %cross_grams.1), channel_id=1, source_target_pairs={{0,1},{1,0},{2,3},{3,2},{4,5},{5,4},{6,7},{7,6},{8,9},{9,8},{10,11... | collective-permute-start | bytes 12296 | tf_op jit(solution)/shard_map/ppermute | solution.py:305
  18.4 7.5 %collective-permute-start.13 = (f32[2,8,576]{2,1,0:T(8,128)S(1)}, f32[2,8,576]{2,1,0:T(8,128)S(1)}, u32[]{:S(2)}, u32[]{:S(2)}) collective-permute-start(f32[2,8,576]{2,1,0:T(8,128)S(1)} %get-tuple-element.29.out_e), channel_id=1, source_target_pairs={{0,1},{1,0},{2,3},{3,2},{4,5},{5,4},{6,7},{7,6},{8,9},{9,8},{10,11... | collective-permute-start | bytes 110600 | tf_op jit(solution)/shard_map/ppermute | solution.py:277
  18.9 7.0 %collective-permute-start.12 = (f32[2,8,640]{2,1,0:T(8,128)S(1)}, f32[2,8,640]{2,1,0:T(8,128)S(1)}, u32[]{:S(2)}, u32[]{:S(2)}) collective-permute-start(f32[2,8,640]{2,1,0:T(8,128)S(1)} %get-tuple-element.31.out_o), channel_id=1, source_target_pairs={{0,16},{1,2},{2,1},{3,4},{4,3},{5,6},{6,5},{7,8},{8,7},{9,10},{10,... | collective-permute-start | bytes 122888 | tf_op jit(solution)/shard_map/ppermute | solution.py:290
  21.8 6.1 %collective-permute-start.11 = (f32[8,128]{1,0:T(8,128)S(1)}, f32[8,128]{1,0:T(8,128)S(1)}, u32[]{:S(2)}, u32[]{:S(2)}) collective-permute-start(f32[8,128]{1,0:T(8,128)S(1)} %add_add_fusion.refs_0_), channel_id=1, source_target_pairs={{0,13},{1,12},{2,15},{3,14},{4,9},{5,8},{6,11},{7,10},{8,5},{9,4},... | collective-permute-start | bytes 12296 | tf_op jit(solution)/shard_map/ppermute | solution.py:305
  23.6 4.2 %collective-permute-start.10 = (f32[8,256]{1,0:T(8,128)S(1)}, f32[8,256]{1,0:T(8,128)S(1)}, u32[]{:S(2)}, u32[]{:S(2)}) collective-permute-start(f32[8,256]{1,0:T(8,128)S(1)} %pad.14), channel_id=1, source_target_pairs={{0,9},{1,8},{2,11},{3,10},{4,13},{5,12},{6,15},{7,14},{8,1},{9,0},... | collective-permute-start | bytes 24584 | tf_op jit(solution)/shard_map/ppermute | solution.py:305
  24.6 3.7 %collective-permute-start.9 = (f32[8,384]{1,0:T(8,128)S(1)}, f32[8,384]{1,0:T(8,128)S(1)}, u32[]{:S(2)}, u32[]{:S(2)}) collective-permute-start(f32[8,384]{1,0:T(8,128)S(1)} %pad.13), channel_id=1, source_target_pairs={{0,4},{1,5},{2,6},{3,7},{4,0},{5,1},{6,2},{7,3},{8,12},{9,13},{10,... | collective-permute-start | bytes 36872 | tf_op jit(solution)/shard_map/ppermute | solution.py:305

commit v8 on v7

--- a/solution.py
+++ b/solution.py
@@ -296,7 +296,7 @@
     base = 1
     while True:
         cross = 1 if base > 1 else 0
-        masks = [base, 2 * base + cross, 3 * base + cross] if 2 * base < count else [base]
+        masks = [base + cross, 2 * base, 3 * base + cross] if 2 * base < count else [base]
         got = []
         for i, mask in enumerate(masks):
             extra = (len(masks) - 1 - i) * width if base > 1 else 0

time: 30.1 us -> 30.1 us (level)
  no operation moved by 1% of the time
where the time goes in v8:
time: 30.1 us; the launch traced here: 30 us
  starting transfers between devices  15.2 us (50%)
  Pallas kernels  11.7 us (39%)
  waiting for transfers between devices  2.29 us (8%)
  between operations  0.78 us (3%)
    ppermute x4, starting transfers between devices, odd_swap(): return lax.ppermute(x, ('groups', 'row'), route)  8.39 us
    ppermute x6, starting transfers between devices, swapped_sums(): got.append(lax.ppermute(sent, 'row', route))  5.99 us
    pallas_call x1, Pallas kernels, shards(): call(reverse_first, (half, field, field, field), [vmem, smem, vmem], [acc...  2.33 us
    pallas_call x1, Pallas kernels, shards(): call(reverse_second, (field, field, wide, gram_shape), [vmem, smem] + [vm...  2.23 us
    ppermute x6, waiting for transfers between devices, swapped_sums(): got.append(lax.ppermute(sent, 'row', route))  2.19 us
    pallas_call x1, Pallas kernels, shards(): call(functools.partial(forward, reverses=1), (field, half), [vmem, vmem,...  2.15 us
    pallas_call x1, Pallas kernels, shards(): call(functools.partial(forward, reverses=3), field, [vmem, vmem, smem] +...  1.87 us
    pallas_call x1, Pallas kernels, shards(): call(lambda *refs: finish(*refs, rounds=len(sums), shift=shift), (out, ou...  1.7 us
  transfers between devices with their start and end apart: 14, of which 3 were waited for; matrix products, arithmetic and copies ran while one was open for 0% of the time, Pallas kernels for 29%

profile of v8, /device:TPU:0, one launch (start us, length us, event | category | flops | bytes accessed | tf_op | source)
XLA Modules:
  0.0 30.0 jit_solution(684543734483822002)
XLA Ops:
  0.7 0.0 slice-start.2
  0.7 1.0 %prepare.1 = (f32[2,8,576]{2,1,0:T(8,128)S(1)}, f32[2,8,576]{2,1,0:T(8,128)S(1)}, f32[2,8,640]{2,1,0:T(8,128)S(1)}, f32[2,1,576]{2,1,0:T(1,128)S(1)}, f32[2,1,576]{2,1,0:T(1,128)S(1)}) custom-call(f32[3,8,384]{2,1,0:T(8,128)} %bitcast.9, s32[384]{0:T(512)} %refs_1_.1, f32[3,384]{1,0:T(4,128)} %refs_2_.1), custom_call_target="tpu_custom_call" | custom-call | flops 10000000000 | bytes 1048576 | tf_op jit(solution)/shard_map/prepare/pallas_call | solution.py:325
  1.7 3.0 %collective-permute-start = (f32[2,8,640]{2,1,0:T(8,128)S(1)}, f32[2,8,640]{2,1,0:T(8,128)S(1)}, u32[]{:S(2)}, u32[]{:S(2)}) collective-permute-start(f32[2,8,640]{2,1,0:T(8,128)S(1)} %get-tuple-element.21), channel_id=1, source_target_pairs={{0,16},{1,2},{2,1},{3,4},{4,3},{5,6},{6,5},{7,8},{8,7},{9,10},{10,... | collective-permute-start | bytes 122888 | tf_op jit(solution)/shard_map/ppermute | solution.py:290
  4.7 0.1 collective-permute-start.1
  4.9 2.3 %reverse_first.1 = (bf16[2,3,576,576]{3,2,1,0:T(8,128)(2,1)S(1)}, f32[2,8,576]{2,1,0:T(8,128)S(1)}, f32[2,8,576]{2,1,0:T(8,128)S(1)}, f32[2,8,576]{2,1,0:T(8,128)S(1)}) custom-call(f32[2,3,576,576]{3,2,1,0:T(8,128)S(1)} %bitcast.7, s32[2,3]{1,0:T(2,128)S(1)} %copy-done, f32[2,8,576]{2,1,0:T(8,128)S(1)} %get-tuple-element.19.y0.y), custom_call_target="tpu_custom_call" | custom-call | flops 254803968 | bytes 1048576 | tf_op jit(solution)/shard_map/reverse_first/pallas_call | solution.py:338
  7.2 2.3 %collective-permute-start.2 = (f32[2,8,576]{2,1,0:T(8,128)S(1)}, f32[2,8,576]{2,1,0:T(8,128)S(1)}, u32[]{:S(2)}, u32[]{:S(2)}) collective-permute-start(f32[2,8,576]{2,1,0:T(8,128)S(1)} %get-tuple-element.27), channel_id=1, source_target_pairs={{0,16},{1,2},{2,1},{3,4},{4,3},{5,6},{6,5},{7,8},{8,7},{9,10},{10,... | collective-permute-start | bytes 110600 | tf_op jit(solution)/shard_map/ppermute | solution.py:290
  9.5 0.1 collective-permute-start.3
  9.7 2.1 %forward_first.1 = (f32[2,8,576]{2,1,0:T(8,128)S(1)}, bf16[2,3,576,576]{3,2,1,0:T(8,128)(2,1)S(1)}) custom-call(bf16[2,3,576,576]{3,2,1,0:T(8,128)(2,1)S(1)} %get-tuple-element.20.th, f32[2,3,576,576]{3,2,1,0:T(8,128)S(1)} %bitcast.7, s32[2,3]{1,0:T(2,128)S(1)} %copy-done, f32[2,8,576]{2,1,0:T(8,128)S(1)} %get-tuple-element.19.y0.y, ...), custom_call_target="tpu_custom_call" | custom-call | flops 254803968 | bytes 1048576 | tf_op jit(solution)/shard_map/forward_first/pallas_call | solution.py:343
  11.8 0.0 collective-permute-done.2
  11.9 1.7 %collective-permute-start.5 = (f32[2,8,640]{2,1,0:T(8,128)S(1)}, f32[2,8,640]{2,1,0:T(8,128)S(1)}, u32[]{:S(2)}, u32[]{:S(2)}) collective-permute-start(f32[2,8,640]{2,1,0:T(8,128)S(1)} %pad.12), channel_id=1, source_target_pairs={{0,16},{1,2},{2,1},{3,4},{4,3},{5,6},{6,5},{7,8},{8,7},{9,10},{10,... | collective-permute-start | bytes 122888 | tf_op jit(solution)/shard_map/ppermute | solution.py:290
  13.6 2.2 %reverse_second.1 = (f32[2,8,576]{2,1,0:T(8,128)S(1)}, f32[2,8,576]{2,1,0:T(8,128)S(1)}, f32[2,8,640]{2,1,0:T(8,128)S(1)}, f32[8,128]{1,0:T(8,128)S(1)}) custom-call(f32[2,3,576,576]{3,2,1,0:T(8,128)S(1)} %bitcast.7, s32[2,3]{1,0:T(2,128)S(1)} %copy-done, f32[2,8,576]{2,1,0:T(8,128)S(1)} %get-tuple-element.36.y1.y, ...), custom_call_target="tpu_custom_call" | custom-call | flops 254803968 | bytes 1048576 | tf_op jit(solution)/shard_map/reverse_second/pallas_call | solution.py:350
  15.9 0.1 collective-permute-done.5.y_o
  15.9 0.4 %cross_grams.1 = f32[8,128]{1,0:T(8,128)S(1)} custom-call(f32[2,8,576]{2,1,0:T(8,128)S(1)} %get-tuple-element.29.out_e, f32[2,8,576]{2,1,0:T(8,128)S(1)} %get-tuple-element.30.out_m.rest_0_, f32[2,8,640]{2,1,0:T(8,128)S(1)} %get-tuple-element.31.out_o, f32[2,8,576]{2,1,0:T(8,128)S(1)} %collective-permute-done.4.y_e, ...), custom_call_target="tpu_custom_call" | custom-call | bytes 1048576 | tf_op jit(solution)/shard_map/cross_grams/pallas_call | solution.py:354
  16.3 1.8 %collective-permute-start.8 = (f32[8,128]{1,0:T(8,128)S(1)}, f32[8,128]{1,0:T(8,128)S(1)}, u32[]{:S(2)}, u32[]{:S(2)}) collective-permute-start(f32[8,128]{1,0:T(8,128)S(1)} %cross_grams.1), channel_id=1, source_target_pairs={{0,3},{1,2},{2,1},{3,0},{4,7},{5,6},{6,5},{7,4},{8,11},{9,10},{10,... | collective-permute-start | bytes 12296 | tf_op jit(solution)/shard_map/ppermute | solution.py:305
  18.1 0.3 collective-permute-start.7
  18.4 0.5 %collective-permute-start.13 = (f32[2,8,576]{2,1,0:T(8,128)S(1)}, f32[2,8,576]{2,1,0:T(8,128)S(1)}, u32[]{:S(2)}, u32[]{:S(2)}) collective-permute-start(f32[2,8,576]{2,1,0:T(8,128)S(1)} %get-tuple-element.29.out_e), channel_id=1, source_target_pairs={{0,1},{1,0},{2,3},{3,2},{4,5},{5,4},{6,7},{7,6},{8,9},{9,8},{10,11... | collective-permute-start | bytes 110600 | tf_op jit(solution)/shard_map/ppermute | solution.py:277
  18.9 1.4 %collective-permute-start.12 = (f32[2,8,640]{2,1,0:T(8,128)S(1)}, f32[2,8,640]{2,1,0:T(8,128)S(1)}, u32[]{:S(2)}, u32[]{:S(2)}) collective-permute-start(f32[2,8,640]{2,1,0:T(8,128)S(1)} %get-tuple-element.31.out_o), channel_id=1, source_target_pairs={{0,16},{1,2},{2,1},{3,4},{4,3},{5,6},{6,5},{7,8},{8,7},{9,10},{10,... | collective-permute-start | bytes 122888 | tf_op jit(solution)/shard_map/ppermute | solution.py:290
  20.3 1.4 %collective-permute-done.7 = f32[8,128]{1,0:T(8,128)S(1)} collective-permute-done((f32[8,128]{1,0:T(8,128)S(1)}, f32[8,128]{1,0:T(8,128)S(1)}, u32[]{:S(2)}, u32[]{:S(2)}) %collective-permute-start.7) | collective-permute-done | bytes 4128 | tf_op jit(solution)/shard_map/ppermute | solution.py:305
  21.8 1.8 %collective-permute-start.11 = (f32[8,128]{1,0:T(8,128)S(1)}, f32[8,128]{1,0:T(8,128)S(1)}, u32[]{:S(2)}, u32[]{:S(2)}) collective-permute-start(f32[8,128]{1,0:T(8,128)S(1)} %add_add_fusion.refs_0_), channel_id=1, source_target_pairs={{0,13},{1,12},{2,15},{3,14},{4,9},{5,8},{6,11},{7,10},{8,5},{9,4},... | collective-permute-start | bytes 12296 | tf_op jit(solution)/shard_map/ppermute | solution.py:305
  23.6 0.9 %collective-permute-start.10 = (f32[8,256]{1,0:T(8,128)S(1)}, f32[8,256]{1,0:T(8,128)S(1)}, u32[]{:S(2)}, u32[]{:S(2)}) collective-permute-start(f32[8,256]{1,0:T(8,128)S(1)} %pad.14), channel_id=1, source_target_pairs={{0,8},{1,9},{2,10},{3,11},{4,12},{5,13},{6,14},{7,15},{8,0},{9,1},... | collective-permute-start | bytes 24584 | tf_op jit(solution)/shard_map/ppermute | solution.py:305
  24.5 1.2 %collective-permute-start.9 = (f32[8,384]{1,0:T(8,128)S(1)}, f32[8,384]{1,0:T(8,128)S(1)}, u32[]{:S(2)}, u32[]{:S(2)}) collective-permute-start(f32[8,384]{1,0:T(8,128)S(1)} %pad.13), channel_id=1, source_target_pairs={{0,5},{1,4},{2,7},{3,6},{4,1},{5,0},{6,3},{7,2},{8,13},{9,12},{10,... | collective-permute-start | bytes 36872 | tf_op jit(solution)/shard_map/ppermute | solution.py:305
  25.7 1.9 %forward_second.1.refs_6_ = f32[2,8,576]{2,1,0:T(8,128)S(1)} custom-call(bf16[2,3,576,576]{3,2,1,0:T(8,128)(2,1)S(1)} %get-tuple-element.20.th, bf16[2,3,576,576]{3,2,1,0:T(8,128)(2,1)S(1)} %get-tuple-element.33.source, s32[2,3]{1,0:T(2,128)S(1)} %copy-done, f32[2,8,576]{2,1,0:T(8,128)S(1)} %get-tuple-element.36.y1.y, ...), custom_call_target="tpu_custom_call" | custom-call | flops 254803968 | bytes 1048576 | tf_op jit(solution)/shard_map/forward_second/pallas_call | solution.py:359
  27.5 0.7 %collective-permute-done.10.refs_2_ = f32[8,256]{1,0:T(8,128)S(1)} collective-permute-done((f32[8,256]{1,0:T(8,128)S(1)}, f32[8,256]{1,0:T(8,128)S(1)}, u32[]{:S(2)}, u32[]{:S(2)}) %collective-permute-start.10) | collective-permute-done | bytes 8224 | tf_op jit(solution)/shard_map/ppermute | solution.py:305
  28.3 1.7 %finish.1 = (f32[3,8,384]{2,1,0:T(8,128)}, f32[3,8,384]{2,1,0:T(8,128)}) custom-call(f32[8,128]{1,0:T(8,128)S(1)} %add_add_fusion.refs_0_, f32[8,384]{1,0:T(8,128)S(1)} %collective-permute-done.9.refs_1_, f32[8,256]{1,0:T(8,128)S(1)} %collective-permute-done.10.refs_2_, f32[8,128]{1,0:T(8,128)S(1)} %collective-permute-done.11.refs_3_, ...), custom_call_target="tpu_custom_call" | custom-call | bytes 1048576 | tf_op jit(solution)/shard_map/finish/pallas_call | solution.py:364
  (26 shorter events, 0.1 us)
Async XLA Ops:
  0.6 4.2 %slice-start = ((s8[8847360]{0:T(1024)(128)(4,1)}), s8[4194304]{0:T(1024)(128)(4,1)S(1)}, s32[]{:S(2)}) async-start(s8[8847360]{0:T(1024)(128)(4,1)} %bitcast.6), calls=%async_computation | async-start | bytes 8388608
  0.6 4.2 %slice-start.1 = ((s8[8847360]{0:T(1024)(128)(4,1)}), s8[4194304]{0:T(1024)(128)(4,1)S(1)}, s32[]{:S(2)}) async-start(s8[8847360]{0:T(1024)(128)(4,1)} %bitcast.6), calls=%async_computation.1 | async-start | bytes 8388608
  0.7 4.2 %slice-start.2 = ((s8[8847360]{0:T(1024)(128)(4,1)}), s8[458752]{0:T(1024)(128)(4,1)S(1)}, s32[]{:S(2)}) async-start(s8[8847360]{0:T(1024)(128)(4,1)} %bitcast.6), calls=%async_computation.2 | async-start | bytes 917504
  0.7 4.2 %copy-start = (s32[2,3]{1,0:T(2,128)S(1)}, s32[2,3]{1,0:T(2,128)}, u32[]{:S(2)}) copy-start(s32[2,3]{1,0:T(2,128)} %cols.7) | copy-start | bytes 76
  1.7 7.9 %collective-permute-start = (f32[2,8,640]{2,1,0:T(8,128)S(1)}, f32[2,8,640]{2,1,0:T(8,128)S(1)}, u32[]{:S(2)}, u32[]{:S(2)}) collective-permute-start(f32[2,8,640]{2,1,0:T(8,128)S(1)} %get-tuple-element.21), channel_id=1, source_target_pairs={{0,16},{1,2},{2,1},{3,4},{4,3},{5,6},{6,5},{7,8},{8,7},{9,10},{10,... | collective-permute-start | bytes 122888 | tf_op jit(solution)/shard_map/ppermute | solution.py:290
  4.7 4.9 %collective-permute-start.1 = (f32[2,8,576]{2,1,0:T(8,128)S(1)}, f32[2,8,576]{2,1,0:T(8,128)S(1)}, u32[]{:S(2)}, u32[]{:S(2)}) collective-permute-start(f32[2,8,576]{2,1,0:T(8,128)S(1)} %get-tuple-element.19.y0.y), channel_id=1, source_target_pairs={{0,1},{1,0},{2,3},{3,2},{4,5},{5,4},{6,7},{7,6},{8,9},{9,8},{10,11... | collective-permute-start | bytes 110600 | tf_op jit(solution)/shard_map/ppermute | solution.py:277
  7.2 4.6 %collective-permute-start.2 = (f32[2,8,576]{2,1,0:T(8,128)S(1)}, f32[2,8,576]{2,1,0:T(8,128)S(1)}, u32[]{:S(2)}, u32[]{:S(2)}) collective-permute-start(f32[2,8,576]{2,1,0:T(8,128)S(1)} %get-tuple-element.27), channel_id=1, source_target_pairs={{0,16},{1,2},{2,1},{3,4},{4,3},{5,6},{6,5},{7,8},{8,7},{9,10},{10,... | collective-permute-start | bytes 110600 | tf_op jit(solution)/shard_map/ppermute | solution.py:290
  9.5 2.3 %collective-permute-start.3 = (f32[2,8,576]{2,1,0:T(8,128)S(1)}, f32[2,8,576]{2,1,0:T(8,128)S(1)}, u32[]{:S(2)}, u32[]{:S(2)}) collective-permute-start(f32[2,8,576]{2,1,0:T(8,128)S(1)} %get-tuple-element.28), channel_id=1, source_target_pairs={{0,1},{1,0},{2,3},{3,2},{4,5},{5,4},{6,7},{7,6},{8,9},{9,8},{10,11... | collective-permute-start | bytes 110600 | tf_op jit(solution)/shard_map/ppermute | solution.py:277
  11.9 4.1 %collective-permute-start.5 = (f32[2,8,640]{2,1,0:T(8,128)S(1)}, f32[2,8,640]{2,1,0:T(8,128)S(1)}, u32[]{:S(2)}, u32[]{:S(2)}) collective-permute-start(f32[2,8,640]{2,1,0:T(8,128)S(1)} %pad.12), channel_id=1, source_target_pairs={{0,16},{1,2},{2,1},{3,4},{4,3},{5,6},{6,5},{7,8},{8,7},{9,10},{10,... | collective-permute-start | bytes 122888 | tf_op jit(solution)/shard_map/ppermute | solution.py:290
  13.6 2.2 %collective-permute-start.4 = (f32[2,8,576]{2,1,0:T(8,128)S(1)}, f32[2,8,576]{2,1,0:T(8,128)S(1)}, u32[]{:S(2)}, u32[]{:S(2)}) collective-permute-start(f32[2,8,576]{2,1,0:T(8,128)S(1)} %get-tuple-element.36.y1.y), channel_id=1, source_target_pairs={{0,1},{1,0},{2,3},{3,2},{4,5},{5,4},{6,7},{7,6},{8,9},{9,8},{10,11... | collective-permute-start | bytes 110600 | tf_op jit(solution)/shard_map/ppermute | solution.py:277
  16.3 4.0 %collective-permute-start.8 = (f32[8,128]{1,0:T(8,128)S(1)}, f32[8,128]{1,0:T(8,128)S(1)}, u32[]{:S(2)}, u32[]{:S(2)}) collective-permute-start(f32[8,128]{1,0:T(8,128)S(1)} %cross_grams.1), channel_id=1, source_target_pairs={{0,3},{1,2},{2,1},{3,0},{4,7},{5,6},{6,5},{7,4},{8,11},{9,10},{10,... | collective-permute-start | bytes 12296 | tf_op jit(solution)/shard_map/ppermute | solution.py:305
  18.1 3.6 %collective-permute-start.7 = (f32[8,128]{1,0:T(8,128)S(1)}, f32[8,128]{1,0:T(8,128)S(1)}, u32[]{:S(2)}, u32[]{:S(2)}) collective-permute-start(f32[8,128]{1,0:T(8,128)S(1)} %cross_grams.1), channel_id=1, source_target_pairs={{0,2},{1,3},{2,0},{3,1},{4,6},{5,7},{6,4},{7,5},{8,10},{9,11},{10,... | collective-permute-start | bytes 12296 | tf_op jit(solution)/shard_map/ppermute | solution.py:305
  18.4 3.3 %collective-permute-start.6 = (f32[8,128]{1,0:T(8,128)S(1)}, f32[8,128]{1,0:T(8,128)S(1)}, u32[]{:S(2)}, u32[]{:S(2)}) collective-permute-start(f32[8,128]{1,0:T(8,128)S(1)} %cross_grams.1), channel_id=1, source_target_pairs={{0,1},{1,0},{2,3},{3,2},{4,5},{5,4},{6,7},{7,6},{8,9},{9,8},{10,11... | collective-permute-start | bytes 12296 | tf_op jit(solution)/shard_map/ppermute | solution.py:305
  18.4 7.3 %collective-permute-start.13 = (f32[2,8,576]{2,1,0:T(8,128)S(1)}, f32[2,8,576]{2,1,0:T(8,128)S(1)}, u32[]{:S(2)}, u32[]{:S(2)}) collective-permute-start(f32[2,8,576]{2,1,0:T(8,128)S(1)} %get-tuple-element.29.out_e), channel_id=1, source_target_pairs={{0,1},{1,0},{2,3},{3,2},{4,5},{5,4},{6,7},{7,6},{8,9},{9,8},{10,11... | collective-permute-start | bytes 110600 | tf_op jit(solution)/shard_map/ppermute | solution.py:277
  18.9 6.8 %collective-permute-start.12 = (f32[2,8,640]{2,1,0:T(8,128)S(1)}, f32[2,8,640]{2,1,0:T(8,128)S(1)}, u32[]{:S(2)}, u32[]{:S(2)}) collective-permute-start(f32[2,8,640]{2,1,0:T(8,128)S(1)} %get-tuple-element.31.out_o), channel_id=1, source_target_pairs={{0,16},{1,2},{2,1},{3,4},{4,3},{5,6},{6,5},{7,8},{8,7},{9,10},{10,... | collective-permute-start | bytes 122888 | tf_op jit(solution)/shard_map/ppermute | solution.py:290
  21.8 5.8 %collective-permute-start.11 = (f32[8,128]{1,0:T(8,128)S(1)}, f32[8,128]{1,0:T(8,128)S(1)}, u32[]{:S(2)}, u32[]{:S(2)}) collective-permute-start(f32[8,128]{1,0:T(8,128)S(1)} %add_add_fusion.refs_0_), channel_id=1, source_target_pairs={{0,13},{1,12},{2,15},{3,14},{4,9},{5,8},{6,11},{7,10},{8,5},{9,4},... | collective-permute-start | bytes 12296 | tf_op jit(solution)/shard_map/ppermute | solution.py:305
  23.6 4.7 %collective-permute-start.10 = (f32[8,256]{1,0:T(8,128)S(1)}, f32[8,256]{1,0:T(8,128)S(1)}, u32[]{:S(2)}, u32[]{:S(2)}) collective-permute-start(f32[8,256]{1,0:T(8,128)S(1)} %pad.14), channel_id=1, source_target_pairs={{0,8},{1,9},{2,10},{3,11},{4,12},{5,13},{6,14},{7,15},{8,0},{9,1},... | collective-permute-start | bytes 24584 | tf_op jit(solution)/shard_map/ppermute | solution.py:305
  24.5 3.8 %collective-permute-start.9 = (f32[8,384]{1,0:T(8,128)S(1)}, f32[8,384]{1,0:T(8,128)S(1)}, u32[]{:S(2)}, u32[]{:S(2)}) collective-permute-start(f32[8,384]{1,0:T(8,128)S(1)} %pad.13), channel_id=1, source_target_pairs={{0,5},{1,4},{2,7},{3,6},{4,1},{5,0},{6,3},{7,2},{8,13},{9,12},{10,... | collective-permute-start | bytes 36872 | tf_op jit(solution)/shard_map/ppermute | solution.py:305
